TPU v7x, 256 devices: a whole 4x4x8 slice. The times are simulated.
256 devices in a mesh: dp: 8 (over y, z_hi), tm: 32 (over z_lo, x, core).
Axes of the slice: x: 4, y: 4, z: 8 (z_hi: 2, z_lo: 4; z = z_hi * 4 + z_lo), core: 2. Of those that a mesh axis runs over, the one named last changes fastest.
Arguments:
- queries: bfloat16 [8, 4096, 1024], P('dp', 'tm'), may hold values from -6 to 6
- key_vectors: bfloat16 [8, 4096, 1024], P('dp', 'tm'), may hold values from -6 to 6
- values: bfloat16 [8, 4096, 1024], P('dp', 'tm'), may hold values from -6 to 6
- cotangent: bfloat16 [8, 4096, 2048], P('dp', 'tm'), may hold values from -6 to 6
- out_weight: bfloat16 [1024, 2048], P('tm', 'dp'), may hold values from -0.1875 to 0.1875
- offsets: int32 [8, 12], P('dp'), may hold values from 0 to 4095, as said below
Outputs:
- encoded: bfloat16 [8, 4096, 2048], P('dp', 'tm')
- grad_queries: bfloat16 [8, 4096, 1024], P('dp', 'tm')
- grad_keys: bfloat16 [8, 4096, 1024], P('dp', 'tm')
- grad_values: bfloat16 [8, 4096, 1024], P('dp', 'tm')
- grad_weight: float32 [1024, 2048], P('tm', 'dp')
Inputs may be any that keep to these rules, and one draw needn't show every extreme that they name: Each row holds 12 strictly increasing frame offsets, the first of them 0 and the last 4095, so that the last utterance is the recording's final frame alone; an utterance covers the frames from its offset up to the next offset, the last one up to 4096.
All inputs are finite; a program needn't handle non-finite values.
Results may differ from a plain program's by a relative error of at most 0.0052.
Values may be sent and summed in bfloat16 or wider, within the bound.
No kernel may reach another device: no remote copies, remote signals or barrier semaphores. Data moves between devices by JAX's collectives and lax.ppermute only.
A program may use at most 192 MiB of HBM per device.

v0:
```python
import math

import jax
import jax.numpy as jnp
from jax import lax
from jax.sharding import PartitionSpec as P

HD = 128


def entering(value, axis, join, neutral, backward):
    count, mine = (lax.axis_size(axis), lax.axis_index(axis))
    pieces = jax.tree.map(lambda part: lax.all_gather(part, axis), value)
    if backward:
        pieces = jax.tree.map(lambda part: part[::-1], pieces)
        mine = count - 1 - mine
    running = jax.tree.map(
        lambda part, zero: jnp.full_like(part, 0) + jnp.asarray(zero, part.dtype), value, neutral
    )

    def step(position, running):
        longer = join(running, jax.tree.map(lambda part: part[position], pieces))
        return jax.tree.map(lambda new, old: jnp.where(position < mine, new, old), longer, running)

    return lax.fori_loop(0, count - 1, step, running)


def combine_open(earlier, following):
    keeping = 1.0 - following[-1]
    merged = tuple(
        (
            late_state + keeping * early_state
            for early_state, late_state in zip(earlier[:-1], following[:-1])
        )
    )
    return merged + (jnp.maximum(earlier[-1], following[-1]),)


def apply_state(form, rows, state):
    return jnp.einsum(form, rows.astype(jnp.float32), state, precision=lax.Precision.HIGHEST)


def body(queries, key_vectors, values, cotangent, out_weight, offsets):
    tm_devices = lax.axis_size("tm")
    dp_devices = lax.axis_size("dp")
    block_index = lax.axis_index("tm")
    frames = queries.shape[1]
    head_count = queries.shape[2] // HD
    total_frames = frames * tm_devices
    starts_row = offsets[0]
    positions = block_index * frames + jnp.arange(frames, dtype=jnp.int32)
    utterance = jnp.sum((positions[:, None] >= starts_row[None, :]).astype(jnp.int32), axis=1) - 1
    ends_row = jnp.concatenate([starts_row[1:], jnp.full((1,), total_frames, jnp.int32)])
    span_table = ends_row - starts_row
    picked = utterance[:, None] == jnp.arange(starts_row.shape[0], dtype=jnp.int32)[None, :]
    span_frame = jnp.sum(jnp.where(picked, span_table[None, :], 0), axis=1)
    frame_scale = 1.0 / jnp.sqrt((HD * span_frame).astype(jnp.float32))
    inside = (starts_row >= positions[0]) & (starts_row < positions[0] + frames)
    start_flag = jnp.minimum(jnp.sum(inside.astype(jnp.float32)), 1.0).reshape(1, 1, 1)
    opening = jnp.sum((starts_row == positions[0]).astype(jnp.float32))
    first_mask = (utterance == utterance[0]).astype(jnp.float32) * (1.0 - opening)
    last_mask = (utterance == utterance[-1]).astype(jnp.float32)
    same_mask = (utterance[:, None] == utterance[None, :]).astype(jnp.float32)
    first_col = first_mask[:, None, None]
    last_col = last_mask[:, None, None]
    query_heads = queries[0].reshape(frames, head_count, HD)
    key_heads = key_vectors[0].reshape(frames, head_count, HD)
    value_heads = values[0].reshape(frames, head_count, HD)
    cot_rows = cotangent[0]
    first_keys = key_heads * first_col.astype(jnp.bfloat16)
    last_keys = key_heads * last_col.astype(jnp.bfloat16)
    first_state = jnp.einsum(
        "jhd,jhe->hde", first_keys, value_heads, preferred_element_type=jnp.float32
    )
    last_state = jnp.einsum(
        "jhd,jhe->hde", last_keys, value_heads, preferred_element_type=jnp.float32
    )
    zero_state = jnp.zeros((head_count, HD, HD), jnp.float32)
    zero_flag = jnp.zeros((1, 1, 1), jnp.float32)
    weight_columns = lax.all_gather(out_weight, "dp", axis=1, tiled=True)
    full_weight = lax.all_gather(weight_columns, "tm", axis=0, tiled=True)
    left_state, unused_left = entering(
        (last_state, start_flag), "tm", combine_open, (zero_state, zero_flag), False
    )
    right_state, unused_right = entering(
        (first_state, start_flag), "tm", combine_open, (zero_state, zero_flag), True
    )
    scores = (
        jnp.einsum("ihd,jhd->hij", query_heads, key_heads, preferred_element_type=jnp.float32)
        * same_mask[None]
    ).astype(jnp.bfloat16)
    mixed_out = jnp.einsum("hij,jhe->ihe", scores, value_heads, preferred_element_type=jnp.float32)
    mixed_out = mixed_out + first_col * apply_state("ihd,hde->ihe", query_heads, left_state)
    mixed_out = mixed_out + last_col * apply_state("ihd,hde->ihe", query_heads, right_state)
    forward_attended = (
        (mixed_out * frame_scale[:, None, None])
        .astype(jnp.bfloat16)
        .reshape(frames, head_count * HD)
    )
    scores, attended = (scores, forward_attended)
    encoded = jnp.dot(attended, full_weight, preferred_element_type=jnp.float32).astype(
        jnp.bfloat16
    )
    scaled_cot = (
        lax.dot_general(
            cot_rows, full_weight, (((1,), (1,)), ((), ())), preferred_element_type=jnp.float32
        )
        * frame_scale[:, None]
    ).astype(jnp.bfloat16)
    cot_heads = scaled_cot.reshape(frames, head_count, HD)
    first_dstate = jnp.einsum(
        "jhd,jhe->hde",
        query_heads * first_col.astype(jnp.bfloat16),
        cot_heads,
        preferred_element_type=jnp.float32,
    )
    last_dstate = jnp.einsum(
        "jhd,jhe->hde",
        query_heads * last_col.astype(jnp.bfloat16),
        cot_heads,
        preferred_element_type=jnp.float32,
    )
    first_dstate, last_dstate = (first_dstate, last_dstate)
    left_grad, unused_lgrad = entering(
        (last_dstate, start_flag), "tm", combine_open, (zero_state, zero_flag), False
    )
    right_grad, unused_rgrad = entering(
        (first_dstate, start_flag), "tm", combine_open, (zero_state, zero_flag), True
    )
    grad_scores = (
        jnp.einsum("ihe,jhe->hij", cot_heads, value_heads, preferred_element_type=jnp.float32)
        * same_mask[None]
    ).astype(jnp.bfloat16)
    grad_query = jnp.einsum(
        "hij,jhd->ihd", grad_scores, key_heads, preferred_element_type=jnp.float32
    )
    grad_query = grad_query + first_col * apply_state("ihe,hde->ihd", cot_heads, left_state)
    grad_query = grad_query + last_col * apply_state("ihe,hde->ihd", cot_heads, right_state)
    grad_key = jnp.einsum(
        "hij,ihd->jhd", grad_scores, query_heads, preferred_element_type=jnp.float32
    )
    grad_key = grad_key + first_col * apply_state("jhe,hde->jhd", value_heads, left_grad)
    grad_key = grad_key + last_col * apply_state("jhe,hde->jhd", value_heads, right_grad)
    grad_value = jnp.einsum("hij,ihe->jhe", scores, cot_heads, preferred_element_type=jnp.float32)
    grad_value = grad_value + first_col * apply_state("jhd,hde->jhe", key_heads, left_grad)
    grad_value = grad_value + last_col * apply_state("jhd,hde->jhe", key_heads, right_grad)
    time_part = lax.psum_scatter(
        lax.dot_general(
            attended, cot_rows, (((0,), (0,)), ((), ())), preferred_element_type=jnp.float32
        ),
        "tm",
        scatter_dimension=0,
        tiled=True,
    )
    grad_weight = lax.psum_scatter(time_part, "dp", scatter_dimension=1, tiled=True)
    grad_weight = grad_weight / math.sqrt(dp_devices * total_frames)
    return (
        encoded[None],
        grad_query.astype(jnp.bfloat16).reshape(1, frames, head_count * HD),
        grad_key.astype(jnp.bfloat16).reshape(1, frames, head_count * HD),
        grad_value.astype(jnp.bfloat16).reshape(1, frames, head_count * HD),
        grad_weight,
    )


def solution(mesh):
    in_specs = (
        P("dp", "tm", None),
        P("dp", "tm", None),
        P("dp", "tm", None),
        P("dp", "tm", None),
        P("tm", "dp"),
        P("dp", None),
    )
    out_specs = (
        P("dp", "tm", None),
        P("dp", "tm", None),
        P("dp", "tm", None),
        P("dp", "tm", None),
        P("tm", "dp"),
    )
    return jax.shard_map(body, mesh=mesh, in_specs=in_specs, out_specs=out_specs, check_vma=False)
```

profile of v0, /device:TPU:1, one launch (start us, length us, event | category | flops | bytes accessed | tf_op | source)
XLA Modules:
  0.0 779.4 jit_solution(13463321952791285529)
XLA Ops:
  7.2 42.9 %all_gather.41 = bf16[32,2048]{1,0:T(8,128)(2,1)} all-gather(bf16[32,256]{1,0:T(8,128)(2,1)} %param.18), channel_id=1, replica_groups=mesh['dp'=8,'tm'=32] {'dp'}, dimensions={1}, use_global_device_ids=true | all-gather | bytes 147456 | tf_op jit(solution)/shard_map/all_gather | solution.py:80
  62.1 58.7 %all-gather.10.cloned.1.call-done = bf16[1024,2048]{1,0:T(8,128)(2,1)} async-done(((bf16[32,2048]{1,0:T(8,128)(2,1)}), bf16[1024,2048]{1,0:T(8,128)(2,1)}) %all-gather.10.cloned.1.call-update) | async-done | bytes 4194320 | tf_op jit(solution)/shard_map/all_gather | solution.py:81
  120.8 3.7 fusion.25
  129.7 68.4 %all-reduce = f32[32]{0:T(128)S(1)} all-reduce(f32[32]{0:T(128)S(1)} %dynamic-update-slice), channel_id=1, replica_groups=mesh['dp'=8,'tm'=32] {'tm'}, use_global_device_ids=true, to_apply=%add | all-reduce | flops 32 | bytes 256
  201.4 21.2 %all-gather.14.cloned.1.call-done = f32[256,128,128]{2,1,0:T(8,128)} async-done(((f32[8,128,128]{2,1,0:T(8,128)}), f32[256,128,128]{2,1,0:T(8,128)}) %all-gather.14.cloned.1.call-update) | async-done | bytes 16777232 | tf_op jit(solution)/shard_map/all_gather | solution.py:13
  222.6 11.7 %rev.10 = f32[32,8,128,128]{3,2,1,0:T(8,128)} reverse(f32[32,8,128,128]{3,2,1,0:T(8,128)} %bitcast.140), dimensions={0} | reverse | bytes 33554432 | tf_op jit(solution)/shard_map/rev | solution.py:15
  234.3 84.9 %while.57 = (s32[]{:T(128)}, f32[8,128,128]{2,1,0:T(8,128)S(1)}, s32[]{:T(128)}, f32[32,8,128,128]{3,2,1,0:T(8,128)}, f32[32,1,1,1]{0,3,2,1:T(1,128)S(1)}, /*index=5*/s32[]{:T(128)}, s32[]{:T(128)}) while((s32[]{:T(128)}, f32[8,128,128]{2,1,0:T(8,128)S(1)}, s32[]{:T(128)}, f32[32,8,128,128]{3,2,1,0:T(8,128)}, ...), condition=%wide.region_6.7_spmd.clone, body=%wide.region_5.6_spmd.clone.sunk | while | flops 524293 | bytes 1572989 | solution.py:25
  262.2 2.2 fusion.98
  265.0 2.2 fusion.98
  267.8 2.2 fusion.98
  270.6 2.2 fusion.98
  317.1 2.2 fusion.98
  321.8 3.2 all-gather.12.cloned.1.call-done
  325.0 84.8 %while.56 = (s32[]{:T(128)}, f32[8,128,128]{2,1,0:T(8,128)S(1)}, s32[]{:T(128)}, f32[32,8,128,128]{3,2,1,0:T(8,128)}, f32[32,1,1,1]{0,3,2,1:T(1,128)S(1)}, /*index=5*/s32[]{:T(128)}, s32[]{:T(128)}) while((s32[]{:T(128)}, f32[8,128,128]{2,1,0:T(8,128)S(1)}, s32[]{:T(128)}, f32[32,8,128,128]{3,2,1,0:T(8,128)}, ...), condition=%wide.region_4.5_spmd.clone, body=%wide.region_3.4_spmd.clone.sunk | while | flops 524293 | bytes 1572989 | solution.py:25
  342.0 2.2 fusion.96
  388.4 2.2 fusion.96
  391.2 2.2 fusion.96
  394.0 2.2 fusion.96
  396.8 2.2 fusion.96
  413.2 4.5 fusion.26
  417.9 3.8 fusion.4
  424.0 3.4 all-gather.18.cloned.1.call-done
  427.4 11.6 %rev.12 = f32[32,8,128,128]{3,2,1,0:T(8,128)} reverse(f32[32,8,128,128]{3,2,1,0:T(8,128)} %bitcast.139), dimensions={0} | reverse | bytes 33554432 | tf_op jit(solution)/shard_map/rev | solution.py:15
  439.0 84.9 %while.59 = (s32[]{:T(128)}, f32[8,128,128]{2,1,0:T(8,128)S(1)}, s32[]{:T(128)}, f32[32,8,128,128]{3,2,1,0:T(8,128)}, f32[32,1,1,1]{0,3,2,1:T(1,128)S(1)}, /*index=5*/s32[]{:T(128)}, s32[]{:T(128)}) while((s32[]{:T(128)}, f32[8,128,128]{2,1,0:T(8,128)S(1)}, s32[]{:T(128)}, f32[32,8,128,128]{3,2,1,0:T(8,128)}, ...), condition=%wide.region_11.12_spmd.clone, body=%wide.region_10.11_spmd.clone.sunk | while | flops 524293 | bytes 1572989 | solution.py:25
  466.9 2.2 fusion.102
  469.7 2.2 fusion.102
  472.5 2.2 fusion.102
  475.2 2.2 fusion.102
  525.4 4.3 all-gather.16.cloned.1.call-done
  529.7 84.5 %while.58 = (s32[]{:T(128)}, f32[8,128,128]{2,1,0:T(8,128)S(1)}, s32[]{:T(128)}, f32[32,8,128,128]{3,2,1,0:T(8,128)}, f32[32,1,1,1]{0,3,2,1:T(1,128)S(1)}, /*index=5*/s32[]{:T(128)}, s32[]{:T(128)}) while((s32[]{:T(128)}, f32[8,128,128]{2,1,0:T(8,128)S(1)}, s32[]{:T(128)}, f32[32,8,128,128]{3,2,1,0:T(8,128)}, ...), condition=%wide.region_9.10_spmd.clone, body=%wide.region_8.9_spmd.clone.sunk | while | flops 524293 | bytes 1572989 | solution.py:25
  617.6 67.2 %reduce-scatter.3.cloned.1.call-done = f32[32,2048]{1,0:T(8,128)} async-done(((f32[1024,2048]{1,0:T(8,128)}), f32[32,2048]{1,0:T(8,128)}) %reduce-scatter.3.cloned.1.call-update) | async-done | bytes 262160 | tf_op jit(solution)/shard_map/reduce_scatter | solution.py:147
  686.5 84.7 %reduce-scatter.5.cloned.1.call-done = f32[32,256]{1,0:T(8,128)} async-done(((f32[32,2048]{1,0:T(8,128)}), f32[32,256]{1,0:T(8,128)}) %reduce-scatter.5.cloned.1.call-update) | async-done | bytes 32784 | tf_op jit(solution)/shard_map/reduce_scatter | solution.py:155
  (311 shorter events, 342.0 us)
Async XLA Ops:
  7.2 113.6 %copy-start = (bf16[1,128,2048]{2,1,0:T(8,128)(2,1)S(1)}, bf16[1,128,2048]{2,1,0:T(8,128)(2,1)}, u32[]{:S(2)}) copy-start(bf16[1,128,2048]{2,1,0:T(8,128)(2,1)} %param.17) | copy-start | bytes 1572868
  7.2 113.6 %all-gather.10.cloned.1.call-start = ((), (), s32[]{:S(2)}) async-start(), calls=%async_computation.2 | async-start | bytes 4325376 | tf_op jit(solution)/shard_map/all_gather | solution.py:81
  50.2 172.4 %all-gather.14.cloned.1.call-start = ((), (), s32[]{:S(2)}) async-start(), calls=%async_computation.6 | async-start | bytes 17301504 | tf_op jit(solution)/shard_map/all_gather | solution.py:13
  51.2 75.8 %copy-start.1 = (bf16[16,8,8,128]{3,2,1,0:T(8,128)(2,1)}, bf16[16,8,8,128]{3,2,1,0:T(8,128)(2,1)S(1)}, u32[]{:S(2)}) copy-start(bf16[16,8,8,128]{3,2,1,0:T(8,128)(2,1)S(1)} %copy.110) | copy-start | bytes 786436
  51.5 75.6 %copy-start.3 = (bf16[128,8,128]{0,2,1:T(8,128)(2,1)}, bf16[128,8,128]{0,2,1:T(8,128)(2,1)S(1)}, u32[]{:S(2)}) copy-start(bf16[128,8,128]{0,2,1:T(8,128)(2,1)S(1)} %copy.76) | copy-start | bytes 786436
  57.6 267.5 %all-gather.12.cloned.1.call-start = ((), (), s32[]{:S(2)}) async-start(), calls=%async_computation.5 | async-start | bytes 17301504 | tf_op jit(solution)/shard_map/all_gather | solution.py:13
  59.3 368.0 %all-gather.18.cloned.1.call-start = ((), (), s32[]{:S(2)}) async-start(), calls=%async_computation.8 | async-start | bytes 17301504 | tf_op jit(solution)/shard_map/all_gather | solution.py:13
  125.8 403.9 %all-gather.16.cloned.1.call-start = ((), (), s32[]{:S(2)}) async-start(), calls=%async_computation.7 | async-start | bytes 17301504 | tf_op jit(solution)/shard_map/all_gather | solution.py:13
  127.0 557.9 %reduce-scatter.3.cloned.1.call-start = ((), (), s32[]{:S(2)}) async-start(), calls=%async_computation.3 | async-start | bytes 8650752 | tf_op jit(solution)/shard_map/reduce_scatter | solution.py:147
  325.0 96.7 %copy-start.4 = (bf16[128,8,128]{0,2,1:T(8,128)(2,1)S(1)}, bf16[128,8,128]{0,2,1:T(8,128)(2,1)}, u32[]{:S(2)}) copy-start(bf16[128,8,128]{0,2,1:T(8,128)(2,1)} %copy-done.3) | copy-start | bytes 786436
  411.6 10.1 %copy-start.7 = (f32[128,8,128]{0,2,1:T(8,128)S(1)}, f32[128,8,128]{0,2,1:T(8,128)}, u32[]{:S(2)}) copy-start(f32[128,8,128]{0,2,1:T(8,128)} %fusion.15) | copy-start | bytes 1572868
  417.7 353.6 %reduce-scatter.5.cloned.1.call-start = ((), (), s32[]{:S(2)}) async-start(), calls=%async_computation.4 | async-start | bytes 294912 | tf_op jit(solution)/shard_map/reduce_scatter | solution.py:155
  439.0 175.9 %copy-start.5 = (bf16[8,128,128]{2,1,0:T(8,128)(2,1)S(1)}, bf16[8,128,128]{2,1,0:T(8,128)(2,1)}, u32[]{:S(2)}) copy-start(bf16[8,128,128]{2,1,0:T(8,128)(2,1)} %fusion.24) | copy-start | bytes 786436
  439.0 178.0 %copy-start.2 = (bf16[16,8,8,128]{3,2,1,0:T(8,128)(2,1)S(1)}, bf16[16,8,8,128]{3,2,1,0:T(8,128)(2,1)}, u32[]{:S(2)}) copy-start(bf16[16,8,8,128]{3,2,1,0:T(8,128)(2,1)} %copy-done.1) | copy-start | bytes 786436
  439.0 246.5 %copy-start.6 = (bf16[8,128,128]{2,1,0:T(8,128)(2,1)S(1)}, bf16[8,128,128]{2,1,0:T(8,128)(2,1)}, u32[]{:S(2)}) copy-start(bf16[8,128,128]{2,1,0:T(8,128)(2,1)} %fusion.23) | copy-start | bytes 786436
Sparse Core Ops, SparseCore 0:
  50.3 70.4 all-gather.9
  123.2 99.3 all-gather.13
  224.5 100.5 all-gather.11
  326.7 100.5 all-gather.17
  429.1 100.5 all-gather.15
  532.1 152.6 reduce-scatter.2
  688.7 82.4 reduce-scatter.4
where the time goes:
time: 788 us; the launch traced here: 779 us
  other arithmetic  343 us (44%)
  waiting for transfers between devices  243 us (31%)
  blocking collectives  111 us (14%)
  local copies, waits for them, and re-layouts  32.9 us (4%)
  matrix products  31.4 us (4%)
  between operations  15.7 us (2%)
    select_n x124, other arithmetic, step(): jnp.where(position < mine, new, old)  265 us
    reduce_scatter x1, waiting for transfers between devices, body(): lax.psum_scatter(time_part, 'dp', scatter_dimension=1, tiled=True)  84.7 us
    sub x124, other arithmetic, combine_open(): keeping = 1.0 - following[-1]  72.6 us
    unnamed x1, blocking collectives  68.4 us
    reduce_scatter x1, waiting for transfers between devices, body(): lax.psum_scatter(lax.dot_general(attended, cot_rows, (((0,), (0,)), ((),...  67.2 us
    all_gather x1, waiting for transfers between devices, body(): full_weight = lax.all_gather(weight_columns, 'tm', axis=0, tiled=True)  58.7 us
    all_gather x1, blocking collectives, body(): weight_columns = lax.all_gather(out_weight, 'dp', axis=1, tiled=True)  42.9 us
    all_gather x4, waiting for transfers between devices, entering(): pieces = jax.tree.map(lambda part: lax.all_gather(part, axis), value)  32.1 us
  transfers between devices with their start and end apart: 7, of which 7 were waited for; matrix products, arithmetic and copies ran while one was open for 52% of the time, Pallas kernels for 0%

commit v1 on v0

v1 whole, which is shorter than its diff:
```python
import math

import jax
import jax.numpy as jnp
import numpy as np
from jax import lax
from jax.sharding import Mesh
from jax.sharding import PartitionSpec as P

HD = 128
Y, H, Z, X, C = 4, 2, 4, 4, 2
PLANE = ("x", "c")
ACROSS = ("y", "h", "z")
ALL = ("y", "h", "z", "x", "c")
BF = jnp.bfloat16
F32 = jnp.float32


def flat(y, h, z, x, c):
    return (((y * H + h) * Z + z) * X + x) * C + c


def swap_pairs():
    return [
        (flat(y, h, z, x, c), flat(y, c, x, z, h))
        for y in range(Y)
        for h in range(H)
        for z in range(Z)
        for x in range(X)
        for c in range(C)
    ]


def mm(a, b, dims):
    return lax.dot_general(a, b, (dims, ((), ())), preferred_element_type=F32)


def body(queries, key_vectors, values, cotangent, out_weight, offsets):
    plane = lax.axis_index("z")
    core = lax.axis_index("c")
    frames = queries.shape[1]
    chunk = frames * X * C
    length = chunk * Z
    starts = offsets[0]
    utts = starts.shape[0]

    positions = plane * chunk + jnp.arange(chunk, dtype=jnp.int32)
    utterance = jnp.sum((positions[:, None] >= starts[None, :]).astype(jnp.int32), axis=1) - 1
    ends = jnp.concatenate([starts[1:], jnp.full((1,), length, jnp.int32)])
    picked = utterance[:, None] == jnp.arange(utts, dtype=jnp.int32)[None, :]
    span = jnp.sum(jnp.where(picked, (ends - starts)[None, :], 0), axis=1)
    scale = (1.0 / jnp.sqrt((HD * span).astype(F32)))[:, None]
    mask = picked.astype(BF)
    plane_first = jnp.arange(Z, dtype=jnp.int32) * chunk
    first_utt = jnp.sum((plane_first[:, None] >= starts[None, :]).astype(jnp.int32), axis=1) - 1
    last_utt = (
        jnp.sum((plane_first[:, None] + (chunk - 1) >= starts[None, :]).astype(jnp.int32), axis=1)
        - 1
    )
    slots = jnp.arange(utts, dtype=jnp.int32)
    other = (jnp.arange(Z) != plane)[:, None]
    take_first = ((slots[None, :] == first_utt[:, None]) & other).astype(F32)
    take_last = (
        (slots[None, :] == last_utt[:, None]) & other & (last_utt != first_utt)[:, None]
    ).astype(F32)

    def spread(rows):
        return (rows[:, None, :] * mask[:, :, None]).reshape(chunk, utts * HD)

    def totals(left, right):
        own = mm(spread(left), right, ((0,), (0,))).reshape(utts, HD, HD)
        first = lax.dynamic_index_in_dim(own, first_utt[plane], 0, False)
        last = lax.dynamic_index_in_dim(own, last_utt[plane], 0, False)
        edge = jnp.stack([first, last])
        edges = lax.all_to_all(jnp.broadcast_to(edge[None], (Z, 2, HD, HD)), "z", 0, 0, tiled=True)
        for z in range(Z):
            own = own + take_first[z][:, None, None] * edges[z, 0]
            own = own + take_last[z][:, None, None] * edges[z, 1]
        return own.astype(BF)

    heads = jnp.stack(
        [
            part[0].reshape(frames, X * C, HD).transpose(1, 0, 2)
            for part in (queries, key_vectors, values)
        ],
        axis=1,
    )
    heads = lax.all_to_all(heads, PLANE, 0, 0, tiled=True)
    query, key, value = (heads[:, i].reshape(chunk, HD) for i in range(3))

    moved = lax.ppermute(out_weight, ALL, swap_pairs())
    group = Y * H * Z
    pieces = lax.all_to_all(
        jnp.broadcast_to(moved[None], (group,) + moved.shape), ACROSS, 0, 0, tiled=True
    )
    rows, cols = moved.shape
    block = (
        pieces.reshape(Y, H, Z, rows, cols).transpose(2, 1, 3, 0, 4).reshape(2 * HD, Y * cols)
    )
    weight = lax.all_gather(block, PLANE, axis=0)

    cot_half = cotangent[0].reshape(frames, Y, C, cols).transpose(2, 0, 1, 3)
    cot_half = cot_half.reshape(1, C, frames, Y * cols)
    cot = lax.all_to_all(
        jnp.broadcast_to(cot_half, (X, C, frames, Y * cols)).reshape(X * C, frames, Y * cols),
        PLANE,
        0,
        0,
        tiled=True,
    ).reshape(chunk, Y * cols)

    state = totals(key, value).reshape(utts * HD, HD)
    attended = (mm(spread(query), state, ((1,), (0,))) * scale).astype(BF)

    back = mm(cot, block, ((1,), (1,)))
    swap = [(0, 1), (1, 0)]
    mine = lax.dynamic_slice_in_dim(back, core * HD, HD, 1)
    theirs = lax.dynamic_slice_in_dim(back, (1 - core) * HD, HD, 1)
    scaled_cot = ((mine + lax.ppermute(theirs, "c", swap)) * scale).astype(BF)

    partner = lax.ppermute(attended, "c", swap)
    low = jnp.where(core == 0, attended, partner)
    high = jnp.where(core == 0, partner, attended)
    pair = jnp.concatenate([low, high], axis=1)
    term = mm(pair, cot, ((0,), (0,))).astype(BF)
    term = term.reshape(Z, H, rows, Y, cols).transpose(3, 1, 0, 2, 4).reshape(group, rows, cols)
    term = lax.all_to_all(term, ACROSS, 0, 0, tiled=True)
    grad_weight = jnp.sum(term.astype(F32), axis=0) / math.sqrt(Y * H * length)
    grad_weight = lax.ppermute(grad_weight, ALL, swap_pairs())

    grad = totals(query, scaled_cot)
    spread_key = spread(key)
    grad_value = mm(spread_key, grad.reshape(utts * HD, HD), ((1,), (0,))).astype(BF)
    grad_t = grad.transpose(0, 2, 1).reshape(utts * HD, HD)
    grad_key = mm(spread(value), grad_t, ((1,), (0,))).astype(BF)
    state_t = state.reshape(utts, HD, HD).transpose(0, 2, 1).reshape(utts * HD, HD)
    grad_query = mm(spread(scaled_cot), state_t, ((1,), (0,))).astype(BF)

    def home(parts):
        stacked = jnp.stack([part.reshape(X * C, frames, HD) for part in parts], axis=1)
        got = lax.all_to_all(stacked, PLANE, 0, 0, tiled=True)
        return [
            got[:, i].transpose(1, 0, 2).reshape(frames, X * C * HD) for i in range(len(parts))
        ]

    (attended_rows,) = home([attended])
    wide = weight.reshape(X, C, 2 * HD, Y, cols)
    encoded = jnp.stack(
        [mm(attended_rows, wide[:, c].reshape(X * 2 * HD, Y * cols), ((1,), (0,))) for c in range(C)]
    ).astype(BF)
    encoded = encoded.reshape(C, frames, Y, cols).transpose(1, 2, 0, 3).reshape(frames, Y * C * cols)
    grads = home([grad_query, grad_key, grad_value])
    return (encoded[None], grads[0][None], grads[1][None], grads[2][None], grad_weight)


def solution(mesh):
    fine = Mesh(np.asarray(mesh.devices).reshape(Y, H, Z, X, C), ALL)
    dp, tm = ("y", "h"), ("z", "x", "c")
    three = P(dp, tm, None)
    in_specs = (three, three, three, three, P(tm, dp), P(dp, None))
    out_specs = (three, three, three, three, P(tm, dp))
    return jax.shard_map(body, mesh=fine, in_specs=in_specs, out_specs=out_specs, check_vma=False)
```

time: 788 us -> 258 us (0.33)
  other arithmetic: 343 us -> 4.15 us
  waiting for transfers between devices: 243 us -> 75.6 us
  blocking collectives: 111 us -> 0 us
  starting transfers between devices: 0.47 us -> 66.1 us
  local copies, waits for them, and re-layouts: 32.9 us -> 72.4 us
  matrix products: 31.4 us -> 19 us
    select_n x124 -> x1, other arithmetic: 265 us -> 1.07 us  [body(): low = jnp.where(core == 0, attended, partner)]
    reduce_scatter x2 -> x0, waiting for transfers between devices: 152 us -> none  [the longest x1 84.7 us: body(): lax.psum_scatter(time_part, 'dp', scatter_dimension=1, tiled=True)]
    all_gather x5 -> x1, waiting for transfers between devices: 90.8 us -> 0.01 us  [body(): weight = lax.all_gather(block, PLANE, axis=0)]
    sub x125 -> x2, other arithmetic: 72.6 us -> 0.01 us  [the longest x1 0.01 us: body(): jnp.sum((plane_first[:, None] + (chunk - 1) >= starts[None, :]).astype(jn...]
    all_to_all x0 -> x8, waiting for transfers between devices: none -> 70.4 us  [the longest x1 35.5 us: body(): lax.all_to_all(jnp.broadcast_to(cot_half, (X, C, frames, Y * cols)).resha...]
    unnamed x1 -> x0, blocking collectives: 68.4 us -> none
    all_to_all x0 -> x8, starting transfers between devices: none -> 49.2 us  [the longest x2 12.6 us: home(): got = lax.all_to_all(stacked, PLANE, 0, 0, tiled=True)]
    all_gather x1 -> x0, blocking collectives: 42.9 us -> none  [body(): weight_columns = lax.all_gather(out_weight, 'dp', axis=1, tiled=True)]
  transfers between devices with their start and end apart: 7 -> 13, of which waited for: 7 -> 10; matrix products, arithmetic and copies ran while one was open for 52% -> 22% of each run, Pallas kernels for 0% -> 0%
where the time goes in v1:
time: 258 us; the launch traced here: 256 us
  waiting for transfers between devices  75.6 us (29%)
  local copies, waits for them, and re-layouts  72.4 us (28%)
  starting transfers between devices  66.1 us (26%)
  matrix products  19 us (7%)
  between operations  18.7 us (7%)
  other arithmetic  4.15 us (2%)
    all_to_all x1, waiting for transfers between devices, body(): lax.all_to_all(jnp.broadcast_to(cot_half, (X, C, frames, Y * cols)).resha...  35.5 us
    dot_general x10, matrix products, mm(): return lax.dot_general(a, b, (dims, ((), ())), preferred_element_type=F32)  19 us
    unnamed x69, local copies, waits for them, and re-layouts  15.8 us
    all_to_all x2, starting transfers between devices, home(): got = lax.all_to_all(stacked, PLANE, 0, 0, tiled=True)  12.6 us
    all_to_all x2, waiting for transfers between devices, totals(): lax.all_to_all(jnp.broadcast_to(edge[None], (Z, 2, HD, HD)), 'z', 0, 0, t...  12 us
    slice x3, local copies, waits for them, and re-layouts, body(): wide[:, c].reshape(X * 2 * HD, Y * cols)  12 us
    all_to_all x1, starting transfers between devices, body(): heads = lax.all_to_all(heads, PLANE, 0, 0, tiled=True)  11.2 us
    dot_general x4, local copies, waits for them, and re-layouts, mm(): return lax.dot_general(a, b, (dims, ((), ())), preferred_element_type=F32)  10.5 us
  transfers between devices with their start and end apart: 13, of which 10 were waited for; matrix products, arithmetic and copies ran while one was open for 22% of the time, Pallas kernels for 0%

profile of v1, /device:TPU:1, one launch (start us, length us, event | category | flops | bytes accessed | tf_op | source)
XLA Modules:
  0.0 255.9 jit_solution(8613500606594378341)
XLA Ops:
  7.2 10.2 %collective-permute-start = (bf16[32,256]{1,0:T(8,128)(2,1)}, bf16[32,256]{1,0:T(8,128)(2,1)S(1)}, u32[]{:S(2)}, u32[]{:S(2)}) collective-permute-start(bf16[32,256]{1,0:T(8,128)(2,1)} %param.10), channel_id=1, source_target_pairs={{0,0},{1,32},{2,8},{3,40},{4,16},{5,48},{6,24},{7,56},{8,2},{9,34}... | collective-permute-start | bytes 49160 | tf_op jit(solution)/shard_map/ppermute | solution.py:91
  19.9 7.6 %all-to-all-start.3 = ((bf16[32,32,256]{2,1,0:T(8,128)(2,1)}), bf16[32,32,256]{2,1,0:T(8,128)(2,1)S(1)}, u32[]{:S(2)}, u32[]{:S(2)}) async-start(bf16[32,32,256]{2,1,0:T(8,128)(2,1)} %broadcast_in_dim.28), calls=%async_computation.3 | async-start | bytes 1048576 | tf_op jit(solution)/shard_map/all_to_all | solution.py:93
  32.2 7.7 %all-to-all-done.3 = bf16[32,32,256]{2,1,0:T(8,128)(2,1)S(1)} async-done(((bf16[32,32,256]{2,1,0:T(8,128)(2,1)}), bf16[32,32,256]{2,1,0:T(8,128)(2,1)S(1)}, u32[]{:S(2)}, u32[]{:S(2)}) %all-to-all-start.3) | async-done | bytes 524320 | tf_op jit(solution)/shard_map/all_to_all | solution.py:93
  39.9 11.2 %all-to-all-start = ((bf16[8,3,128,128]{3,2,1,0:T(8,128)(2,1)}), bf16[8,3,128,128]{3,2,1,0:T(8,128)(2,1)S(1)}, u32[]{:S(2)}, u32[]{:S(2)}) async-start(bf16[8,3,128,128]{3,2,1,0:T(8,128)(2,1)} %copy.246), calls=%async_computation | async-start | bytes 1572864 | tf_op jit(solution)/shard_map/all_to_all | solution.py:88
  58.8 4.6 %all-to-all-done = bf16[8,3,128,128]{3,2,1,0:T(8,128)(2,1)S(1)} async-done(((bf16[8,3,128,128]{3,2,1,0:T(8,128)(2,1)}), bf16[8,3,128,128]{3,2,1,0:T(8,128)(2,1)S(1)}, u32[]{:S(2)}, u32[]{:S(2)}) %all-to-all-start) | async-done | bytes 786464 | tf_op jit(solution)/shard_map/all_to_all | solution.py:88
  65.0 4.4 %all-to-all-start.4 = ((bf16[8,128,1024]{2,1,0:T(8,128)(2,1)}), bf16[8,128,1024]{2,1,0:T(8,128)(2,1)S(1)}, u32[]{:S(2)}, u32[]{:S(2)}) async-start(bf16[8,128,1024]{2,1,0:T(8,128)(2,1)} %bitcast.55), calls=%async_computation.4 | async-start | bytes 4194304 | tf_op jit(solution)/shard_map/all_to_all | solution.py:104
  72.7 2.0 fusion.5
  75.6 35.5 %all-to-all-done.4 = bf16[8,128,1024]{2,1,0:T(8,128)(2,1)S(1)} async-done(((bf16[8,128,1024]{2,1,0:T(8,128)(2,1)}), bf16[8,128,1024]{2,1,0:T(8,128)(2,1)S(1)}, u32[]{:S(2)}, u32[]{:S(2)}) %all-to-all-start.4) | async-done | bytes 2097184 | tf_op jit(solution)/shard_map/all_to_all | solution.py:104
  112.0 4.5 %all-to-all-start.1 = ((f32[4,2,128,128]{3,2,1,0:T(8,128)}), f32[4,2,128,128]{3,2,1,0:T(8,128)S(1)}, u32[]{:S(2)}, u32[]{:S(2)}) async-start(f32[4,2,128,128]{3,2,1,0:T(8,128)} %broadcast_in_dim.24), calls=%async_computation.1 | async-start | bytes 1048576 | tf_op jit(solution)/shard_map/all_to_all | solution.py:75
  116.7 2.3 copy.250
  124.5 6.0 %all-to-all-done.1 = f32[4,2,128,128]{3,2,1,0:T(8,128)S(1)} async-done(((f32[4,2,128,128]{3,2,1,0:T(8,128)}), f32[4,2,128,128]{3,2,1,0:T(8,128)S(1)}, u32[]{:S(2)}, u32[]{:S(2)}) %all-to-all-start.1) | async-done | bytes 524320 | tf_op jit(solution)/shard_map/all_to_all | solution.py:75
  137.1 3.6 %fusion.37 = bf16[1024,128]{1,0:T(8,128)(2,1)} fusion(bf16[1024,12]{0,1:T(8,128)(2,1)} %copy-done.19, bf16[1024,128]{0,1:T(8,128)(2,1)S(1)} %copy-done.11, f32[12,128,128]{1,2,0:T(8,128)} %copy.250, f32[128,128]{0,1:T(8,128)} %copy.257, f32[12]{0:T(128)} %get-tuple-element.83, f32[128,128]{0,1:T(8,128)} %copy.256, f32[12]{0:T(128)S(1)} %get-tuple-element.79, ...), kind=kOutput, calls=%fused_computation.30 | convolution fusion | flops 407830528 | bytes 1864064 | tf_op jit(solution)/shard_map/dot_general | solution.py:35
  142.1 4.0 %all-to-all-start.2 = ((bf16[8,1,128,128]{3,2,1,0:T(8,128)(2,1)}), bf16[8,1,128,128]{3,2,1,0:T(8,128)(2,1)}, u32[]{:S(2)}, u32[]{:S(2)}) async-start(bf16[8,1,128,128]{3,2,1,0:T(8,128)(2,1)} %bitcast.38), calls=%async_computation.2 | async-start | bytes 524288 | tf_op jit(solution)/shard_map/all_to_all | solution.py:141
  150.3 2.3 all-to-all-done.2
  153.4 3.7 %all-to-all-start.5 = ((f32[4,2,128,128]{2,3,1,0:T(8,128)}), f32[4,2,128,128]{2,3,1,0:T(8,128)S(1)}, u32[]{:S(2)}, u32[]{:S(2)}) async-start(f32[4,2,128,128]{2,3,1,0:T(8,128)} %broadcast_in_dim.31), calls=%async_computation.5 | async-start | bytes 1048576 | tf_op jit(solution)/shard_map/all_to_all | solution.py:75
  161.8 3.1 %fusion.46 = bf16[1024,128]{1,0:T(8,128)(2,1)} fusion(bf16[1024,128]{0,1:T(8,128)(2,1)S(1)} %copy.273, bf16[1024,12]{0,1:T(8,128)(2,1)} %copy-done.19, f32[12,128,128]{2,1,0:T(8,128)S(1)} %copy-done.1, f32[128,128]{0,1:T(8,128)} %get-tuple-element.53, f32[128,128]{0,1:T(8,128)} %get-tuple-element.52, f32[128,128]{0,1:T(8,128)} %get-tuple-element.51, ...), kind=kOutput, calls=%fused_computation.33 | convolution fusion | flops 407699456 | bytes 1859968 | tf_op jit(solution)/shard_map/dot_general | solution.py:35
  164.9 6.0 %all-to-all-done.5 = f32[4,2,128,128]{2,3,1,0:T(8,128)S(1)} async-done(((f32[4,2,128,128]{2,3,1,0:T(8,128)}), f32[4,2,128,128]{2,3,1,0:T(8,128)S(1)}, u32[]{:S(2)}, u32[]{:S(2)}) %all-to-all-start.5) | async-done | bytes 524320 | tf_op jit(solution)/shard_map/all_to_all | solution.py:75
  170.9 5.2 %all-to-all-start.7 = ((bf16[32,32,256]{2,1,0:T(8,128)(2,1)}), bf16[32,32,256]{2,1,0:T(8,128)(2,1)S(1)}, u32[]{:S(2)}, u32[]{:S(2)}) async-start(bf16[32,32,256]{2,1,0:T(8,128)(2,1)} %bitcast.107), calls=%async_computation.7 | async-start | bytes 1048576 | tf_op jit(solution)/shard_map/all_to_all | solution.py:127
  179.1 2.3 fusion.43
  183.9 5.3 %all-to-all-done.7 = bf16[32,32,256]{2,1,0:T(8,128)(2,1)S(1)} async-done(((bf16[32,32,256]{2,1,0:T(8,128)(2,1)}), bf16[32,32,256]{2,1,0:T(8,128)(2,1)S(1)}, u32[]{:S(2)}, u32[]{:S(2)}) %all-to-all-start.7) | async-done | bytes 524320 | tf_op jit(solution)/shard_map/all_to_all | solution.py:127
  189.1 8.7 %all-to-all-start.6 = ((bf16[8,3,128,128]{3,2,1,0:T(8,128)(2,1)}), bf16[8,3,128,128]{3,2,1,0:T(8,128)(2,1)S(1)}, u32[]{:S(2)}, u32[]{:S(2)}) async-start(bf16[8,3,128,128]{3,2,1,0:T(8,128)(2,1)} %pad_maximum_fusion.1), calls=%async_computation.6 | async-start | bytes 1572864 | tf_op jit(solution)/shard_map/all_to_all | solution.py:141
  197.9 4.3 %collective-permute-start.3 = (f32[32,256]{1,0:T(8,128)S(1)}, f32[32,256]{1,0:T(8,128)S(1)}, u32[]{:S(2)}, u32[]{:S(2)}) collective-permute-start(f32[32,256]{1,0:T(8,128)S(1)} %broadcast_multiply_fusion), channel_id=1, source_target_pairs={{0,0},{1,32},{2,8},{3,40},{4,16},{5,48},{6,24},{7,56},{8,2},{9,34}... | collective-permute-start | bytes 98312 | tf_op jit(solution)/shard_map/ppermute | solution.py:129
  203.5 3.6 %collective-permute-done.3 = f32[32,256]{1,0:T(8,128)S(1)} collective-permute-done((f32[32,256]{1,0:T(8,128)S(1)}, f32[32,256]{1,0:T(8,128)S(1)}, u32[]{:S(2)}, u32[]{:S(2)}) %collective-permute-start.3) | collective-permute-done | bytes 32800 | tf_op jit(solution)/shard_map/ppermute | solution.py:129
  207.0 3.1 %all-to-all-done.6 = bf16[8,3,128,128]{3,2,1,0:T(8,128)(2,1)S(1)} async-done(((bf16[8,3,128,128]{3,2,1,0:T(8,128)(2,1)}), bf16[8,3,128,128]{3,2,1,0:T(8,128)(2,1)S(1)}, u32[]{:S(2)}, u32[]{:S(2)}) %all-to-all-start.6) | async-done | bytes 786464 | tf_op jit(solution)/shard_map/all_to_all | solution.py:141
  213.3 6.5 %copy.263 = bf16[8,256,1024]{1,2,0:T(8,128)(2,1)} copy(bf16[8,256,1024]{2,1,0:T(8,128)(2,1)} %all-gather.2.cloned.1.call-done) | data formatting | bytes 8388608 | tf_op jit(solution)/shard_map/all_gather | solution.py:100
  219.8 4.7 %fusion.82 = (bf16[4,1,256,4,256]{2,4,3,1,0:T(8,128)(2,1)}, bf16[4,1,256,4,256]{2,4,3,1,0:T(8,128)(2,1)}) fusion(bf16[4,2,256,4,256]{2,4,3,1,0:T(8,128)(2,1)} %bitcast.269), kind=kLoop, calls=%fused_computation.142 | loop fusion | bytes 8388608 | tf_op jit(solution)/shard_map/slice | solution.py:149
  224.5 3.0 %copy.264 = bf16[4,1,256,4,256]{4,3,2,0,1:T(4,128)(2,1)S(1)} copy(bf16[4,1,256,4,256]{2,4,3,1,0:T(8,128)(2,1)} %get-tuple-element.32) | data formatting | bytes 4194304 | tf_op jit(solution)/shard_map/slice | solution.py:149
  229.4 2.9 %copy.265 = bf16[1024,1024]{1,0:T(8,128)(2,1)S(1)} copy(bf16[1024,1024]{0,1:T(8,128)(2,1)} %bitcast.275) | data formatting | bytes 4194304 | tf_op jit(solution)/shard_map/dot_general | solution.py:35
  232.2 4.3 %copy.266 = bf16[4,1,256,4,256]{4,3,2,0,1:T(4,128)(2,1)} copy(bf16[4,1,256,4,256]{2,4,3,1,0:T(8,128)(2,1)} %get-tuple-element.33) | data formatting | bytes 4194304 | tf_op jit(solution)/shard_map/slice | solution.py:149
  236.5 3.4 %copy.314 = bf16[128,8,4,256]{3,1,2,0:T(8,128)(2,1)} copy(bf16[128,8,4,256]{3,2,1,0:T(4,128)(2,1)} %bitcast.276) | data formatting | bytes 4194304
  239.9 3.9 %copy.267 = bf16[1024,1024]{1,0:T(8,128)(2,1)} copy(bf16[1024,1024]{0,1:T(8,128)(2,1)} %bitcast.277) | data formatting | bytes 4194304 | tf_op jit(solution)/shard_map/dot_general | solution.py:35
  244.7 2.4 fusion.50
  (151 shorter events, 55.1 us)
Async XLA Ops:
  7.2 11.8 %collective-permute-start = (bf16[32,256]{1,0:T(8,128)(2,1)}, bf16[32,256]{1,0:T(8,128)(2,1)S(1)}, u32[]{:S(2)}, u32[]{:S(2)}) collective-permute-start(bf16[32,256]{1,0:T(8,128)(2,1)} %param.10), channel_id=1, source_target_pairs={{0,0},{1,32},{2,8},{3,40},{4,16},{5,48},{6,24},{7,56},{8,2},{9,34}... | collective-permute-start | bytes 49160 | tf_op jit(solution)/shard_map/ppermute | solution.py:91
  19.9 20.1 %all-to-all-start.3 = ((bf16[32,32,256]{2,1,0:T(8,128)(2,1)}), bf16[32,32,256]{2,1,0:T(8,128)(2,1)S(1)}, u32[]{:S(2)}, u32[]{:S(2)}) async-start(bf16[32,32,256]{2,1,0:T(8,128)(2,1)} %broadcast_in_dim.28), calls=%async_computation.3 | async-start | bytes 1048576 | tf_op jit(solution)/shard_map/all_to_all | solution.py:93
  27.5 23.6 %copy-start.21 = (s32[1,12]{1,0:T(1,128)S(1)}, s32[1,12]{1,0:T(1,128)}, u32[]{:S(2)}) copy-start(s32[1,12]{1,0:T(1,128)} %param.11) | copy-start | bytes 148
  27.5 27.7 %copy-start.7 = (bf16[1,128,2048]{2,1,0:T(8,128)(2,1)S(1)}, bf16[1,128,2048]{2,1,0:T(8,128)(2,1)}, u32[]{:S(2)}) copy-start(bf16[1,128,2048]{2,1,0:T(8,128)(2,1)} %param.9) | copy-start | bytes 1572868
  39.9 23.5 %all-to-all-start = ((bf16[8,3,128,128]{3,2,1,0:T(8,128)(2,1)}), bf16[8,3,128,128]{3,2,1,0:T(8,128)(2,1)S(1)}, u32[]{:S(2)}, u32[]{:S(2)}) async-start(bf16[8,3,128,128]{3,2,1,0:T(8,128)(2,1)} %copy.246), calls=%async_computation | async-start | bytes 1572864 | tf_op jit(solution)/shard_map/all_to_all | solution.py:88
  51.1 162.2 %all-gather.2.cloned.1.call-start = ((), (), s32[]{:S(2)}) async-start(), calls=%async_computation.8 | async-start | bytes 4718592 | tf_op jit(solution)/shard_map/all_gather | solution.py:100
  65.0 46.1 %all-to-all-start.4 = ((bf16[8,128,1024]{2,1,0:T(8,128)(2,1)}), bf16[8,128,1024]{2,1,0:T(8,128)(2,1)S(1)}, u32[]{:S(2)}, u32[]{:S(2)}) async-start(bf16[8,128,1024]{2,1,0:T(8,128)(2,1)} %bitcast.55), calls=%async_computation.4 | async-start | bytes 4194304 | tf_op jit(solution)/shard_map/all_to_all | solution.py:104
  70.6 4.9 %copy-start.19 = (bf16[1024,12]{0,1:T(8,128)(2,1)}, bf16[1024,12]{0,1:T(8,128)(2,1)S(1)}, u32[]{:S(2)}) copy-start(bf16[1024,12]{0,1:T(8,128)(2,1)S(1)} %fusion.73) | copy-start | bytes 73732
  74.7 46.1 %copy-start.6 = (bf16[8,1,128,128]{3,2,1,0:T(8,128)(2,1)S(1)}, bf16[8,1,128,128]{3,2,1,0:T(8,128)(2,1)}, u32[]{:S(2)}) copy-start(bf16[8,1,128,128]{3,2,1,0:T(8,128)(2,1)} %get-tuple-element.42) | copy-start | bytes 786436
  112.0 18.5 %all-to-all-start.1 = ((f32[4,2,128,128]{3,2,1,0:T(8,128)}), f32[4,2,128,128]{3,2,1,0:T(8,128)S(1)}, u32[]{:S(2)}, u32[]{:S(2)}) async-start(f32[4,2,128,128]{3,2,1,0:T(8,128)} %broadcast_in_dim.24), calls=%async_computation.1 | async-start | bytes 1048576 | tf_op jit(solution)/shard_map/all_to_all | solution.py:75
  122.5 14.6 %copy-start.11 = (bf16[1024,128]{0,1:T(8,128)(2,1)S(1)}, bf16[1024,128]{0,1:T(8,128)(2,1)}, u32[]{:S(2)}) copy-start(bf16[1024,128]{0,1:T(8,128)(2,1)} %copy.247) | copy-start | bytes 786436
  123.6 22.4 %collective-permute-start.1 = (f32[1024,128]{1,0:T(8,128)}, f32[1024,128]{1,0:T(8,128)}, u32[]{:S(2)}, u32[]{:S(2)}) collective-permute-start(f32[1024,128]{1,0:T(8,128)} %constant_dynamic-slice_fusion.2), channel_id=1, source_target_pairs={{0,1},{1,0},{2,3},{3,2},{4,5},{5,4},{6,7},{7,6},{8,9},{9,8},{10,11... | collective-permute-start | bytes 1572872 | tf_op jit(solution)/shard_map/ppermute | solution.py:119
  137.1 9.0 %copy-start.5 = (f32[1024,256]{1,0:T(8,128)S(1)}, f32[1024,256]{1,0:T(8,128)}, u32[]{:S(2)}) copy-start(f32[1024,256]{1,0:T(8,128)} %copy-done.4) | copy-start | bytes 3145732
  140.6 16.5 %collective-permute-start.2 = (bf16[1024,128]{1,0:T(8,128)(2,1)}, bf16[1024,128]{1,0:T(8,128)(2,1)}, u32[]{:S(2)}, u32[]{:S(2)}) collective-permute-start(bf16[1024,128]{1,0:T(8,128)(2,1)} %fusion.37), channel_id=1, source_target_pairs={{0,1},{1,0},{2,3},{3,2},{4,5},{5,4},{6,7},{7,6},{8,9},{9,8},{10,11... | collective-permute-start | bytes 786440 | tf_op jit(solution)/shard_map/ppermute | solution.py:121
  142.1 10.5 %all-to-all-start.2 = ((bf16[8,1,128,128]{3,2,1,0:T(8,128)(2,1)}), bf16[8,1,128,128]{3,2,1,0:T(8,128)(2,1)}, u32[]{:S(2)}, u32[]{:S(2)}) async-start(bf16[8,1,128,128]{3,2,1,0:T(8,128)(2,1)} %bitcast.38), calls=%async_computation.2 | async-start | bytes 524288 | tf_op jit(solution)/shard_map/all_to_all | solution.py:141
  153.4 17.4 %all-to-all-start.5 = ((f32[4,2,128,128]{2,3,1,0:T(8,128)}), f32[4,2,128,128]{2,3,1,0:T(8,128)S(1)}, u32[]{:S(2)}, u32[]{:S(2)}) async-start(f32[4,2,128,128]{2,3,1,0:T(8,128)} %broadcast_in_dim.31), calls=%async_computation.5 | async-start | bytes 1048576 | tf_op jit(solution)/shard_map/all_to_all | solution.py:75
  158.2 3.6 %copy-start.22 = (f32[12]{0:T(128)S(1)}, f32[12]{0:T(128)}, u32[]{:S(2)}) copy-start(f32[12]{0:T(128)} %get-tuple-element.81) | copy-start | bytes 148
  158.9 2.8 %copy-start.1 = (f32[12,128,128]{2,1,0:T(8,128)S(1)}, f32[12,128,128]{2,1,0:T(8,128)}, u32[]{:S(2)}) copy-start(f32[12,128,128]{2,1,0:T(8,128)} %copy-done) | copy-start | bytes 2359300
  164.9 14.1 %copy-start.3 = (f32[12,128,128]{2,1,0:T(8,128)S(1)}, f32[12,128,128]{2,1,0:T(8,128)}, u32[]{:S(2)}) copy-start(f32[12,128,128]{2,1,0:T(8,128)} %copy-done.2) | copy-start | bytes 2359300
  164.9 14.1 %copy-start.10 = (bf16[1024,128]{0,1:T(8,128)(2,1)S(1)}, bf16[1024,128]{0,1:T(8,128)(2,1)}, u32[]{:S(2)}) copy-start(bf16[1024,128]{0,1:T(8,128)(2,1)} %copy.276) | copy-start | bytes 786436
  170.9 18.3 %all-to-all-start.7 = ((bf16[32,32,256]{2,1,0:T(8,128)(2,1)}), bf16[32,32,256]{2,1,0:T(8,128)(2,1)S(1)}, u32[]{:S(2)}, u32[]{:S(2)}) async-start(bf16[32,32,256]{2,1,0:T(8,128)(2,1)} %bitcast.107), calls=%async_computation.7 | async-start | bytes 1048576 | tf_op jit(solution)/shard_map/all_to_all | solution.py:127
  178.9 2.5 copy-start.13
  179.0 2.5 copy-start.14
  179.0 2.5 copy-start.15
  179.0 2.5 copy-start.16
  179.0 2.5 copy-start.17
  179.0 2.5 copy-start.18
  179.0 2.5 copy-start.20
  179.0 2.5 copy-start.23
  179.0 2.5 copy-start.24
  189.1 21.0 %all-to-all-start.6 = ((bf16[8,3,128,128]{3,2,1,0:T(8,128)(2,1)}), bf16[8,3,128,128]{3,2,1,0:T(8,128)(2,1)S(1)}, u32[]{:S(2)}, u32[]{:S(2)}) async-start(bf16[8,3,128,128]{3,2,1,0:T(8,128)(2,1)} %pad_maximum_fusion.1), calls=%async_computation.6 | async-start | bytes 1572864 | tf_op jit(solution)/shard_map/all_to_all | solution.py:141
  197.9 9.2 %collective-permute-start.3 = (f32[32,256]{1,0:T(8,128)S(1)}, f32[32,256]{1,0:T(8,128)S(1)}, u32[]{:S(2)}, u32[]{:S(2)}) collective-permute-start(f32[32,256]{1,0:T(8,128)S(1)} %broadcast_multiply_fusion), channel_id=1, source_target_pairs={{0,0},{1,32},{2,8},{3,40},{4,16},{5,48},{6,24},{7,56},{8,2},{9,34}... | collective-permute-start | bytes 98312 | tf_op jit(solution)/shard_map/ppermute | solution.py:129
  (8 other events, 13.8 us)
Sparse Core Ops, SparseCore 0:
  58.8 47.9 all-gather.1

commit v2 on v1

v2 whole, which is shorter than its diff:
```python
import math

import jax
import jax.numpy as jnp
import numpy as np
from jax import lax
from jax.experimental import pallas as pl
from jax.experimental.pallas import tpu as pltpu
from jax.sharding import Mesh
from jax.sharding import PartitionSpec as P

HD = 128
FRAMES = 128
Y, H, Z, X, C = 4, 2, 4, 4, 2
BLOCKS = X * C
CHUNK = BLOCKS * FRAMES
LENGTH = Z * CHUNK
UTTS = 12
ROWS = 32
COLS = 256
HALF = Y * COLS
ALL = ("y", "h", "z", "x", "c")
PLANE = ("x", "c")
ACROSS = ("y", "h", "z")
BF = jnp.bfloat16
F32 = jnp.float32

VMEM = pl.BlockSpec(memory_space=pltpu.VMEM)
SMEM = pl.BlockSpec(memory_space=pltpu.SMEM)


def call(kernel, outs, *args, scratch=(), smem=0):
    return pl.pallas_call(
        kernel,
        out_shape=[jax.ShapeDtypeStruct(shape, dtype) for shape, dtype in outs],
        in_specs=[SMEM] * smem + [VMEM] * (len(args) - smem),
        out_specs=[VMEM] * len(outs),
        scratch_shapes=list(scratch),
        compiler_params=pltpu.CompilerParams(vmem_limit_bytes=40 * 1024 * 1024),
    )(*args)


def dot(a, b, left=1, right=0):
    return lax.dot_general(
        a, b, (((left,), (right,)), ((), ())), preferred_element_type=F32
    )


def limits(off_ref, u, plane):
    base = plane * CHUNK
    end = off_ref[0, u + 1] if u + 1 < UTTS else LENGTH
    return off_ref[0, u] - base, end - base


def present(off_ref, u, plane):
    low, high = limits(off_ref, u, plane)
    return (low < CHUNK) & (high > 0)


def row_mask(off_ref, u, plane):
    low, high = limits(off_ref, u, plane)
    rows = lax.broadcasted_iota(jnp.int32, (CHUNK, HD), 0)
    return (rows >= low) & (rows < high)


def lane_mask(off_ref, u, plane):
    low, high = limits(off_ref, u, plane)
    lanes = lax.broadcasted_iota(jnp.int32, (HD, CHUNK), 1)
    return (lanes >= low) & (lanes < high)


def scale_of(off_ref, u, plane):
    low, high = limits(off_ref, u, plane)
    span = jnp.full((1, HD), HD * (high - low), jnp.int32).astype(F32)
    return 1.0 / jnp.sqrt(span)


def utterance_at(off_ref, frame):
    count = jnp.int32(-1)
    for u in range(UTTS):
        count = count + (off_ref[0, u] <= frame).astype(jnp.int32)
    return count


def partial_sums(off_ref, plane, left_t, right, own_ref, edge_ref):
    for u in range(UTTS):

        @pl.when(present(off_ref, u, plane))
        def _(u=u):
            masked = jnp.where(lane_mask(off_ref, u, plane), left_t, 0.0).astype(BF)
            own_ref[u] = dot(masked, right)

    first = utterance_at(off_ref, plane * CHUNK)
    last = utterance_at(off_ref, plane * CHUNK + CHUNK - 1)
    edge_ref[0] = own_ref[first]
    edge_ref[1] = own_ref[last]


def edge_utterances(off_ref, plane):
    found = []
    for shift in range(1, Z):
        source = lax.rem(plane + Z - shift, Z)
        first = utterance_at(off_ref, source * CHUNK)
        last = utterance_at(off_ref, source * CHUNK + CHUNK - 1)
        found.append((first, jnp.where(last == first, -1, last)))
    return found


def whole_sum(u, own_ref, edge_refs, found):
    total = own_ref[u]
    for edge_ref, (first, last) in zip(edge_refs, found):
        total = total + edge_ref[0] * (first == u).astype(F32)
        total = total + edge_ref[1] * (last == u).astype(F32)
    return total.astype(BF)


def prepare_kernel(q_ref, k_ref, v_ref, cot_ref, heads_ref, keep_ref, give_ref):
    core = lax.axis_index("c")
    for head in range(BLOCKS):
        columns = slice(head * HD, (head + 1) * HD)
        heads_ref[head, 0] = q_ref[0, :, columns]
        heads_ref[head, 1] = k_ref[0, :, columns]
        heads_ref[head, 2] = v_ref[0, :, columns]

    def halves(zero_ref, one_ref):
        for y in range(Y):
            start = y * C * COLS
            zero_ref[:, y * COLS : (y + 1) * COLS] = cot_ref[0, :, start : start + COLS]
            one_ref[:, y * COLS : (y + 1) * COLS] = cot_ref[0, :, start + COLS : start + 2 * COLS]

    @pl.when(core == 0)
    def _():
        halves(keep_ref, give_ref)

    @pl.when(core == 1)
    def _():
        halves(give_ref, keep_ref)


def state_kernel(off_ref, heads_ref, own_ref, edge_ref):
    plane = lax.axis_index("z")
    key = heads_ref[:, 1].reshape(CHUNK, HD).astype(F32)
    value = heads_ref[:, 2].reshape(CHUNK, HD)
    partial_sums(off_ref, plane, key.T, value, own_ref, edge_ref)


def attended_kernel(off_ref, heads_ref, own_ref, e1, e2, e3, attended_ref, state_ref, total_ref):
    plane = lax.axis_index("z")
    found = edge_utterances(off_ref, plane)
    query = heads_ref[:, 0].reshape(CHUNK, HD)
    for u in range(UTTS):

        @pl.when(present(off_ref, u, plane))
        def _(u=u):
            state = whole_sum(u, own_ref, (e1, e2, e3), found)
            state_ref[u] = state
            rows = dot(query, state) * scale_of(off_ref, u, plane)
            total_ref[...] = jnp.where(row_mask(off_ref, u, plane), rows, total_ref[...])

    attended_ref[...] = total_ref[...].astype(BF).reshape(BLOCKS, FRAMES, HD)


def block_order():
    x = lax.axis_index("x")
    c = lax.axis_index("c")
    sources = (x, lax.rem(x + X - 1, X), lax.rem(x + 1, X), lax.rem(x + 2, X))
    return [source * C + core for source in sources for core in (c, 1 - c)]


def cotangent_kernel(pieces_ref, *refs):
    cots, (mine_ref, theirs_ref, weight_ref) = refs[:BLOCKS], refs[BLOCKS:]
    core = lax.axis_index("c")
    for y in range(Y):
        for h in range(H):
            for z in range(Z):
                row = (z * H + h) * ROWS
                weight_ref[row : row + ROWS, y * COLS : (y + 1) * COLS] = pieces_ref[
                    (y * H + h) * Z + z
                ]
    weight = weight_ref[...]
    for cot_ref, block in zip(cots, block_order()):
        back = dot(cot_ref[...], weight, 1, 1)
        low, high = back[:, :HD], back[:, HD:]
        mine_ref[block] = jnp.where(core == 0, low, high)
        theirs_ref[block] = jnp.where(core == 0, high, low)


def gradient_kernel(off_ref, heads_ref, mine_ref, came_ref, scaled_ref, own_ref, edge_ref, total_ref):
    plane = lax.axis_index("z")
    back = (mine_ref[...] + came_ref[...]).reshape(CHUNK, HD)
    for u in range(UTTS):

        @pl.when(present(off_ref, u, plane))
        def _(u=u):
            rows = back * scale_of(off_ref, u, plane)
            total_ref[...] = jnp.where(row_mask(off_ref, u, plane), rows, total_ref[...])

    scaled = total_ref[...].astype(BF)
    scaled_ref[...] = scaled
    query = heads_ref[:, 0].reshape(CHUNK, HD).astype(F32)
    partial_sums(off_ref, plane, query.T, scaled, own_ref, edge_ref)


def home_kernel(off_ref, heads_ref, scaled_ref, state_ref, own_ref, e1, e2, e3, out_ref, gq, gk, gv):
    plane = lax.axis_index("z")
    found = edge_utterances(off_ref, plane)
    key = heads_ref[:, 1].reshape(CHUNK, HD)
    value = heads_ref[:, 2].reshape(CHUNK, HD)
    scaled = scaled_ref[...]
    for u in range(UTTS):

        @pl.when(present(off_ref, u, plane))
        def _(u=u):
            grad = whole_sum(u, own_ref, (e1, e2, e3), found)
            mask = row_mask(off_ref, u, plane)
            gq[...] = jnp.where(mask, dot(scaled, state_ref[u], 1, 1), gq[...])
            gk[...] = jnp.where(mask, dot(value, grad, 1, 1), gk[...])
            gv[...] = jnp.where(mask, dot(key, grad), gv[...])

    for place, ref in enumerate((gq, gk, gv)):
        out_ref[:, place] = ref[...].astype(BF).reshape(BLOCKS, FRAMES, HD)


def weight_kernel(own_ref, partner_ref, *refs):
    cots, (term_ref, s0, s1, s2, s3, pair_ref) = refs[:BLOCKS], refs[BLOCKS:]
    core = lax.axis_index("c")
    x = lax.axis_index("x")
    own, partner = own_ref[...], partner_ref[...]

    @pl.when(core == 0)
    def _():
        pair_ref[:, :, :HD] = own
        pair_ref[:, :, HD:] = partner

    @pl.when(core == 1)
    def _():
        pair_ref[:, :, :HD] = partner
        pair_ref[:, :, HD:] = own

    for shift, ref in enumerate((s0, s1, s2, s3)):
        target = lax.rem(x + shift, X) * C
        for c in range(C):
            ref[c] = pair_ref[target + c]
    order = block_order()
    term = None
    for i in range(0, BLOCKS, 2):
        left = jnp.concatenate([pair_ref[order[i]], pair_ref[order[i + 1]]], axis=0)
        right = jnp.concatenate([cots[i][...], cots[i + 1][...]], axis=0)
        part = dot(left, right, 0, 0)
        term = part if term is None else term + part
    term = term.astype(BF)
    for y in range(Y):
        for h in range(H):
            for z in range(Z):
                row = (z * H + h) * ROWS
                term_ref[(y * H + h) * Z + z] = term[
                    row : row + ROWS, y * COLS : (y + 1) * COLS
                ]


def encode_kernel(a0, a1, a2, a3, w0, w1, w2, top, bottom, mine_ref, theirs_ref):
    core = lax.axis_index("c")
    total = None
    for a_ref, w in (
        (a0, w0[...]),
        (a1, w1[...]),
        (a2, w2[...]),
        (a3, jnp.concatenate([top[...], bottom[...]], axis=0)),
    ):
        part = dot(a_ref[...].reshape(C * FRAMES, 2 * HD), w)
        total = part if total is None else total + part
    total = total.astype(BF)
    zero, one = total[:FRAMES], total[FRAMES:]

    @pl.when(core == 0)
    def _():
        mine_ref[...] = zero
        theirs_ref[...] = one

    @pl.when(core == 1)
    def _():
        mine_ref[...] = one
        theirs_ref[...] = zero


def encoded_kernel(mine_ref, came_ref, out_ref):
    core = lax.axis_index("c")

    def place(zero_ref, one_ref):
        for y in range(Y):
            start = y * C * COLS
            columns = slice(y * COLS, (y + 1) * COLS)
            out_ref[0, :, start : start + COLS] = zero_ref[:, columns]
            out_ref[0, :, start + COLS : start + 2 * COLS] = one_ref[:, columns]

    @pl.when(core == 0)
    def _():
        place(mine_ref, came_ref)

    @pl.when(core == 1)
    def _():
        place(came_ref, mine_ref)


def grads_kernel(got_ref, q_ref, k_ref, v_ref):
    for head in range(BLOCKS):
        columns = slice(head * HD, (head + 1) * HD)
        for place, ref in enumerate((q_ref, k_ref, v_ref)):
            ref[0, :, columns] = got_ref[head, place]


def flat(y, h, z, x, c):
    return (((y * H + h) * Z + z) * X + x) * C + c


def swap_pairs():
    return [
        (flat(y, h, z, x, c), flat(y, c, x, z, h))
        for y in range(Y)
        for h in range(H)
        for z in range(Z)
        for x in range(X)
        for c in range(C)
    ]


def turn(value, axis, size, shift):
    return lax.ppermute(value, axis, [(i, (i + shift) % size) for i in range(size)])


def swap_cores(value):
    return turn(value, "c", C, 1)


def edges_of(edge):
    return [turn(edge, "z", Z, shift) for shift in range(1, Z)]


def body(queries, key_vectors, values, cotangent, out_weight, offsets):
    group = Y * H * Z
    state_shape = (UTTS, HD, HD)
    edge_shape = (2, HD, HD)
    chunk_scratch = pltpu.VMEM((CHUNK, HD), F32)

    moved = lax.ppermute(out_weight, ALL, swap_pairs())
    heads, keep, give = call(
        prepare_kernel,
        [((BLOCKS, 3, FRAMES, HD), BF), ((FRAMES, HALF), BF), ((FRAMES, HALF), BF)],
        queries,
        key_vectors,
        values,
        cotangent,
    )
    partner = swap_cores(give)
    back_keep, back_partner = turn(keep, "x", X, 1), turn(partner, "x", X, 1)
    next_keep, next_partner = turn(keep, "x", X, -1), turn(partner, "x", X, -1)
    far_keep, far_partner = turn(back_keep, "x", X, 1), turn(next_partner, "x", X, -1)
    cots = [keep, partner, back_keep, back_partner, next_keep, next_partner, far_keep, far_partner]

    heads = lax.all_to_all(heads, PLANE, 0, 0, tiled=True)
    pieces = lax.all_to_all(
        jnp.broadcast_to(moved[None], (group, ROWS, COLS)), ACROSS, 0, 0, tiled=True
    )

    own, edge = call(
        state_kernel, [(state_shape, F32), (edge_shape, F32)], offsets, heads, smem=1
    )
    attended, state = call(
        attended_kernel,
        [((BLOCKS, FRAMES, HD), BF), (state_shape, BF)],
        offsets,
        heads,
        own,
        *edges_of(edge),
        scratch=[chunk_scratch],
        smem=1,
    )
    term, s0, s1, s2, s3 = call(
        weight_kernel,
        [((group, ROWS, COLS), BF)] + [((C, FRAMES, 2 * HD), BF)] * X,
        attended,
        swap_cores(attended),
        *cots,
        scratch=[pltpu.VMEM((BLOCKS, FRAMES, 2 * HD), BF)],
    )
    a1, a2, a3 = turn(s1, "x", X, 1), turn(s3, "x", X, -1), turn(s2, "x", X, 2)

    mine, theirs, weight = call(
        cotangent_kernel,
        [((BLOCKS, FRAMES, HD), F32)] * 2 + [((2 * HD, HALF), BF)],
        pieces,
        *cots,
    )
    scaled, gown, gedge = call(
        gradient_kernel,
        [((CHUNK, HD), BF), (state_shape, F32), (edge_shape, F32)],
        offsets,
        heads,
        mine,
        swap_cores(theirs),
        scratch=[chunk_scratch],
        smem=1,
    )
    w1, w2 = turn(weight, "x", X, 1), turn(weight, "x", X, -1)
    top, bottom = turn(w1[:HD], "x", X, 1), turn(w2[HD:], "x", X, -1)

    term = lax.all_to_all(term, ACROSS, 0, 0, tiled=True)
    grad_weight = jnp.sum(term.astype(F32), axis=0) / math.sqrt(Y * H * LENGTH)
    grad_weight = lax.ppermute(grad_weight, ALL, swap_pairs())

    (homeward,) = call(
        home_kernel,
        [((BLOCKS, 3, FRAMES, HD), BF)],
        offsets,
        heads,
        scaled,
        state,
        gown,
        *edges_of(gedge),
        scratch=[chunk_scratch] * 3,
        smem=1,
    )
    mine, theirs = call(
        encode_kernel,
        [((FRAMES, HALF), BF)] * 2,
        s0,
        a1,
        a2,
        a3,
        weight,
        w1,
        w2,
        top,
        bottom,
    )
    (encoded,) = call(
        encoded_kernel, [((1, FRAMES, C * HALF), BF)], mine, swap_cores(theirs)
    )
    got = lax.all_to_all(homeward, PLANE, 0, 0, tiled=True)
    grads = call(grads_kernel, [((1, FRAMES, BLOCKS * HD), BF)] * 3, got)
    return (encoded, grads[0], grads[1], grads[2], grad_weight)


def solution(mesh):
    fine = Mesh(np.asarray(mesh.devices).reshape(Y, H, Z, X, C), ALL)
    dp, tm = ("y", "h"), ("z", "x", "c")
    three = P(dp, tm, None)
    in_specs = (three, three, three, three, P(tm, dp), P(dp, None))
    out_specs = (three, three, three, three, P(tm, dp))
    return jax.shard_map(body, mesh=fine, in_specs=in_specs, out_specs=out_specs, check_vma=False)
```

time: 258 us -> 152 us (0.59)
  local copies, waits for them, and re-layouts: 72.4 us -> 8.91 us
  waiting for transfers between devices: 75.6 us -> 54.2 us
  matrix products: 19 us -> 0 us
  Pallas kernels: 0 us -> 19 us
  between operations: 18.7 us -> 0.84 us
  other arithmetic: 4.15 us -> 1.13 us
    all_to_all x6 -> x2, waiting for transfers between devices: 60.5 us -> 0.01 us  [the longest x1 0.01 us: body(): got = lax.all_to_all(homeward, PLANE, 0, 0, tiled=True)]
    ppermute x2 -> x23, waiting for transfers between devices: 0.01 us -> 45.7 us  [turn(): lax.ppermute(value, axis, [(i, (i + shift) % size) for i in range(size)])]
    ppermute x2 -> x23, starting transfers between devices: 2.31 us -> 26.5 us  [turn(): lax.ppermute(value, axis, [(i, (i + shift) % size) for i in range(size)])]
    pallas_call x0 -> x10, Pallas kernels: none -> 19 us  [call(): pl.pallas_call(kernel, out_shape=[jax.ShapeDtypeStruct(shape, dtype) for...]
    dot_general x10 -> x0, matrix products: 19 us -> none  [mm(): return lax.dot_general(a, b, (dims, ((), ())), preferred_element_type=F32)]
    all_to_all x6 -> x2, starting transfers between devices: 32.8 us -> 14.8 us  [the longest x1 10.3 us: body(): lax.all_to_all(jnp.broadcast_to(moved[None], (group, ROWS, COLS)), ACROSS...]
    mul x22 -> x0, local copies, waits for them, and re-layouts: 13.4 us -> none  [the longest x11 6.02 us: totals(): own = own + take_first[z][:, None, None] * edges[z, 0]]
    slice x6 -> x2, local copies, waits for them, and re-layouts: 13 us -> 0.04 us  [body(): top, bottom = (turn(w1[:HD], 'x', X, 1), turn(w2[HD:], 'x', X, -1))]
  transfers between devices with their start and end apart: 13 -> 29, of which waited for: 10 -> 13; matrix products, arithmetic and copies ran while one was open for 22% -> 1% of each run, Pallas kernels for 0% -> 11%
where the time goes in v2:
time: 152 us
  starting transfers between devices  67.4 us (44%)
  waiting for transfers between devices  54.2 us (36%)
  Pallas kernels  19 us (12%)
  local copies, waits for them, and re-layouts  8.91 us (6%)
    ppermute x23, waiting for transfers between devices, turn(): lax.ppermute(value, axis, [(i, (i + shift) % size) for i in range(size)])  45.7 us
    ppermute x23, starting transfers between devices, turn(): lax.ppermute(value, axis, [(i, (i + shift) % size) for i in range(size)])  26.5 us
    pallas_call x10, Pallas kernels, call(): pl.pallas_call(kernel, out_shape=[jax.ShapeDtypeStruct(shape, dtype) for...  19 us
    all_to_all x1, starting transfers between devices, body(): lax.all_to_all(jnp.broadcast_to(moved[None], (group, ROWS, COLS)), ACROSS...  10.3 us
    unnamed x31, local copies, waits for them, and re-layouts  8.02 us
    ppermute x1, starting transfers between devices, body(): moved = lax.ppermute(out_weight, ALL, swap_pairs())  7.82 us
    all_to_all x1, starting transfers between devices, body(): term = lax.all_to_all(term, ACROSS, 0, 0, tiled=True)  7.25 us
    all_to_all x1, starting transfers between devices, body(): heads = lax.all_to_all(heads, PLANE, 0, 0, tiled=True)  6.81 us
  transfers between devices with their start and end apart: 29, of which 13 were waited for; matrix products, arithmetic and copies ran while one was open for 1% of the time, Pallas kernels for 11%

profile of v2, /device:TPU:1, one launch (start us, length us, event | category | flops | bytes accessed | tf_op | source)
XLA Modules:
  0.0 151.5 jit_solution(10867912844766192921)
XLA Ops:
  5.6 6.8 %all-to-all-start = ((bf16[8,3,128,128]{3,2,1,0:T(8,128)(2,1)}), bf16[8,3,128,128]{3,2,1,0:T(8,128)(2,1)S(1)}, u32[]{:S(2)}, u32[]{:S(2)}) async-start(bf16[8,3,128,128]{3,2,1,0:T(8,128)(2,1)} %get-tuple-element.28), calls=%async_computation | async-start | bytes 1572864 | tf_op jit(solution)/shard_map/all_to_all | solution.py:360
  12.4 7.8 %collective-permute-start.14 = (bf16[32,256]{1,0:T(8,128)(2,1)S(1)}, bf16[32,256]{1,0:T(8,128)(2,1)S(1)}, u32[]{:S(2)}, u32[]{:S(2)}) collective-permute-start(bf16[32,256]{1,0:T(8,128)(2,1)S(1)} %copy-done.14), channel_id=1, source_target_pairs={{0,0},{1,32},{2,8},{3,40},{4,16},{5,48},{6,24},{7,56},{8,2},{9,34}... | collective-permute-start | bytes 49160 | tf_op jit(solution)/shard_map/ppermute | solution.py:345
  20.3 1.5 collective-permute-done.14
  21.8 3.0 %all-to-all-done.heads_ref = bf16[8,3,128,128]{3,2,1,0:T(8,128)(2,1)S(1)} async-done(((bf16[8,3,128,128]{3,2,1,0:T(8,128)(2,1)}), bf16[8,3,128,128]{3,2,1,0:T(8,128)(2,1)S(1)}, u32[]{:S(2)}, u32[]{:S(2)}) %all-to-all-start) | async-done | bytes 786464 | tf_op jit(solution)/shard_map/all_to_all | solution.py:360
  25.6 10.3 %all-to-all-start.1 = ((bf16[32,32,256]{2,1,0:T(8,128)(2,1)}), bf16[32,32,256]{2,1,0:T(8,128)(2,1)S(1)}, u32[]{:S(2)}, u32[]{:S(2)}) async-start(bf16[32,32,256]{2,1,0:T(8,128)(2,1)} %broadcast_in_dim.2), calls=%async_computation.1 | async-start | bytes 1048576 | tf_op jit(solution)/shard_map/all_to_all | solution.py:361
  35.9 1.2 collective-permute-start.4
  38.3 1.5 %collective-permute-start.8 = (bf16[128,1024]{1,0:T(8,128)(2,1)S(1)}, bf16[128,1024]{1,0:T(8,128)(2,1)S(1)}, u32[]{:S(2)}, u32[]{:S(2)}) collective-permute-start(bf16[128,1024]{1,0:T(8,128)(2,1)S(1)} %collective-permute-done.4.refs_1_), channel_id=1, source_target_pairs={{0,6},{2,0},{4,2},{6,4},{1,7},{3,1},{5,3},{7,5},{8,14},{10,8},{12,... | collective-permute-start | bytes 786440 | tf_op jit(solution)/shard_map/ppermute | solution.py:328
  39.9 1.9 %shard_map.102 = (f32[12,128,128]{2,1,0:T(8,128)S(1)}, f32[2,128,128]{2,1,0:T(8,128)S(1)}) custom-call(s32[1,12]{1,0:T(1,128)S(1)} %copy-done.7, bf16[8,3,128,128]{3,2,1,0:T(8,128)(2,1)S(1)} %all-to-all-done.heads_ref), custom_call_target="tpu_custom_call" | custom-call | tf_op jit(solution)/shard_map/pallas_call | solution.py:33
  41.7 3.0 %collective-permute-start.2 = (f32[2,128,128]{2,1,0:T(8,128)S(1)}, f32[2,128,128]{2,1,0:T(8,128)S(1)}, u32[]{:S(2)}, u32[]{:S(2)}) collective-permute-start(f32[2,128,128]{2,1,0:T(8,128)S(1)} %get-tuple-element.30), channel_id=1, source_target_pairs={{0,24},{8,0},{16,8},{24,16},{1,25},{9,1},{17,9},{25,17},{2,26},{10... | collective-permute-start | bytes 393224 | tf_op jit(solution)/shard_map/ppermute | solution.py:328
  46.2 1.5 collective-permute-start.6
  47.7 3.6 %collective-permute-done.2.e3 = f32[2,128,128]{2,1,0:T(8,128)S(1)} collective-permute-done((f32[2,128,128]{2,1,0:T(8,128)S(1)}, f32[2,128,128]{2,1,0:T(8,128)S(1)}, u32[]{:S(2)}, u32[]{:S(2)}) %collective-permute-start.2) | collective-permute-done | bytes 131104 | tf_op jit(solution)/shard_map/ppermute | solution.py:328
  51.4 9.3 %collective-permute-done.1.e2 = f32[2,128,128]{2,1,0:T(8,128)S(1)} collective-permute-done((f32[2,128,128]{2,1,0:T(8,128)S(1)}, f32[2,128,128]{2,1,0:T(8,128)S(1)}, u32[]{:S(2)}, u32[]{:S(2)}) %collective-permute-start.1) | collective-permute-done | bytes 131104 | tf_op jit(solution)/shard_map/ppermute | solution.py:328
  61.9 2.4 %shard_map.103 = (bf16[8,128,128]{2,1,0:T(8,128)(2,1)S(1)}, bf16[12,128,128]{2,1,0:T(8,128)(2,1)S(1)}) custom-call(s32[1,12]{1,0:T(1,128)S(1)} %copy-done.7, bf16[8,3,128,128]{3,2,1,0:T(8,128)(2,1)S(1)} %all-to-all-done.heads_ref, f32[12,128,128]{2,1,0:T(8,128)S(1)} %get-tuple-element.29.own_ref, f32[2,128,128]{2,1,0:T(8,128)S(1)} %collective-permute-done.e1, ...), custom_call_target="tpu_custom_call" | custom-call | tf_op jit(solution)/shard_map/pallas_call | solution.py:33
  65.1 1.7 %collective-permute-start.3 = (bf16[8,128,128]{2,1,0:T(8,128)(2,1)S(1)}, bf16[8,128,128]{2,1,0:T(8,128)(2,1)S(1)}, u32[]{:S(2)}, u32[]{:S(2)}) collective-permute-start(bf16[8,128,128]{2,1,0:T(8,128)(2,1)S(1)} %get-tuple-element.31.own_ref), channel_id=1, source_target_pairs={{0,1},{1,0},{2,3},{3,2},{4,5},{5,4},{6,7},{7,6},{8,9},{9,8},{10,11... | collective-permute-start | bytes 786440 | tf_op jit(solution)/shard_map/ppermute | solution.py:328
  71.7 7.2 %all-to-all-start.3 = ((bf16[32,32,256]{2,1,0:T(8,128)(2,1)}), bf16[32,32,256]{2,1,0:T(8,128)(2,1)}, u32[]{:S(2)}, u32[]{:S(2)}) async-start(bf16[32,32,256]{2,1,0:T(8,128)(2,1)} %copy-done.1), calls=%async_computation.3 | async-start | bytes 1048576 | tf_op jit(solution)/shard_map/all_to_all | solution.py:407
  78.9 2.1 %shard_map.105 = (f32[8,128,128]{2,1,0:T(8,128)S(1)}, f32[8,128,128]{2,1,0:T(8,128)S(1)}, bf16[256,1024]{1,0:T(8,128)(2,1)}) custom-call(bf16[32,32,256]{2,1,0:T(8,128)(2,1)S(1)} %all-to-all-done.1.pieces_ref, bf16[128,1024]{1,0:T(8,128)(2,1)S(1)} %get-tuple-element.32.refs_0_, bf16[128,1024]{1,0:T(8,128)(2,1)S(1)} %collective-permute-done.4.refs_1_, ...), custom_call_target="tpu_custom_call" | custom-call | tf_op jit(solution)/shard_map/pallas_call | solution.py:33
  81.0 2.2 %collective-permute-start.20 = (f32[8,128,128]{2,1,0:T(8,128)S(1)}, f32[8,128,128]{2,1,0:T(8,128)S(1)}, u32[]{:S(2)}, u32[]{:S(2)}) collective-permute-start(f32[8,128,128]{2,1,0:T(8,128)S(1)} %get-tuple-element.42), channel_id=1, source_target_pairs={{0,1},{1,0},{2,3},{3,2},{4,5},{5,4},{6,7},{7,6},{8,9},{9,8},{10,11... | collective-permute-start | bytes 1572872 | tf_op jit(solution)/shard_map/ppermute | solution.py:328
  83.2 2.4 %collective-permute-start.16 = (bf16[256,1024]{1,0:T(8,128)(2,1)}, bf16[256,1024]{1,0:T(8,128)(2,1)S(1)}, u32[]{:S(2)}, u32[]{:S(2)}) collective-permute-start(bf16[256,1024]{1,0:T(8,128)(2,1)} %get-tuple-element.38.w0), channel_id=1, source_target_pairs={{0,6},{2,0},{4,2},{6,4},{1,7},{3,1},{5,3},{7,5},{8,14},{10,8},{12,... | collective-permute-start | bytes 1572872 | tf_op jit(solution)/shard_map/ppermute | solution.py:328
  85.6 2.7 %shard_map.108 = (bf16[1024,128]{1,0:T(8,128)(2,1)S(1)}, f32[12,128,128]{2,1,0:T(8,128)S(1)}, f32[2,128,128]{2,1,0:T(8,128)S(1)}) custom-call(s32[1,12]{1,0:T(1,128)S(1)} %copy-done.7, bf16[8,3,128,128]{3,2,1,0:T(8,128)(2,1)S(1)} %all-to-all-done.heads_ref, f32[8,128,128]{2,1,0:T(8,128)S(1)} %get-tuple-element.41.mine_ref, ...), custom_call_target="tpu_custom_call" | custom-call | tf_op jit(solution)/shard_map/pallas_call | solution.py:33
  88.3 2.6 %collective-permute-start.23 = (f32[2,128,128]{2,1,0:T(8,128)S(1)}, f32[2,128,128]{2,1,0:T(8,128)S(1)}, u32[]{:S(2)}, u32[]{:S(2)}) collective-permute-start(f32[2,128,128]{2,1,0:T(8,128)S(1)} %get-tuple-element.46), channel_id=1, source_target_pairs={{0,24},{8,0},{16,8},{24,16},{1,25},{9,1},{17,9},{25,17},{2,26},{10... | collective-permute-start | bytes 393224 | tf_op jit(solution)/shard_map/ppermute | solution.py:328
  91.5 3.3 %collective-permute-done.23.e3 = f32[2,128,128]{2,1,0:T(8,128)S(1)} collective-permute-done((f32[2,128,128]{2,1,0:T(8,128)S(1)}, f32[2,128,128]{2,1,0:T(8,128)S(1)}, u32[]{:S(2)}, u32[]{:S(2)}) %collective-permute-start.23) | collective-permute-done | bytes 131104 | tf_op jit(solution)/shard_map/ppermute | solution.py:328
  94.8 9.7 %collective-permute-done.22.e2 = f32[2,128,128]{2,1,0:T(8,128)S(1)} collective-permute-done((f32[2,128,128]{2,1,0:T(8,128)S(1)}, f32[2,128,128]{2,1,0:T(8,128)S(1)}, u32[]{:S(2)}, u32[]{:S(2)}) %collective-permute-start.22) | collective-permute-done | bytes 131104 | tf_op jit(solution)/shard_map/ppermute | solution.py:328
  104.4 4.3 %shard_map.109 = bf16[8,3,128,128]{3,2,1,0:T(8,128)(2,1)} custom-call(s32[1,12]{1,0:T(1,128)S(1)} %copy-done.7, bf16[8,3,128,128]{3,2,1,0:T(8,128)(2,1)S(1)} %all-to-all-done.heads_ref, bf16[1024,128]{1,0:T(8,128)(2,1)S(1)} %get-tuple-element.43.scaled_ref, bf16[12,128,128]{2,1,0:T(8,128)(2,1)S(1)} %copy-done.3, ...), custom_call_target="tpu_custom_call" | custom-call | tf_op jit(solution)/shard_map/pallas_call | solution.py:33
  108.7 4.5 %all-to-all-start.2 = ((bf16[8,3,128,128]{3,2,1,0:T(8,128)(2,1)}), bf16[8,3,128,128]{3,2,1,0:T(8,128)(2,1)S(1)}, u32[]{:S(2)}, u32[]{:S(2)}) async-start(bf16[8,3,128,128]{3,2,1,0:T(8,128)(2,1)} %shard_map.109), calls=%async_computation.2 | async-start | bytes 1572864 | tf_op jit(solution)/shard_map/all_to_all | solution.py:439
  113.3 2.7 %collective-permute-start.18 = (bf16[128,1024]{1,0:T(8,128)(2,1)S(1)}, bf16[128,1024]{1,0:T(8,128)(2,1)S(1)}, u32[]{:S(2)}, u32[]{:S(2)}) collective-permute-start(bf16[128,1024]{1,0:T(8,128)(2,1)S(1)} %slice.9), channel_id=1, source_target_pairs={{0,6},{2,0},{4,2},{6,4},{1,7},{3,1},{5,3},{7,5},{8,14},{10,8},{12,... | collective-permute-start | bytes 786440 | tf_op jit(solution)/shard_map/ppermute | solution.py:328
  116.3 2.5 %collective-permute-start.12 = (bf16[2,128,256]{2,1,0:T(8,128)(2,1)S(1)}, bf16[2,128,256]{2,1,0:T(8,128)(2,1)S(1)}, u32[]{:S(2)}, u32[]{:S(2)}) collective-permute-start(bf16[2,128,256]{2,1,0:T(8,128)(2,1)S(1)} %copy-done.11), channel_id=1, source_target_pairs={{0,6},{2,0},{4,2},{6,4},{1,7},{3,1},{5,3},{7,5},{8,14},{10,8},{12,... | collective-permute-start | bytes 393224 | tf_op jit(solution)/shard_map/ppermute | solution.py:328
  118.8 1.2 collective-permute-start.13
  120.0 13.8 %collective-permute-done.11.a1 = bf16[2,128,256]{2,1,0:T(8,128)(2,1)S(1)} collective-permute-done((bf16[2,128,256]{2,1,0:T(8,128)(2,1)S(1)}, bf16[2,128,256]{2,1,0:T(8,128)(2,1)S(1)}, u32[]{:S(2)}, u32[]{:S(2)}) %collective-permute-start.11) | collective-permute-done | bytes 131104 | tf_op jit(solution)/shard_map/ppermute | solution.py:328
  133.8 3.0 %collective-permute-done.13.a3 = bf16[2,128,256]{2,1,0:T(8,128)(2,1)S(1)} collective-permute-done((bf16[2,128,256]{2,1,0:T(8,128)(2,1)S(1)}, bf16[2,128,256]{2,1,0:T(8,128)(2,1)S(1)}, u32[]{:S(2)}, u32[]{:S(2)}) %collective-permute-start.13) | collective-permute-done | bytes 131104 | tf_op jit(solution)/shard_map/ppermute | solution.py:328
  136.8 1.8 %shard_map.106 = (bf16[128,1024]{1,0:T(8,128)(2,1)S(1)}, bf16[128,1024]{1,0:T(8,128)(2,1)S(1)}) custom-call(bf16[2,128,256]{2,1,0:T(8,128)(2,1)S(1)} %get-tuple-element.34.a0, bf16[2,128,256]{2,1,0:T(8,128)(2,1)S(1)} %collective-permute-done.11.a1, bf16[2,128,256]{2,1,0:T(8,128)(2,1)S(1)} %collective-permute-done.12.a2, ...), custom_call_target="tpu_custom_call" | custom-call | tf_op jit(solution)/shard_map/pallas_call | solution.py:33
  140.7 4.3 %collective-permute-start.24 = (f32[32,256]{1,0:T(8,128)S(1)}, f32[32,256]{1,0:T(8,128)S(1)}, u32[]{:S(2)}, u32[]{:S(2)}) collective-permute-start(f32[32,256]{1,0:T(8,128)S(1)} %broadcast_multiply_fusion), channel_id=1, source_target_pairs={{0,0},{1,32},{2,8},{3,40},{4,16},{5,48},{6,24},{7,56},{8,2},{9,34}... | collective-permute-start | bytes 98312 | tf_op jit(solution)/shard_map/ppermute | solution.py:409
  145.8 4.0 %collective-permute-done.24 = f32[32,256]{1,0:T(8,128)S(1)} collective-permute-done((f32[32,256]{1,0:T(8,128)S(1)}, f32[32,256]{1,0:T(8,128)S(1)}, u32[]{:S(2)}, u32[]{:S(2)}) %collective-permute-start.24) | collective-permute-done | bytes 32800 | tf_op jit(solution)/shard_map/ppermute | solution.py:409
  (72 shorter events, 21.0 us)
Async XLA Ops:
  5.6 6.8 %copy-start.14 = (bf16[32,256]{1,0:T(8,128)(2,1)S(1)}, bf16[32,256]{1,0:T(8,128)(2,1)}, u32[]{:S(2)}) copy-start(bf16[32,256]{1,0:T(8,128)(2,1)} %param.10) | copy-start | bytes 49156
  5.6 19.1 %all-to-all-start = ((bf16[8,3,128,128]{3,2,1,0:T(8,128)(2,1)}), bf16[8,3,128,128]{3,2,1,0:T(8,128)(2,1)S(1)}, u32[]{:S(2)}, u32[]{:S(2)}) async-start(bf16[8,3,128,128]{3,2,1,0:T(8,128)(2,1)} %get-tuple-element.28), calls=%async_computation | async-start | bytes 1572864 | tf_op jit(solution)/shard_map/all_to_all | solution.py:360
  12.4 9.3 %collective-permute-start.14 = (bf16[32,256]{1,0:T(8,128)(2,1)S(1)}, bf16[32,256]{1,0:T(8,128)(2,1)S(1)}, u32[]{:S(2)}, u32[]{:S(2)}) collective-permute-start(bf16[32,256]{1,0:T(8,128)(2,1)S(1)} %copy-done.14), channel_id=1, source_target_pairs={{0,0},{1,32},{2,8},{3,40},{4,16},{5,48},{6,24},{7,56},{8,2},{9,34}... | collective-permute-start | bytes 49160 | tf_op jit(solution)/shard_map/ppermute | solution.py:345
  25.6 46.1 %all-to-all-start.1 = ((bf16[32,32,256]{2,1,0:T(8,128)(2,1)}), bf16[32,32,256]{2,1,0:T(8,128)(2,1)S(1)}, u32[]{:S(2)}, u32[]{:S(2)}) async-start(bf16[32,32,256]{2,1,0:T(8,128)(2,1)} %broadcast_in_dim.2), calls=%async_computation.1 | async-start | bytes 1048576 | tf_op jit(solution)/shard_map/all_to_all | solution.py:361
  35.9 2.4 %collective-permute-start.4 = (bf16[128,1024]{1,0:T(8,128)(2,1)S(1)}, bf16[128,1024]{1,0:T(8,128)(2,1)S(1)}, u32[]{:S(2)}, u32[]{:S(2)}) collective-permute-start(bf16[128,1024]{1,0:T(8,128)(2,1)S(1)} %get-tuple-element.33), channel_id=1, source_target_pairs={{0,1},{1,0},{2,3},{3,2},{4,5},{5,4},{6,7},{7,6},{8,9},{9,8},{10,11... | collective-permute-start | bytes 786440 | tf_op jit(solution)/shard_map/ppermute | solution.py:328
  37.2 9.1 %collective-permute-start.5 = (bf16[128,1024]{1,0:T(8,128)(2,1)S(1)}, bf16[128,1024]{1,0:T(8,128)(2,1)S(1)}, u32[]{:S(2)}, u32[]{:S(2)}) collective-permute-start(bf16[128,1024]{1,0:T(8,128)(2,1)S(1)} %get-tuple-element.32.refs_0_), channel_id=1, source_target_pairs={{0,2},{2,4},{4,6},{6,0},{1,3},{3,5},{5,7},{7,1},{8,10},{10,12},{12... | collective-permute-start | bytes 786440 | tf_op jit(solution)/shard_map/ppermute | solution.py:328
  38.3 7.9 %collective-permute-start.8 = (bf16[128,1024]{1,0:T(8,128)(2,1)S(1)}, bf16[128,1024]{1,0:T(8,128)(2,1)S(1)}, u32[]{:S(2)}, u32[]{:S(2)}) collective-permute-start(bf16[128,1024]{1,0:T(8,128)(2,1)S(1)} %collective-permute-done.4.refs_1_), channel_id=1, source_target_pairs={{0,6},{2,0},{4,2},{6,4},{1,7},{3,1},{5,3},{7,5},{8,14},{10,8},{12,... | collective-permute-start | bytes 786440 | tf_op jit(solution)/shard_map/ppermute | solution.py:328
  41.7 9.6 %collective-permute-start.2 = (f32[2,128,128]{2,1,0:T(8,128)S(1)}, f32[2,128,128]{2,1,0:T(8,128)S(1)}, u32[]{:S(2)}, u32[]{:S(2)}) collective-permute-start(f32[2,128,128]{2,1,0:T(8,128)S(1)} %get-tuple-element.30), channel_id=1, source_target_pairs={{0,24},{8,0},{16,8},{24,16},{1,25},{9,1},{17,9},{25,17},{2,26},{10... | collective-permute-start | bytes 393224 | tf_op jit(solution)/shard_map/ppermute | solution.py:328
  44.7 16.1 %collective-permute-start.1 = (f32[2,128,128]{2,1,0:T(8,128)S(1)}, f32[2,128,128]{2,1,0:T(8,128)S(1)}, u32[]{:S(2)}, u32[]{:S(2)}) collective-permute-start(f32[2,128,128]{2,1,0:T(8,128)S(1)} %get-tuple-element.30), channel_id=1, source_target_pairs={{0,16},{8,24},{16,0},{24,8},{1,17},{9,25},{17,1},{25,9},{2,18},{10... | collective-permute-start | bytes 393224 | tf_op jit(solution)/shard_map/ppermute | solution.py:328
  44.7 17.2 %collective-permute-start = (f32[2,128,128]{2,1,0:T(8,128)S(1)}, f32[2,128,128]{2,1,0:T(8,128)S(1)}, u32[]{:S(2)}, u32[]{:S(2)}) collective-permute-start(f32[2,128,128]{2,1,0:T(8,128)S(1)} %get-tuple-element.30), channel_id=1, source_target_pairs={{0,8},{8,16},{16,24},{24,0},{1,9},{9,17},{17,25},{25,1},{2,10},{10... | collective-permute-start | bytes 393224 | tf_op jit(solution)/shard_map/ppermute | solution.py:328
  46.2 20.6 %collective-permute-start.7 = (bf16[128,1024]{1,0:T(8,128)(2,1)S(1)}, bf16[128,1024]{1,0:T(8,128)(2,1)S(1)}, u32[]{:S(2)}, u32[]{:S(2)}) collective-permute-start(bf16[128,1024]{1,0:T(8,128)(2,1)S(1)} %get-tuple-element.32.refs_0_), channel_id=1, source_target_pairs={{0,6},{2,0},{4,2},{6,4},{1,7},{3,1},{5,3},{7,5},{8,14},{10,8},{12,... | collective-permute-start | bytes 786440 | tf_op jit(solution)/shard_map/ppermute | solution.py:328
  46.2 20.6 %collective-permute-start.6 = (bf16[128,1024]{1,0:T(8,128)(2,1)S(1)}, bf16[128,1024]{1,0:T(8,128)(2,1)S(1)}, u32[]{:S(2)}, u32[]{:S(2)}) collective-permute-start(bf16[128,1024]{1,0:T(8,128)(2,1)S(1)} %collective-permute-done.4.refs_1_), channel_id=1, source_target_pairs={{0,2},{2,4},{4,6},{6,0},{1,3},{3,5},{5,7},{7,1},{8,10},{10,12},{12... | collective-permute-start | bytes 786440 | tf_op jit(solution)/shard_map/ppermute | solution.py:328
  51.3 15.6 %collective-permute-start.9 = (bf16[128,1024]{1,0:T(8,128)(2,1)S(1)}, bf16[128,1024]{1,0:T(8,128)(2,1)S(1)}, u32[]{:S(2)}, u32[]{:S(2)}) collective-permute-start(bf16[128,1024]{1,0:T(8,128)(2,1)S(1)} %collective-permute-done.5.refs_2_), channel_id=1, source_target_pairs={{0,2},{2,4},{4,6},{6,0},{1,3},{3,5},{5,7},{7,1},{8,10},{10,12},{12... | collective-permute-start | bytes 786440 | tf_op jit(solution)/shard_map/ppermute | solution.py:328
  60.8 6.3 %collective-permute-start.10 = (bf16[128,1024]{1,0:T(8,128)(2,1)S(1)}, bf16[128,1024]{1,0:T(8,128)(2,1)S(1)}, u32[]{:S(2)}, u32[]{:S(2)}) collective-permute-start(bf16[128,1024]{1,0:T(8,128)(2,1)S(1)} %collective-permute-done.8.refs_5_), channel_id=1, source_target_pairs={{0,6},{2,0},{4,2},{6,4},{1,7},{3,1},{5,3},{7,5},{8,14},{10,8},{12,... | collective-permute-start | bytes 786440 | tf_op jit(solution)/shard_map/ppermute | solution.py:328
  65.1 2.9 %collective-permute-start.3 = (bf16[8,128,128]{2,1,0:T(8,128)(2,1)S(1)}, bf16[8,128,128]{2,1,0:T(8,128)(2,1)S(1)}, u32[]{:S(2)}, u32[]{:S(2)}) collective-permute-start(bf16[8,128,128]{2,1,0:T(8,128)(2,1)S(1)} %get-tuple-element.31.own_ref), channel_id=1, source_target_pairs={{0,1},{1,0},{2,3},{3,2},{4,5},{5,4},{6,7},{7,6},{8,9},{9,8},{10,11... | collective-permute-start | bytes 786440 | tf_op jit(solution)/shard_map/ppermute | solution.py:328
  71.7 37.0 %all-to-all-start.3 = ((bf16[32,32,256]{2,1,0:T(8,128)(2,1)}), bf16[32,32,256]{2,1,0:T(8,128)(2,1)}, u32[]{:S(2)}, u32[]{:S(2)}) async-start(bf16[32,32,256]{2,1,0:T(8,128)(2,1)} %copy-done.1), calls=%async_computation.3 | async-start | bytes 1048576 | tf_op jit(solution)/shard_map/all_to_all | solution.py:407
  81.0 4.6 %collective-permute-start.20 = (f32[8,128,128]{2,1,0:T(8,128)S(1)}, f32[8,128,128]{2,1,0:T(8,128)S(1)}, u32[]{:S(2)}, u32[]{:S(2)}) collective-permute-start(f32[8,128,128]{2,1,0:T(8,128)S(1)} %get-tuple-element.42), channel_id=1, source_target_pairs={{0,1},{1,0},{2,3},{3,2},{4,5},{5,4},{6,7},{7,6},{8,9},{9,8},{10,11... | collective-permute-start | bytes 1572872 | tf_op jit(solution)/shard_map/ppermute | solution.py:328
  83.2 30.0 %collective-permute-start.16 = (bf16[256,1024]{1,0:T(8,128)(2,1)}, bf16[256,1024]{1,0:T(8,128)(2,1)S(1)}, u32[]{:S(2)}, u32[]{:S(2)}) collective-permute-start(bf16[256,1024]{1,0:T(8,128)(2,1)} %get-tuple-element.38.w0), channel_id=1, source_target_pairs={{0,6},{2,0},{4,2},{6,4},{1,7},{3,1},{5,3},{7,5},{8,14},{10,8},{12,... | collective-permute-start | bytes 1572872 | tf_op jit(solution)/shard_map/ppermute | solution.py:328
  85.6 30.4 %collective-permute-start.15 = (bf16[256,1024]{1,0:T(8,128)(2,1)}, bf16[256,1024]{1,0:T(8,128)(2,1)S(1)}, u32[]{:S(2)}, u32[]{:S(2)}) collective-permute-start(bf16[256,1024]{1,0:T(8,128)(2,1)} %get-tuple-element.38.w0), channel_id=1, source_target_pairs={{0,2},{2,4},{4,6},{6,0},{1,3},{3,5},{5,7},{7,1},{8,10},{10,12},{12... | collective-permute-start | bytes 1572872 | tf_op jit(solution)/shard_map/ppermute | solution.py:328
  85.6 18.8 %copy-start.3 = (bf16[12,128,128]{2,1,0:T(8,128)(2,1)S(1)}, bf16[12,128,128]{2,1,0:T(8,128)(2,1)}, u32[]{:S(2)}) copy-start(bf16[12,128,128]{2,1,0:T(8,128)(2,1)} %copy-done.2) | copy-start | bytes 1179652
  88.3 6.5 %collective-permute-start.23 = (f32[2,128,128]{2,1,0:T(8,128)S(1)}, f32[2,128,128]{2,1,0:T(8,128)S(1)}, u32[]{:S(2)}, u32[]{:S(2)}) collective-permute-start(f32[2,128,128]{2,1,0:T(8,128)S(1)} %get-tuple-element.46), channel_id=1, source_target_pairs={{0,24},{8,0},{16,8},{24,16},{1,25},{9,1},{17,9},{25,17},{2,26},{10... | collective-permute-start | bytes 393224 | tf_op jit(solution)/shard_map/ppermute | solution.py:328
  90.9 13.5 %collective-permute-start.22 = (f32[2,128,128]{2,1,0:T(8,128)S(1)}, f32[2,128,128]{2,1,0:T(8,128)S(1)}, u32[]{:S(2)}, u32[]{:S(2)}) collective-permute-start(f32[2,128,128]{2,1,0:T(8,128)S(1)} %get-tuple-element.46), channel_id=1, source_target_pairs={{0,16},{8,24},{16,0},{24,8},{1,17},{9,25},{17,1},{25,9},{2,18},{10... | collective-permute-start | bytes 393224 | tf_op jit(solution)/shard_map/ppermute | solution.py:328
  90.9 13.5 %collective-permute-start.21 = (f32[2,128,128]{2,1,0:T(8,128)S(1)}, f32[2,128,128]{2,1,0:T(8,128)S(1)}, u32[]{:S(2)}, u32[]{:S(2)}) collective-permute-start(f32[2,128,128]{2,1,0:T(8,128)S(1)} %get-tuple-element.46), channel_id=1, source_target_pairs={{0,8},{8,16},{16,24},{24,0},{1,9},{9,17},{17,25},{25,1},{2,10},{10... | collective-permute-start | bytes 393224 | tf_op jit(solution)/shard_map/ppermute | solution.py:328
  108.7 41.1 %all-to-all-start.2 = ((bf16[8,3,128,128]{3,2,1,0:T(8,128)(2,1)}), bf16[8,3,128,128]{3,2,1,0:T(8,128)(2,1)S(1)}, u32[]{:S(2)}, u32[]{:S(2)}) async-start(bf16[8,3,128,128]{3,2,1,0:T(8,128)(2,1)} %shard_map.109), calls=%async_computation.2 | async-start | bytes 1572864 | tf_op jit(solution)/shard_map/all_to_all | solution.py:439
  113.3 5.6 %copy-start.9 = (bf16[2,128,256]{2,1,0:T(8,128)(2,1)S(1)}, bf16[2,128,256]{2,1,0:T(8,128)(2,1)}, u32[]{:S(2)}) copy-start(bf16[2,128,256]{2,1,0:T(8,128)(2,1)} %copy-done.8) | copy-start | bytes 393220
  113.3 23.5 %collective-permute-start.18 = (bf16[128,1024]{1,0:T(8,128)(2,1)S(1)}, bf16[128,1024]{1,0:T(8,128)(2,1)S(1)}, u32[]{:S(2)}, u32[]{:S(2)}) collective-permute-start(bf16[128,1024]{1,0:T(8,128)(2,1)S(1)} %slice.9), channel_id=1, source_target_pairs={{0,6},{2,0},{4,2},{6,4},{1,7},{3,1},{5,3},{7,5},{8,14},{10,8},{12,... | collective-permute-start | bytes 786440 | tf_op jit(solution)/shard_map/ppermute | solution.py:328
  116.0 20.8 %collective-permute-start.17 = (bf16[128,1024]{1,0:T(8,128)(2,1)S(1)}, bf16[128,1024]{1,0:T(8,128)(2,1)S(1)}, u32[]{:S(2)}, u32[]{:S(2)}) collective-permute-start(bf16[128,1024]{1,0:T(8,128)(2,1)S(1)} %slice.8), channel_id=1, source_target_pairs={{0,2},{2,4},{4,6},{6,0},{1,3},{3,5},{5,7},{7,1},{8,10},{10,12},{12... | collective-permute-start | bytes 786440 | tf_op jit(solution)/shard_map/ppermute | solution.py:328
  116.1 17.7 %collective-permute-start.11 = (bf16[2,128,256]{2,1,0:T(8,128)(2,1)S(1)}, bf16[2,128,256]{2,1,0:T(8,128)(2,1)S(1)}, u32[]{:S(2)}, u32[]{:S(2)}) collective-permute-start(bf16[2,128,256]{2,1,0:T(8,128)(2,1)S(1)} %copy-done.13), channel_id=1, source_target_pairs={{0,2},{2,4},{4,6},{6,0},{1,3},{3,5},{5,7},{7,1},{8,10},{10,12},{12... | collective-permute-start | bytes 393224 | tf_op jit(solution)/shard_map/ppermute | solution.py:328
  116.3 17.5 %collective-permute-start.12 = (bf16[2,128,256]{2,1,0:T(8,128)(2,1)S(1)}, bf16[2,128,256]{2,1,0:T(8,128)(2,1)S(1)}, u32[]{:S(2)}, u32[]{:S(2)}) collective-permute-start(bf16[2,128,256]{2,1,0:T(8,128)(2,1)S(1)} %copy-done.11), channel_id=1, source_target_pairs={{0,6},{2,0},{4,2},{6,4},{1,7},{3,1},{5,3},{7,5},{8,14},{10,8},{12,... | collective-permute-start | bytes 393224 | tf_op jit(solution)/shard_map/ppermute | solution.py:328
  118.8 17.9 %collective-permute-start.13 = (bf16[2,128,256]{2,1,0:T(8,128)(2,1)S(1)}, bf16[2,128,256]{2,1,0:T(8,128)(2,1)S(1)}, u32[]{:S(2)}, u32[]{:S(2)}) collective-permute-start(bf16[2,128,256]{2,1,0:T(8,128)(2,1)S(1)} %copy-done.9), channel_id=1, source_target_pairs={{0,4},{2,6},{4,0},{6,2},{1,5},{3,7},{5,1},{7,3},{8,12},{10,14},{12... | collective-permute-start | bytes 393224 | tf_op jit(solution)/shard_map/ppermute | solution.py:328
  138.6 6.4 %collective-permute-start.19 = (bf16[128,1024]{1,0:T(8,128)(2,1)S(1)}, bf16[128,1024]{1,0:T(8,128)(2,1)S(1)}, u32[]{:S(2)}, u32[]{:S(2)}) collective-permute-start(bf16[128,1024]{1,0:T(8,128)(2,1)S(1)} %get-tuple-element.40), channel_id=1, source_target_pairs={{0,1},{1,0},{2,3},{3,2},{4,5},{5,4},{6,7},{7,6},{8,9},{9,8},{10,11... | collective-permute-start | bytes 786440 | tf_op jit(solution)/shard_map/ppermute | solution.py:328
  140.7 9.1 %collective-permute-start.24 = (f32[32,256]{1,0:T(8,128)S(1)}, f32[32,256]{1,0:T(8,128)S(1)}, u32[]{:S(2)}, u32[]{:S(2)}) collective-permute-start(f32[32,256]{1,0:T(8,128)S(1)} %broadcast_multiply_fusion), channel_id=1, source_target_pairs={{0,0},{1,32},{2,8},{3,40},{4,16},{5,48},{6,24},{7,56},{8,2},{9,34}... | collective-permute-start | bytes 98312 | tf_op jit(solution)/shard_map/ppermute | solution.py:409
  (12 other events, 17.2 us)

commit v3 on v2

v3 whole, which is shorter than its diff:
```python
import math

import jax
import jax.numpy as jnp
import numpy as np
from jax import lax
from jax.experimental import pallas as pl
from jax.experimental.pallas import tpu as pltpu
from jax.sharding import Mesh
from jax.sharding import PartitionSpec as P

HD = 128
FRAMES = 128
Y, H, Z, X, C = 4, 2, 4, 4, 2
BLOCKS = X * C
CHUNK = BLOCKS * FRAMES
LENGTH = Z * CHUNK
UTTS = 12
ROWS = 32
COLS = 256
HALF = Y * COLS
TILES = HALF // HD
PASSED = TILES + 3
ALL = ("y", "h", "z", "x", "c")
ACROSS = ("y", "h", "z")
BF = jnp.bfloat16
F32 = jnp.float32

VMEM = pl.BlockSpec(memory_space=pltpu.VMEM)
SMEM = pl.BlockSpec(memory_space=pltpu.SMEM)


def call(kernel, outs, *args, scratch=(), smem=0, where=pltpu.VMEM, after=(), mib=40):
    count = len(args)

    def run(*refs):
        kernel(*refs[:count], *refs[count + len(after) :])

    specs = [SMEM] * smem + [pl.BlockSpec(memory_space=where)] * (count - smem)
    return pl.pallas_call(
        run,
        out_shape=[jax.ShapeDtypeStruct(shape, dtype) for shape, dtype in outs],
        in_specs=specs + [pl.BlockSpec(memory_space=pl.ANY)] * len(after),
        out_specs=[VMEM] * len(outs),
        scratch_shapes=list(scratch),
        compiler_params=pltpu.CompilerParams(vmem_limit_bytes=mib * 1024 * 1024),
    )(*args, *after)


def dot(a, b, left=1, right=0):
    return lax.dot_general(
        a, b, (((left,), (right,)), ((), ())), preferred_element_type=F32
    )


def limits(off_ref, u, plane):
    base = plane * CHUNK
    end = off_ref[0, u + 1] if u + 1 < UTTS else LENGTH
    return off_ref[0, u] - base, end - base


def present(off_ref, u, plane):
    low, high = limits(off_ref, u, plane)
    return (low < CHUNK) & (high > 0)


def row_mask(off_ref, u, plane):
    low, high = limits(off_ref, u, plane)
    rows = lax.broadcasted_iota(jnp.int32, (CHUNK, HD), 0)
    return (rows >= low) & (rows < high)


def lane_mask(off_ref, u, plane):
    low, high = limits(off_ref, u, plane)
    lanes = lax.broadcasted_iota(jnp.int32, (HD, CHUNK), 1)
    return (lanes >= low) & (lanes < high)


def scale_of(off_ref, u, plane):
    low, high = limits(off_ref, u, plane)
    span = jnp.full((1, HD), HD * (high - low), jnp.int32).astype(F32)
    return 1.0 / jnp.sqrt(span)


def utterance_at(off_ref, frame):
    count = jnp.int32(-1)
    for u in range(UTTS):
        count = count + (off_ref[0, u] <= frame).astype(jnp.int32)
    return count


def partial_sums(off_ref, plane, left_t, right, own_ref):
    for u in range(UTTS):

        @pl.when(present(off_ref, u, plane))
        def _(u=u):
            masked = jnp.where(lane_mask(off_ref, u, plane), left_t, 0.0).astype(BF)
            own_ref[u] = dot(masked, right)

    first = utterance_at(off_ref, plane * CHUNK)
    last = utterance_at(off_ref, plane * CHUNK + CHUNK - 1)
    return [
        own_ref[jnp.where(plane + shift < Z, last, first)].astype(BF) for shift in range(1, Z)
    ]


def edge_utterances(off_ref, plane):
    found = []
    for shift in range(1, Z):
        source = lax.rem(plane + Z - shift, Z)
        frame = source * CHUNK + jnp.where(source < plane, CHUNK - 1, 0)
        found.append(utterance_at(off_ref, frame))
    return found


def whole_sum(u, own_ref, edge_refs, which, found):
    total = own_ref[u]
    for edge_ref, utterance in zip(edge_refs, found):
        total = total + edge_ref[which].astype(F32) * (utterance == u).astype(F32)
    return total.astype(BF)


def prepare_kernel(q_ref, k_ref, v_ref, cot_ref, keep_ref, give_ref, sems):
    core = lax.axis_index("c")
    copies = []
    for side, (ref, whose) in enumerate(((give_ref, 1 - core), (keep_ref, core))):
        for pair in range(X):
            start = pl.multiple_of((pair * C + whose) * HD, HD)
            for place, source in enumerate((q_ref, k_ref, v_ref)):
                copies.append((source.at[0, :, pl.ds(start, HD)], ref.at[pair * 3 + place], side))
        for tile in range(TILES):
            start = (tile // 2) * C * COLS + whose * COLS + (tile % 2) * HD
            start = pl.multiple_of(start, HD)
            copies.append((cot_ref.at[0, :, pl.ds(start, HD)], ref.at[X * 3 + tile], side))
    copies = [
        pltpu.make_async_copy(source, target, sems.at[i])
        for i, (source, target, _) in enumerate(copies)
    ]
    for copy in copies:
        copy.start()
    for copy in copies:
        copy.wait()


def merge_kernel(keep_ref, came_ref, self_ref, next_ref, back_ref):
    core = lax.axis_index("c")
    x = lax.axis_index("x")
    far = lax.rem(x + 2, X) * 3
    for mine, block in ((keep_ref, core), (came_ref, 1 - core)):
        for first, out, shift in ((0, next_ref, 1), (1, back_ref, 3)):
            near = lax.rem(x + shift, X) * 3
            cot = jnp.where(block == first, 0, PASSED)
            out[pl.ds(cot, TILES)] = mine[X * 3 :]
            out[pl.ds(PASSED + TILES + block * 3, 3)] = mine[pl.ds(near, 3)]

            @pl.when(block == first)
            def _(mine=mine, out=out):
                out[TILES:PASSED] = mine[pl.ds(far, 3)]

        self_ref[pl.ds(block * TILES, TILES)] = mine[X * 3 :]
        self_ref[pl.ds(C * TILES + block * 3, 3)] = mine[pl.ds(x * 3, 3)]


def sources():
    x = lax.axis_index("x")
    return (x, lax.rem(x + X - 1, X), lax.rem(x + 1, X), lax.rem(x + 2, X))


def state_kernel(off_ref, s0, s1, s2, far0, far1, heads_ref, own_ref, edge_ref):
    plane = lax.axis_index("z")
    parts = [[ref[start : start + 3] for start in starts] for ref, starts in (
        (s0, (C * TILES, C * TILES + 3)),
        (s1, (PASSED + TILES, PASSED + TILES + 3)),
        (s2, (PASSED + TILES, PASSED + TILES + 3)),
    )]
    parts.append([far0[TILES:], far1[TILES:]])
    for pair, source in zip(parts, sources()):
        for core, part in enumerate(pair):
            heads_ref[source * C + core] = part
    key = heads_ref[:, 1].reshape(CHUNK, HD).astype(F32)
    value = heads_ref[:, 2].reshape(CHUNK, HD)
    edges = partial_sums(off_ref, plane, key.T, value, own_ref)
    for place, edge in enumerate(edges):
        edge_ref[place] = edge


def attended_kernel(off_ref, heads_ref, own_ref, e1, e2, e3, attended_ref, state_ref, total_ref):
    plane = lax.axis_index("z")
    found = edge_utterances(off_ref, plane)
    query = heads_ref[:, 0].reshape(CHUNK, HD)
    for u in range(UTTS):

        @pl.when(present(off_ref, u, plane))
        def _(u=u):
            state = whole_sum(u, own_ref, (e1, e2, e3), 0, found)
            state_ref[u] = state
            rows = dot(query, state) * scale_of(off_ref, u, plane)
            total_ref[...] = jnp.where(row_mask(off_ref, u, plane), rows, total_ref[...])

    attended_ref[...] = total_ref[...].astype(BF).reshape(BLOCKS, FRAMES, HD)


def wide(tiles):
    return jnp.concatenate([tiles[i] for i in range(TILES)], axis=1)


def chip_cotangents(s0, s1, s2, far0, far1):
    parts = (
        (s0[:TILES], s0[TILES : 2 * TILES]),
        (s1[:TILES], s1[PASSED : PASSED + TILES]),
        (s2[PASSED : PASSED + TILES], s2[:TILES]),
        (far0[:TILES], far1[:TILES]),
    )
    for pair, source in zip(parts, sources()):
        yield source, jnp.concatenate([wide(part) for part in pair], axis=0)


def block_kernel(pieces_ref, weight_ref):
    for y in range(Y):
        for h in range(H):
            for z in range(Z):
                row = (z * H + h) * ROWS
                weight_ref[row : row + ROWS, y * COLS : (y + 1) * COLS] = pieces_ref[
                    (y * H + h) * Z + z
                ]


def cotangent_kernel(weight_ref, s0, s1, s2, far0, far1, mine_ref, theirs_ref):
    core = lax.axis_index("c")
    weight = weight_ref[...]
    for source, rows in chip_cotangents(s0, s1, s2, far0, far1):
        back = dot(rows, weight, 1, 1)
        low, high = back[:, :HD], back[:, HD:]
        mine = jnp.where(core == 0, low, high)
        theirs = jnp.where(core == 0, high, low)
        for c in range(C):
            mine_ref[source * C + c] = mine[c * FRAMES : (c + 1) * FRAMES]
            theirs_ref[source * C + c] = theirs[c * FRAMES : (c + 1) * FRAMES]


def gradient_kernel(
    off_ref, heads_ref, mine_ref, came_ref, edge_ref, scaled_ref, own_ref, o1, o2, o3, total_ref
):
    plane = lax.axis_index("z")
    back = (mine_ref[...] + came_ref[...]).reshape(CHUNK, HD)
    for u in range(UTTS):

        @pl.when(present(off_ref, u, plane))
        def _(u=u):
            rows = back * scale_of(off_ref, u, plane)
            total_ref[...] = jnp.where(row_mask(off_ref, u, plane), rows, total_ref[...])

    scaled = total_ref[...].astype(BF)
    scaled_ref[...] = scaled
    query = heads_ref[:, 0].reshape(CHUNK, HD).astype(F32)
    edges = partial_sums(off_ref, plane, query.T, scaled, own_ref)
    for place, (edge, out) in enumerate(zip(edges, (o1, o2, o3))):
        out[0] = edge_ref[place]
        out[1] = edge


def weight_kernel(own_ref, partner_ref, s0, s1, s2, far0, far1, term_ref, pair_ref):
    core = lax.axis_index("c")
    own, partner = own_ref[...], partner_ref[...]
    pair_ref[:, 0] = jnp.where(core == 0, own, partner)
    pair_ref[:, 1] = jnp.where(core == 0, partner, own)
    term = None
    for source, right in chip_cotangents(s0, s1, s2, far0, far1):
        left = jnp.concatenate(
            [
                jnp.concatenate([pair_ref[source * C + c, head] for head in range(C)], axis=1)
                for c in range(C)
            ],
            axis=0,
        )
        part = dot(left, right, 0, 0)
        term = part if term is None else term + part
    term = term.astype(BF)
    for y in range(Y):
        for h in range(H):
            for z in range(Z):
                row = (z * H + h) * ROWS
                term_ref[(y * H + h) * Z + z] = term[
                    row : row + ROWS, y * COLS : (y + 1) * COLS
                ]


def home_kernel(
    off_ref, heads_ref, scaled_ref, state_ref, att_ref, partner_ref, own_ref, e1, e2, e3, *refs
):
    outs, (gq, gk, gv) = refs[:X], refs[X:]
    plane = lax.axis_index("z")
    x = lax.axis_index("x")
    core = lax.axis_index("c")
    found = edge_utterances(off_ref, plane)
    key = heads_ref[:, 1].reshape(CHUNK, HD)
    value = heads_ref[:, 2].reshape(CHUNK, HD)
    scaled = scaled_ref[...]
    for u in range(UTTS):

        @pl.when(present(off_ref, u, plane))
        def _(u=u):
            grad = whole_sum(u, own_ref, (e1, e2, e3), 1, found)
            mask = row_mask(off_ref, u, plane)
            gq[...] = jnp.where(mask, dot(scaled, state_ref[u], 1, 1), gq[...])
            gk[...] = jnp.where(mask, dot(value, grad, 1, 1), gk[...])
            gv[...] = jnp.where(mask, dot(key, grad), gv[...])

    for shift, out in enumerate(outs):
        for c in range(C):
            block = lax.rem(x + shift, X) * C + c
            rows = pl.ds(pl.multiple_of(block * FRAMES, FRAMES), FRAMES)
            for place, ref in enumerate((gq, gk, gv)):
                out[c, place] = ref[rows, :].astype(BF)
            out[c, 3 + core] = att_ref[block]
            out[c, 4 - core] = partner_ref[block]


def encode_kernel(r0, r1, r2, r3, w0, w1, w2, top, bottom, keep_ref, give_ref):
    core = lax.axis_index("c")
    total = None
    weights = (w0[...], w1[...], w2[...], jnp.concatenate([top[...], bottom[...]], axis=0))
    for ref, weight, source in zip((r0, r1, r2, r3), weights, sources()):
        for place in range(3):
            keep_ref[source * 3 + place] = ref[core, place]
            give_ref[source * 3 + place] = ref[1 - core, place]
        left = jnp.concatenate(
            [jnp.concatenate([ref[c, 3], ref[c, 4]], axis=1) for c in range(C)], axis=0
        )
        part = dot(left, weight)
        total = part if total is None else total + part
    total = total.astype(BF)
    zero, one = total[:FRAMES], total[FRAMES:]
    mine = jnp.where(core == 0, zero, one)
    theirs = jnp.where(core == 0, one, zero)
    for tile in range(TILES):
        columns = slice(tile * HD, (tile + 1) * HD)
        keep_ref[X * 3 + tile] = mine[:, columns]
        give_ref[X * 3 + tile] = theirs[:, columns]


def finish_kernel(keep_ref, came_ref, enc_ref, q_ref, k_ref, v_ref):
    core = lax.axis_index("c")

    def place_all(parts):
        for c, part in enumerate(parts):
            for pair in range(X):
                start = (pair * C + c) * HD
                for place, ref in enumerate((q_ref, k_ref, v_ref)):
                    ref[0, :, start : start + HD] = part[pair * 3 + place]
            for tile in range(TILES):
                start = (tile // 2) * C * COLS + c * COLS + (tile % 2) * HD
                enc_ref[0, :, start : start + HD] = part[X * 3 + tile]

    @pl.when(core == 0)
    def _():
        place_all((keep_ref, came_ref))

    @pl.when(core == 1)
    def _():
        place_all((came_ref, keep_ref))


def flat(y, h, z, x, c):
    return (((y * H + h) * Z + z) * X + x) * C + c


def swap_pairs():
    return [
        (flat(y, h, z, x, c), flat(y, c, x, z, h))
        for y in range(Y)
        for h in range(H)
        for z in range(Z)
        for x in range(X)
        for c in range(C)
    ]


def turn(value, axis, size, shift):
    return lax.ppermute(value, axis, [(i, (i + shift) % size) for i in range(size)])


def swap_cores(value):
    return turn(value, "c", C, 1)


def body(queries, key_vectors, values, cotangent, out_weight, offsets):
    group = Y * H * Z
    state_shape = (UTTS, HD, HD)
    edge_shape = (2, HD, HD)
    side = (X * 3 + TILES, FRAMES, HD)
    chunk_scratch = pltpu.VMEM((CHUNK, HD), F32)

    moved = lax.ppermute(out_weight, ALL, swap_pairs())
    pieces = lax.all_to_all(
        jnp.broadcast_to(moved[None], (group, ROWS, COLS)), ACROSS, 0, 0, tiled=True
    )
    keep, give = call(
        prepare_kernel,
        [(side, BF)] * 2,
        queries,
        key_vectors,
        values,
        cotangent,
        scratch=[pltpu.SemaphoreType.DMA((2 * side[0],))],
        where=pl.ANY,
        mib=60,
    )
    s0, to_next, to_back = call(
        merge_kernel,
        [((C * PASSED, FRAMES, HD), BF)] + [((C * PASSED + 3, FRAMES, HD), BF)] * 2,
        keep,
        swap_cores(give),
        after=[moved],
    )
    s1, s2 = turn(to_next, "x", X, 1), turn(to_back, "x", X, -1)
    rows = (s0, s1, s2, turn(s1[:PASSED], "x", X, 1), turn(s2[:PASSED], "x", X, -1))

    (weight,) = call(block_kernel, [((2 * HD, HALF), BF)], pieces)
    w1, w2 = turn(weight, "x", X, 1), turn(weight, "x", X, -1)
    top, bottom = turn(w1[:HD], "x", X, 1), turn(w2[HD:], "x", X, -1)
    mine, theirs = call(
        cotangent_kernel, [((BLOCKS, FRAMES, HD), F32)] * 2, weight, *rows
    )
    heads, own, edge = call(
        state_kernel,
        [((BLOCKS, 3, FRAMES, HD), BF), (state_shape, F32), ((Z - 1, HD, HD), BF)],
        offsets,
        *rows,
        smem=1,
        after=[theirs],
    )
    scaled, gown, *edges = call(
        gradient_kernel,
        [((CHUNK, HD), BF), (state_shape, F32)] + [(edge_shape, BF)] * (Z - 1),
        offsets,
        heads,
        mine,
        swap_cores(theirs),
        edge,
        scratch=[chunk_scratch],
        smem=1,
    )
    edges = [turn(part, "z", Z, shift) for shift, part in enumerate(edges, 1)]
    attended, state = call(
        attended_kernel,
        [((BLOCKS, FRAMES, HD), BF), (state_shape, BF)],
        offsets,
        heads,
        own,
        *edges,
        scratch=[chunk_scratch],
        smem=1,
        after=[w1, w2],
    )
    partner = swap_cores(attended)
    r0, h1, h2, h3 = call(
        home_kernel,
        [((C, 5, FRAMES, HD), BF)] * X,
        offsets,
        heads,
        scaled,
        state,
        attended,
        partner,
        gown,
        *edges,
        scratch=[chunk_scratch] * 3,
        smem=1,
    )
    (term,) = call(
        weight_kernel,
        [((group, ROWS, COLS), BF)],
        attended,
        partner,
        *rows,
        scratch=[pltpu.VMEM((BLOCKS, C, FRAMES, HD), BF)],
        after=[r0, top, bottom],
    )
    term = lax.all_to_all(term, ACROSS, 0, 0, tiled=True)
    grad_weight = jnp.sum(term.astype(F32), axis=0) / math.sqrt(Y * H * LENGTH)
    grad_weight = lax.ppermute(grad_weight, ALL, swap_pairs())

    keep, give = call(
        encode_kernel,
        [(side, BF)] * 2,
        r0,
        turn(h1, "x", X, 1),
        turn(h3, "x", X, -1),
        turn(h2, "x", X, 2),
        weight,
        w1,
        w2,
        top,
        bottom,
    )
    encoded, *grads = call(
        finish_kernel,
        [((1, FRAMES, C * HALF), BF)] + [((1, FRAMES, BLOCKS * HD), BF)] * 3,
        keep,
        swap_cores(give),
    )
    return (encoded, grads[0], grads[1], grads[2], grad_weight)


def solution(mesh):
    fine = Mesh(np.asarray(mesh.devices).reshape(Y, H, Z, X, C), ALL)
    dp, tm = ("y", "h"), ("z", "x", "c")
    three = P(dp, tm, None)
    in_specs = (three, three, three, three, P(tm, dp), P(dp, None))
    out_specs = (three, three, three, three, P(tm, dp))
    return jax.shard_map(body, mesh=fine, in_specs=in_specs, out_specs=out_specs, check_vma=False)
```

time: 152 us -> 134 us (0.88); the launches traced: 152 us -> 131 us
  waiting for transfers between devices: 54.2 us -> 38.7 us
  starting transfers between devices: 67.4 us -> 57.5 us
  local copies, waits for them, and re-layouts: 8.91 us -> 13.5 us
    all_to_all x2 -> x0, starting transfers between devices: 11.3 us -> none  [the longest x1 6.81 us: body(): heads = lax.all_to_all(heads, PLANE, 0, 0, tiled=True)]
    ppermute x23 -> x18, waiting for transfers between devices: 45.7 us -> 34.6 us  [turn(): lax.ppermute(value, axis, [(i, (i + shift) % size) for i in range(size)])]
    ppermute x1, waiting for transfers between devices: 4.01 us -> 0.85 us  [body(): grad_weight = lax.ppermute(grad_weight, ALL, swap_pairs())]
    unnamed x31 -> x43, local copies, waits for them, and re-layouts: 8.02 us -> 11.1 us
    all_to_all x2 -> x0, waiting for transfers between devices: 2.97 us -> none  [the longest x1 2.97 us: body(): heads = lax.all_to_all(heads, PLANE, 0, 0, tiled=True)]
    ppermute x1, starting transfers between devices: 4.27 us -> 6.88 us  [body(): grad_weight = lax.ppermute(grad_weight, ALL, swap_pairs())]
    all_to_all x1, starting transfers between devices: 10.3 us -> 8.7 us  [body(): lax.all_to_all(jnp.broadcast_to(moved[None], (group, ROWS, COLS)), ACROSS...]
    slice x0 -> x2, local copies, waits for them, and re-layouts: none -> 1.55 us  [the longest x1 0.8 us: body(): s2[:PASSED]]
  transfers between devices with their start and end apart: 29 -> 22, of which waited for: 13 -> 10; matrix products, arithmetic and copies ran while one was open for 1% -> 3% of each run, Pallas kernels for 11% -> 7%
where the time goes in v3:
time: 134 us; the launch traced here: 131 us
  starting transfers between devices  57.5 us (43%)
  waiting for transfers between devices  38.7 us (29%)
  Pallas kernels  19.4 us (14%)
  local copies, waits for them, and re-layouts  13.5 us (10%)
    ppermute x18, waiting for transfers between devices, turn(): lax.ppermute(value, axis, [(i, (i + shift) % size) for i in range(size)])  34.6 us
    ppermute x18, starting transfers between devices, turn(): lax.ppermute(value, axis, [(i, (i + shift) % size) for i in range(size)])  27.5 us
    pallas_call x11, Pallas kernels, call(): pl.pallas_call(run, out_shape=[jax.ShapeDtypeStruct(shape, dtype) for sha...  19.4 us
    unnamed x43, local copies, waits for them, and re-layouts  11.1 us
    all_to_all x1, starting transfers between devices, body(): lax.all_to_all(jnp.broadcast_to(moved[None], (group, ROWS, COLS)), ACROSS...  8.7 us
    all_to_all x1, starting transfers between devices, body(): term = lax.all_to_all(term, ACROSS, 0, 0, tiled=True)  7.46 us
    ppermute x1, starting transfers between devices, body(): moved = lax.ppermute(out_weight, ALL, swap_pairs())  6.99 us
    ppermute x1, starting transfers between devices, body(): grad_weight = lax.ppermute(grad_weight, ALL, swap_pairs())  6.88 us
  transfers between devices with their start and end apart: 22, of which 10 were waited for; matrix products, arithmetic and copies ran while one was open for 3% of the time, Pallas kernels for 7%

profile of v3, /device:TPU:1, one launch (start us, length us, event | category | flops | bytes accessed | tf_op | source)
XLA Modules:
  0.0 131.2 jit_solution(252392413347403996)
XLA Ops:
  0.6 2.7 %shard_map.101 = (bf16[20,128,128]{2,1,0:T(8,128)(2,1)}, bf16[20,128,128]{2,1,0:T(8,128)(2,1)}) custom-call(bf16[1,128,1024]{2,1,0:T(8,128)(2,1)} %refs_0_.5, bf16[1,128,1024]{2,1,0:T(8,128)(2,1)} %refs_1_.1, bf16[1,128,1024]{2,1,0:T(8,128)(2,1)} %refs_2_.1, bf16[1,128,2048]{2,1,0:T(8,128)(2,1)} %refs_3_.1), custom_call_target="tpu_custom_call" | custom-call | tf_op jit(solution)/shard_map/pallas_call | solution.py:40
  3.4 3.3 %collective-permute-start = (bf16[20,128,128]{2,1,0:T(8,128)(2,1)}, bf16[20,128,128]{2,1,0:T(8,128)(2,1)S(1)}, u32[]{:S(2)}, u32[]{:S(2)}) collective-permute-start(bf16[20,128,128]{2,1,0:T(8,128)(2,1)} %get-tuple-element.33), channel_id=1, source_target_pairs={{0,1},{1,0},{2,3},{3,2},{4,5},{5,4},{6,7},{7,6},{8,9},{9,8},{10,11... | collective-permute-start | bytes 1966088 | tf_op jit(solution)/shard_map/ppermute | solution.py:380
  6.7 7.0 %collective-permute-start.1 = (bf16[32,256]{1,0:T(8,128)(2,1)S(1)}, bf16[32,256]{1,0:T(8,128)(2,1)S(1)}, u32[]{:S(2)}, u32[]{:S(2)}) collective-permute-start(bf16[32,256]{1,0:T(8,128)(2,1)S(1)} %copy-done.20), channel_id=1, source_target_pairs={{0,0},{1,32},{2,8},{3,40},{4,16},{5,48},{6,24},{7,56},{8,2},{9,34}... | collective-permute-start | bytes 49160 | tf_op jit(solution)/shard_map/ppermute | solution.py:394
  13.7 2.0 %collective-permute-done.1.refs_2_ = bf16[32,256]{1,0:T(8,128)(2,1)S(1)} collective-permute-done((bf16[32,256]{1,0:T(8,128)(2,1)S(1)}, bf16[32,256]{1,0:T(8,128)(2,1)S(1)}, u32[]{:S(2)}, u32[]{:S(2)}) %collective-permute-start.1) | collective-permute-done | bytes 16416 | tf_op jit(solution)/shard_map/ppermute | solution.py:394
  16.8 1.3 %shard_map.102 = (bf16[22,128,128]{2,1,0:T(8,128)(2,1)S(1)}, bf16[25,128,128]{2,1,0:T(8,128)(2,1)}, bf16[25,128,128]{2,1,0:T(8,128)(2,1)}) custom-call(bf16[20,128,128]{2,1,0:T(8,128)(2,1)S(1)} %copy-done.14, bf16[20,128,128]{2,1,0:T(8,128)(2,1)S(1)} %collective-permute-done.refs_1_, bf16[32,256]{1,0:T(8,128)(2,1)S(1)} %collective-permute-done.1.refs_2_), custom_call_target="tpu_custom_call" | custom-call | tf_op jit(solution)/shard_map/pallas_call | solution.py:40
  18.4 2.4 %collective-permute-start.3 = (bf16[25,128,128]{2,1,0:T(8,128)(2,1)}, bf16[25,128,128]{2,1,0:T(8,128)(2,1)S(1)}, u32[]{:S(2)}, u32[]{:S(2)}) collective-permute-start(bf16[25,128,128]{2,1,0:T(8,128)(2,1)} %get-tuple-element.36), channel_id=1, source_target_pairs={{0,6},{2,0},{4,2},{6,4},{1,7},{3,1},{5,3},{7,5},{8,14},{10,8},{12,... | collective-permute-start | bytes 2457608 | tf_op jit(solution)/shard_map/ppermute | solution.py:380
  21.6 8.7 %all-to-all-start = ((bf16[32,32,256]{2,1,0:T(8,128)(2,1)}), bf16[32,32,256]{2,1,0:T(8,128)(2,1)S(1)}, u32[]{:S(2)}, u32[]{:S(2)}) async-start(bf16[32,32,256]{2,1,0:T(8,128)(2,1)} %broadcast_in_dim.2), calls=%async_computation | async-start | bytes 1048576 | tf_op jit(solution)/shard_map/all_to_all | solution.py:395
  30.3 8.0 %collective-permute-done.2.refs_2_.refs_3_ = bf16[25,128,128]{2,1,0:T(8,128)(2,1)S(1)} collective-permute-done((bf16[25,128,128]{2,1,0:T(8,128)(2,1)}, bf16[25,128,128]{2,1,0:T(8,128)(2,1)S(1)}, u32[]{:S(2)}, u32[]{:S(2)}) %collective-permute-start.2) | collective-permute-done | bytes 819232 | tf_op jit(solution)/shard_map/ppermute | solution.py:380
  39.9 2.7 %collective-permute-start.5 = (bf16[11,128,128]{2,1,0:T(8,128)(2,1)}, bf16[11,128,128]{2,1,0:T(8,128)(2,1)}, u32[]{:S(2)}, u32[]{:S(2)}) collective-permute-start(bf16[11,128,128]{2,1,0:T(8,128)(2,1)} %slice.17), channel_id=1, source_target_pairs={{0,6},{2,0},{4,2},{6,4},{1,7},{3,1},{5,3},{7,5},{8,14},{10,8},{12,... | collective-permute-start | bytes 1081352 | tf_op jit(solution)/shard_map/ppermute | solution.py:380
  42.6 1.3 %all-to-all-done.refs_0_ = bf16[32,32,256]{2,1,0:T(8,128)(2,1)S(1)} async-done(((bf16[32,32,256]{2,1,0:T(8,128)(2,1)}), bf16[32,32,256]{2,1,0:T(8,128)(2,1)S(1)}, u32[]{:S(2)}, u32[]{:S(2)}) %all-to-all-start) | async-done | bytes 524320 | tf_op jit(solution)/shard_map/all_to_all | solution.py:395
  45.8 5.1 %collective-permute-done.4.refs_4_.refs_5_ = bf16[11,128,128]{2,1,0:T(8,128)(2,1)S(1)} collective-permute-done((bf16[11,128,128]{2,1,0:T(8,128)(2,1)}, bf16[11,128,128]{2,1,0:T(8,128)(2,1)S(1)}, u32[]{:S(2)}, u32[]{:S(2)}) %collective-permute-start.4) | collective-permute-done | bytes 360480 | tf_op jit(solution)/shard_map/ppermute | solution.py:380
  51.0 1.9 %shard_map.104 = (f32[8,128,128]{2,1,0:T(8,128)S(1)}, f32[8,128,128]{2,1,0:T(8,128)S(1)}) custom-call(bf16[256,1024]{1,0:T(8,128)(2,1)S(1)} %shard_map.103.refs_0_.refs_4_, bf16[22,128,128]{2,1,0:T(8,128)(2,1)S(1)} %get-tuple-element.34.refs_1_.refs_2_, bf16[25,128,128]{2,1,0:T(8,128)(2,1)S(1)} %collective-permute-done.2.refs_2_.refs_3_, ...), custom_call_target="tpu_custom_call" | custom-call | tf_op jit(solution)/shard_map/pallas_call | solution.py:40
  54.3 2.5 %collective-permute-start.11 = (bf16[256,1024]{1,0:T(8,128)(2,1)S(1)}, bf16[256,1024]{1,0:T(8,128)(2,1)S(1)}, u32[]{:S(2)}, u32[]{:S(2)}) collective-permute-start(bf16[256,1024]{1,0:T(8,128)(2,1)S(1)} %shard_map.103.refs_0_.refs_4_), channel_id=1, source_target_pairs={{0,6},{2,0},{4,2},{6,4},{1,7},{3,1},{5,3},{7,5},{8,14},{10,8},{12,... | collective-permute-start | bytes 1572872 | tf_op jit(solution)/shard_map/ppermute | solution.py:380
  57.8 2.2 %shard_map.105 = (bf16[8,3,128,128]{3,2,1,0:T(8,128)(2,1)S(1)}, f32[12,128,128]{2,1,0:T(8,128)S(1)}, bf16[3,128,128]{2,1,0:T(8,128)(2,1)S(1)}) custom-call(s32[1,12]{1,0:T(1,128)S(1)} %copy-done.15, bf16[22,128,128]{2,1,0:T(8,128)(2,1)S(1)} %get-tuple-element.34.refs_1_.refs_2_, bf16[25,128,128]{2,1,0:T(8,128)(2,1)S(1)} %collective-permute-done.2.refs_2_.refs_3_, ...), custom_call_target="tpu_custom_call" | custom-call | tf_op jit(solution)/shard_map/pallas_call | solution.py:40
  60.0 2.5 %shard_map.106 = (bf16[1024,128]{1,0:T(8,128)(2,1)S(1)}, f32[12,128,128]{2,1,0:T(8,128)S(1)}, bf16[2,128,128]{2,1,0:T(8,128)(2,1)S(1)}, bf16[2,128,128]{2,1,0:T(8,128)(2,1)S(1)}, bf16[2,128,128]{2,1,0:T(8,128)(2,1)S(1)}) custom-call(s32[1,12]{1,0:T(1,128)S(1)} %copy-done.15, bf16[8,3,128,128]{3,2,1,0:T(8,128)(2,1)S(1)} %get-tuple-element.38.refs_1_, ...), custom_call_target="tpu_custom_call" | custom-call | tf_op jit(solution)/shard_map/pallas_call | solution.py:40
  62.5 1.4 %collective-permute-start.7 = (bf16[2,128,128]{2,1,0:T(8,128)(2,1)S(1)}, bf16[2,128,128]{2,1,0:T(8,128)(2,1)S(1)}, u32[]{:S(2)}, u32[]{:S(2)}) collective-permute-start(bf16[2,128,128]{2,1,0:T(8,128)(2,1)S(1)} %get-tuple-element.43), channel_id=1, source_target_pairs={{0,8},{8,16},{16,24},{24,0},{1,9},{9,17},{17,25},{25,1},{2,10},{10... | collective-permute-start | bytes 196616 | tf_op jit(solution)/shard_map/ppermute | solution.py:380
  63.9 3.5 %collective-permute-start.8 = (bf16[2,128,128]{2,1,0:T(8,128)(2,1)S(1)}, bf16[2,128,128]{2,1,0:T(8,128)(2,1)S(1)}, u32[]{:S(2)}, u32[]{:S(2)}) collective-permute-start(bf16[2,128,128]{2,1,0:T(8,128)(2,1)S(1)} %get-tuple-element.44), channel_id=1, source_target_pairs={{0,16},{8,24},{16,0},{24,8},{1,17},{9,25},{17,1},{25,9},{2,18},{10... | collective-permute-start | bytes 196616 | tf_op jit(solution)/shard_map/ppermute | solution.py:380
  67.4 1.6 %collective-permute-done.10.refs_6_.refs_5_ = bf16[256,1024]{1,0:T(8,128)(2,1)S(1)} collective-permute-done((bf16[256,1024]{1,0:T(8,128)(2,1)S(1)}, bf16[256,1024]{1,0:T(8,128)(2,1)S(1)}, u32[]{:S(2)}, u32[]{:S(2)}) %collective-permute-start.10) | collective-permute-done | bytes 524320 | tf_op jit(solution)/shard_map/ppermute | solution.py:380
  69.0 3.4 %collective-permute-done.8.refs_4_.refs_8_ = bf16[2,128,128]{2,1,0:T(8,128)(2,1)S(1)} collective-permute-done((bf16[2,128,128]{2,1,0:T(8,128)(2,1)S(1)}, bf16[2,128,128]{2,1,0:T(8,128)(2,1)S(1)}, u32[]{:S(2)}, u32[]{:S(2)}) %collective-permute-start.8) | collective-permute-done | bytes 65568 | tf_op jit(solution)/shard_map/ppermute | solution.py:380
  72.4 1.9 %shard_map.107 = (bf16[8,128,128]{2,1,0:T(8,128)(2,1)S(1)}, bf16[12,128,128]{2,1,0:T(8,128)(2,1)S(1)}) custom-call(s32[1,12]{1,0:T(1,128)S(1)} %copy-done.15, bf16[8,3,128,128]{3,2,1,0:T(8,128)(2,1)S(1)} %get-tuple-element.38.refs_1_, f32[12,128,128]{2,1,0:T(8,128)S(1)} %get-tuple-element.42.refs_2_, ...), custom_call_target="tpu_custom_call" | custom-call | tf_op jit(solution)/shard_map/pallas_call | solution.py:40
  74.3 1.2 collective-permute-start.12
  75.6 2.7 %collective-permute-start.17 = (bf16[128,1024]{1,0:T(8,128)(2,1)S(1)}, bf16[128,1024]{1,0:T(8,128)(2,1)S(1)}, u32[]{:S(2)}, u32[]{:S(2)}) collective-permute-start(bf16[128,1024]{1,0:T(8,128)(2,1)S(1)} %slice.19), channel_id=1, source_target_pairs={{0,6},{2,0},{4,2},{6,4},{1,7},{3,1},{5,3},{7,5},{8,14},{10,8},{12,... | collective-permute-start | bytes 786440 | tf_op jit(solution)/shard_map/ppermute | solution.py:380
  78.4 2.9 %shard_map.108 = (bf16[2,5,128,128]{3,2,1,0:T(8,128)(2,1)S(1)}, bf16[2,5,128,128]{3,2,1,0:T(8,128)(2,1)S(1)}, bf16[2,5,128,128]{3,2,1,0:T(8,128)(2,1)S(1)}, bf16[2,5,128,128]{3,2,1,0:T(8,128)(2,1)S(1)}) custom-call(s32[1,12]{1,0:T(1,128)S(1)} %copy-done.15, bf16[8,3,128,128]{3,2,1,0:T(8,128)(2,1)S(1)} %get-tuple-element.38.refs_1_, ...), custom_call_target="tpu_custom_call" | custom-call | tf_op jit(solution)/shard_map/pallas_call | solution.py:40
  82.1 2.7 %collective-permute-done.16.refs_7_.refs_8_ = bf16[128,1024]{1,0:T(8,128)(2,1)S(1)} collective-permute-done((bf16[128,1024]{1,0:T(8,128)(2,1)S(1)}, bf16[128,1024]{1,0:T(8,128)(2,1)S(1)}, u32[]{:S(2)}, u32[]{:S(2)}) %collective-permute-start.16) | collective-permute-done | bytes 262176 | tf_op jit(solution)/shard_map/ppermute | solution.py:380
  84.7 1.8 %shard_map.111 = bf16[32,32,256]{2,1,0:T(8,128)(2,1)S(1)} custom-call(bf16[8,128,128]{2,1,0:T(8,128)(2,1)S(1)} %get-tuple-element.47.refs_4_.refs_0_, bf16[8,128,128]{2,1,0:T(8,128)(2,1)S(1)} %collective-permute-done.12.refs_5_.refs_1_, bf16[22,128,128]{2,1,0:T(8,128)(2,1)S(1)} %get-tuple-element.34.refs_1_.refs_2_, ...), custom_call_target="tpu_custom_call" | custom-call | tf_op jit(solution)/shard_map/pallas_call | solution.py:40
  89.5 7.5 %all-to-all-start.1 = ((bf16[32,32,256]{2,1,0:T(8,128)(2,1)}), bf16[32,32,256]{2,1,0:T(8,128)(2,1)}, u32[]{:S(2)}, u32[]{:S(2)}) async-start(bf16[32,32,256]{2,1,0:T(8,128)(2,1)} %copy-done.5), calls=%async_computation.1 | async-start | bytes 1048576 | tf_op jit(solution)/shard_map/all_to_all | solution.py:480
  97.1 2.7 %collective-permute-start.14 = (bf16[2,5,128,128]{3,2,1,0:T(8,128)(2,1)}, bf16[2,5,128,128]{3,2,1,0:T(8,128)(2,1)S(1)}, u32[]{:S(2)}, u32[]{:S(2)}) collective-permute-start(bf16[2,5,128,128]{3,2,1,0:T(8,128)(2,1)} %copy-done.18), channel_id=1, source_target_pairs={{0,6},{2,0},{4,2},{6,4},{1,7},{3,1},{5,3},{7,5},{8,14},{10,8},{12,... | collective-permute-start | bytes 983048 | tf_op jit(solution)/shard_map/ppermute | solution.py:380
  100.7 6.0 %collective-permute-done.13.refs_1_ = bf16[2,5,128,128]{3,2,1,0:T(8,128)(2,1)S(1)} collective-permute-done((bf16[2,5,128,128]{3,2,1,0:T(8,128)(2,1)}, bf16[2,5,128,128]{3,2,1,0:T(8,128)(2,1)S(1)}, u32[]{:S(2)}, u32[]{:S(2)}) %collective-permute-start.13) | collective-permute-done | bytes 327712 | tf_op jit(solution)/shard_map/ppermute | solution.py:380
  106.7 7.6 %collective-permute-done.15.refs_3_ = bf16[2,5,128,128]{3,2,1,0:T(8,128)(2,1)S(1)} collective-permute-done((bf16[2,5,128,128]{3,2,1,0:T(8,128)(2,1)S(1)}, bf16[2,5,128,128]{3,2,1,0:T(8,128)(2,1)S(1)}, u32[]{:S(2)}, u32[]{:S(2)}) %collective-permute-start.15) | collective-permute-done | bytes 327712 | tf_op jit(solution)/shard_map/ppermute | solution.py:380
  118.0 2.3 %collective-permute-start.18 = (bf16[20,128,128]{2,1,0:T(8,128)(2,1)S(1)}, bf16[20,128,128]{2,1,0:T(8,128)(2,1)S(1)}, u32[]{:S(2)}, u32[]{:S(2)}) collective-permute-start(bf16[20,128,128]{2,1,0:T(8,128)(2,1)S(1)} %get-tuple-element.54), channel_id=1, source_target_pairs={{0,1},{1,0},{2,3},{3,2},{4,5},{5,4},{6,7},{7,6},{8,9},{9,8},{10,11... | collective-permute-start | bytes 1966088 | tf_op jit(solution)/shard_map/ppermute | solution.py:380
  121.4 6.9 %collective-permute-start.19 = (f32[32,256]{1,0:T(8,128)S(1)}, f32[32,256]{1,0:T(8,128)S(1)}, u32[]{:S(2)}, u32[]{:S(2)}) collective-permute-start(f32[32,256]{1,0:T(8,128)S(1)} %broadcast_multiply_fusion), channel_id=1, source_target_pairs={{0,0},{1,32},{2,8},{3,40},{4,16},{5,48},{6,24},{7,56},{8,2},{9,34}... | collective-permute-start | bytes 98312 | tf_op jit(solution)/shard_map/ppermute | solution.py:482
  128.3 1.4 %shard_map.110 = (bf16[1,128,2048]{2,1,0:T(8,128)(2,1)}, bf16[1,128,1024]{2,1,0:T(8,128)(2,1)}, bf16[1,128,1024]{2,1,0:T(8,128)(2,1)}, bf16[1,128,1024]{2,1,0:T(8,128)(2,1)}) custom-call(bf16[20,128,128]{2,1,0:T(8,128)(2,1)S(1)} %get-tuple-element.53.refs_0_, bf16[20,128,128]{2,1,0:T(8,128)(2,1)S(1)} %collective-permute-done.18.refs_1_), custom_call_target="tpu_custom_call" | custom-call | tf_op jit(solution)/shard_map/pallas_call | solution.py:40
  (73 shorter events, 19.1 us)
Async XLA Ops:
  0.6 6.1 %copy-start.20 = (bf16[32,256]{1,0:T(8,128)(2,1)S(1)}, bf16[32,256]{1,0:T(8,128)(2,1)}, u32[]{:S(2)}) copy-start(bf16[32,256]{1,0:T(8,128)(2,1)} %param.10) | copy-start | bytes 49156
  3.4 12.3 %collective-permute-start = (bf16[20,128,128]{2,1,0:T(8,128)(2,1)}, bf16[20,128,128]{2,1,0:T(8,128)(2,1)S(1)}, u32[]{:S(2)}, u32[]{:S(2)}) collective-permute-start(bf16[20,128,128]{2,1,0:T(8,128)(2,1)} %get-tuple-element.33), channel_id=1, source_target_pairs={{0,1},{1,0},{2,3},{3,2},{4,5},{5,4},{6,7},{7,6},{8,9},{9,8},{10,11... | collective-permute-start | bytes 1966088 | tf_op jit(solution)/shard_map/ppermute | solution.py:380
  6.7 9.0 %collective-permute-start.1 = (bf16[32,256]{1,0:T(8,128)(2,1)S(1)}, bf16[32,256]{1,0:T(8,128)(2,1)S(1)}, u32[]{:S(2)}, u32[]{:S(2)}) collective-permute-start(bf16[32,256]{1,0:T(8,128)(2,1)S(1)} %copy-done.20), channel_id=1, source_target_pairs={{0,0},{1,32},{2,8},{3,40},{4,16},{5,48},{6,24},{7,56},{8,2},{9,34}... | collective-permute-start | bytes 49160 | tf_op jit(solution)/shard_map/ppermute | solution.py:394
  15.7 1.1 copy-start.14
  18.1 20.3 %collective-permute-start.2 = (bf16[25,128,128]{2,1,0:T(8,128)(2,1)}, bf16[25,128,128]{2,1,0:T(8,128)(2,1)S(1)}, u32[]{:S(2)}, u32[]{:S(2)}) collective-permute-start(bf16[25,128,128]{2,1,0:T(8,128)(2,1)} %get-tuple-element.35), channel_id=1, source_target_pairs={{0,2},{2,4},{4,6},{6,0},{1,3},{3,5},{5,7},{7,1},{8,10},{10,12},{12... | collective-permute-start | bytes 2457608 | tf_op jit(solution)/shard_map/ppermute | solution.py:380
  18.4 20.7 %collective-permute-start.3 = (bf16[25,128,128]{2,1,0:T(8,128)(2,1)}, bf16[25,128,128]{2,1,0:T(8,128)(2,1)S(1)}, u32[]{:S(2)}, u32[]{:S(2)}) collective-permute-start(bf16[25,128,128]{2,1,0:T(8,128)(2,1)} %get-tuple-element.36), channel_id=1, source_target_pairs={{0,6},{2,0},{4,2},{6,4},{1,7},{3,1},{5,3},{7,5},{8,14},{10,8},{12,... | collective-permute-start | bytes 2457608 | tf_op jit(solution)/shard_map/ppermute | solution.py:380
  21.6 22.3 %all-to-all-start = ((bf16[32,32,256]{2,1,0:T(8,128)(2,1)}), bf16[32,32,256]{2,1,0:T(8,128)(2,1)S(1)}, u32[]{:S(2)}, u32[]{:S(2)}) async-start(bf16[32,32,256]{2,1,0:T(8,128)(2,1)} %broadcast_in_dim.2), calls=%async_computation | async-start | bytes 1048576 | tf_op jit(solution)/shard_map/all_to_all | solution.py:395
  39.1 11.8 %collective-permute-start.4 = (bf16[11,128,128]{2,1,0:T(8,128)(2,1)}, bf16[11,128,128]{2,1,0:T(8,128)(2,1)S(1)}, u32[]{:S(2)}, u32[]{:S(2)}) collective-permute-start(bf16[11,128,128]{2,1,0:T(8,128)(2,1)} %slice.16), channel_id=1, source_target_pairs={{0,2},{2,4},{4,6},{6,0},{1,3},{3,5},{5,7},{7,1},{8,10},{10,12},{12... | collective-permute-start | bytes 1081352 | tf_op jit(solution)/shard_map/ppermute | solution.py:380
  39.9 11.0 %collective-permute-start.5 = (bf16[11,128,128]{2,1,0:T(8,128)(2,1)}, bf16[11,128,128]{2,1,0:T(8,128)(2,1)}, u32[]{:S(2)}, u32[]{:S(2)}) collective-permute-start(bf16[11,128,128]{2,1,0:T(8,128)(2,1)} %slice.17), channel_id=1, source_target_pairs={{0,6},{2,0},{4,2},{6,4},{1,7},{3,1},{5,3},{7,5},{8,14},{10,8},{12,... | collective-permute-start | bytes 1081352 | tf_op jit(solution)/shard_map/ppermute | solution.py:380
  51.0 1.9 %copy-start.2 = (bf16[11,128,128]{2,1,0:T(8,128)(2,1)}, bf16[11,128,128]{2,1,0:T(8,128)(2,1)S(1)}, u32[]{:S(2)}) copy-start(bf16[11,128,128]{2,1,0:T(8,128)(2,1)S(1)} %collective-permute-done.4.refs_4_.refs_5_) | copy-start | bytes 1081348
  52.8 4.0 %copy-start.15 = (s32[1,12]{1,0:T(1,128)S(1)}, s32[1,12]{1,0:T(1,128)}, u32[]{:S(2)}) copy-start(s32[1,12]{1,0:T(1,128)} %refs_0_.9) | copy-start | bytes 148
  52.9 7.1 %collective-permute-start.6 = (f32[8,128,128]{2,1,0:T(8,128)S(1)}, f32[8,128,128]{2,1,0:T(8,128)S(1)}, u32[]{:S(2)}, u32[]{:S(2)}) collective-permute-start(f32[8,128,128]{2,1,0:T(8,128)S(1)} %get-tuple-element.37.refs_6_), channel_id=1, source_target_pairs={{0,1},{1,0},{2,3},{3,2},{4,5},{5,4},{6,7},{7,6},{8,9},{9,8},{10,11... | collective-permute-start | bytes 1572872 | tf_op jit(solution)/shard_map/ppermute | solution.py:380
  53.4 15.6 %collective-permute-start.10 = (bf16[256,1024]{1,0:T(8,128)(2,1)S(1)}, bf16[256,1024]{1,0:T(8,128)(2,1)S(1)}, u32[]{:S(2)}, u32[]{:S(2)}) collective-permute-start(bf16[256,1024]{1,0:T(8,128)(2,1)S(1)} %shard_map.103.refs_0_.refs_4_), channel_id=1, source_target_pairs={{0,2},{2,4},{4,6},{6,0},{1,3},{3,5},{5,7},{7,1},{8,10},{10,12},{12... | collective-permute-start | bytes 1572872 | tf_op jit(solution)/shard_map/ppermute | solution.py:380
  54.3 14.7 %collective-permute-start.11 = (bf16[256,1024]{1,0:T(8,128)(2,1)S(1)}, bf16[256,1024]{1,0:T(8,128)(2,1)S(1)}, u32[]{:S(2)}, u32[]{:S(2)}) collective-permute-start(bf16[256,1024]{1,0:T(8,128)(2,1)S(1)} %shard_map.103.refs_0_.refs_4_), channel_id=1, source_target_pairs={{0,6},{2,0},{4,2},{6,4},{1,7},{3,1},{5,3},{7,5},{8,14},{10,8},{12,... | collective-permute-start | bytes 1572872 | tf_op jit(solution)/shard_map/ppermute | solution.py:380
  62.5 6.5 %collective-permute-start.7 = (bf16[2,128,128]{2,1,0:T(8,128)(2,1)S(1)}, bf16[2,128,128]{2,1,0:T(8,128)(2,1)S(1)}, u32[]{:S(2)}, u32[]{:S(2)}) collective-permute-start(bf16[2,128,128]{2,1,0:T(8,128)(2,1)S(1)} %get-tuple-element.43), channel_id=1, source_target_pairs={{0,8},{8,16},{16,24},{24,0},{1,9},{9,17},{17,25},{25,1},{2,10},{10... | collective-permute-start | bytes 196616 | tf_op jit(solution)/shard_map/ppermute | solution.py:380
  63.9 8.6 %collective-permute-start.8 = (bf16[2,128,128]{2,1,0:T(8,128)(2,1)S(1)}, bf16[2,128,128]{2,1,0:T(8,128)(2,1)S(1)}, u32[]{:S(2)}, u32[]{:S(2)}) collective-permute-start(bf16[2,128,128]{2,1,0:T(8,128)(2,1)S(1)} %get-tuple-element.44), channel_id=1, source_target_pairs={{0,16},{8,24},{16,0},{24,8},{1,17},{9,25},{17,1},{25,9},{2,18},{10... | collective-permute-start | bytes 196616 | tf_op jit(solution)/shard_map/ppermute | solution.py:380
  67.4 5.1 %collective-permute-start.9 = (bf16[2,128,128]{2,1,0:T(8,128)(2,1)S(1)}, bf16[2,128,128]{2,1,0:T(8,128)(2,1)S(1)}, u32[]{:S(2)}, u32[]{:S(2)}) collective-permute-start(bf16[2,128,128]{2,1,0:T(8,128)(2,1)S(1)} %get-tuple-element.45), channel_id=1, source_target_pairs={{0,24},{8,0},{16,8},{24,16},{1,25},{9,1},{17,9},{25,17},{2,26},{10... | collective-permute-start | bytes 196616 | tf_op jit(solution)/shard_map/ppermute | solution.py:380
  69.0 6.6 %copy-start = (bf16[256,1024]{1,0:T(8,128)(2,1)}, bf16[256,1024]{1,0:T(8,128)(2,1)S(1)}, u32[]{:S(2)}) copy-start(bf16[256,1024]{1,0:T(8,128)(2,1)S(1)} %collective-permute-done.11.refs_7_.refs_6_) | copy-start | bytes 1572868
  74.3 4.0 %collective-permute-start.12 = (bf16[8,128,128]{2,1,0:T(8,128)(2,1)S(1)}, bf16[8,128,128]{2,1,0:T(8,128)(2,1)S(1)}, u32[]{:S(2)}, u32[]{:S(2)}) collective-permute-start(bf16[8,128,128]{2,1,0:T(8,128)(2,1)S(1)} %get-tuple-element.47.refs_4_.refs_0_), channel_id=1, source_target_pairs={{0,1},{1,0},{2,3},{3,2},{4,5},{5,4},{6,7},{7,6},{8,9},{9,8},{10,11... | collective-permute-start | bytes 786440 | tf_op jit(solution)/shard_map/ppermute | solution.py:380
  75.5 9.2 %collective-permute-start.16 = (bf16[128,1024]{1,0:T(8,128)(2,1)S(1)}, bf16[128,1024]{1,0:T(8,128)(2,1)S(1)}, u32[]{:S(2)}, u32[]{:S(2)}) collective-permute-start(bf16[128,1024]{1,0:T(8,128)(2,1)S(1)} %slice.18), channel_id=1, source_target_pairs={{0,2},{2,4},{4,6},{6,0},{1,3},{3,5},{5,7},{7,1},{8,10},{10,12},{12... | collective-permute-start | bytes 786440 | tf_op jit(solution)/shard_map/ppermute | solution.py:380
  75.6 9.1 %collective-permute-start.17 = (bf16[128,1024]{1,0:T(8,128)(2,1)S(1)}, bf16[128,1024]{1,0:T(8,128)(2,1)S(1)}, u32[]{:S(2)}, u32[]{:S(2)}) collective-permute-start(bf16[128,1024]{1,0:T(8,128)(2,1)S(1)} %slice.19), channel_id=1, source_target_pairs={{0,6},{2,0},{4,2},{6,4},{1,7},{3,1},{5,3},{7,5},{8,14},{10,8},{12,... | collective-permute-start | bytes 786440 | tf_op jit(solution)/shard_map/ppermute | solution.py:380
  78.4 6.4 %copy-start.4 = (bf16[11,128,128]{2,1,0:T(8,128)(2,1)S(1)}, bf16[11,128,128]{2,1,0:T(8,128)(2,1)}, u32[]{:S(2)}) copy-start(bf16[11,128,128]{2,1,0:T(8,128)(2,1)} %copy-done.2) | copy-start | bytes 1081348
  82.0 2.7 %copy-start.18 = (bf16[2,5,128,128]{3,2,1,0:T(8,128)(2,1)}, bf16[2,5,128,128]{3,2,1,0:T(8,128)(2,1)S(1)}, u32[]{:S(2)}) copy-start(bf16[2,5,128,128]{3,2,1,0:T(8,128)(2,1)S(1)} %get-tuple-element.51) | copy-start | bytes 983044
  82.1 2.7 %copy-start.19 = (bf16[2,5,128,128]{3,2,1,0:T(8,128)(2,1)}, bf16[2,5,128,128]{3,2,1,0:T(8,128)(2,1)S(1)}, u32[]{:S(2)}) copy-start(bf16[2,5,128,128]{3,2,1,0:T(8,128)(2,1)S(1)} %get-tuple-element.50) | copy-start | bytes 983044
  89.5 10.2 %copy-start.17 = (bf16[2,5,128,128]{3,2,1,0:T(8,128)(2,1)S(1)}, bf16[2,5,128,128]{3,2,1,0:T(8,128)(2,1)}, u32[]{:S(2)}) copy-start(bf16[2,5,128,128]{3,2,1,0:T(8,128)(2,1)} %copy-done.16) | copy-start | bytes 983044
  89.5 24.8 %copy-start.1 = (bf16[256,1024]{1,0:T(8,128)(2,1)S(1)}, bf16[256,1024]{1,0:T(8,128)(2,1)}, u32[]{:S(2)}) copy-start(bf16[256,1024]{1,0:T(8,128)(2,1)} %copy-done) | copy-start | bytes 1572868
  89.5 30.8 %all-to-all-start.1 = ((bf16[32,32,256]{2,1,0:T(8,128)(2,1)}), bf16[32,32,256]{2,1,0:T(8,128)(2,1)}, u32[]{:S(2)}, u32[]{:S(2)}) async-start(bf16[32,32,256]{2,1,0:T(8,128)(2,1)} %copy-done.5), calls=%async_computation.1 | async-start | bytes 1048576 | tf_op jit(solution)/shard_map/all_to_all | solution.py:480
  97.0 9.7 %collective-permute-start.13 = (bf16[2,5,128,128]{3,2,1,0:T(8,128)(2,1)}, bf16[2,5,128,128]{3,2,1,0:T(8,128)(2,1)S(1)}, u32[]{:S(2)}, u32[]{:S(2)}) collective-permute-start(bf16[2,5,128,128]{3,2,1,0:T(8,128)(2,1)} %copy-done.19), channel_id=1, source_target_pairs={{0,2},{2,4},{4,6},{6,0},{1,3},{3,5},{5,7},{7,1},{8,10},{10,12},{12... | collective-permute-start | bytes 983048 | tf_op jit(solution)/shard_map/ppermute | solution.py:380
  97.1 9.6 %collective-permute-start.14 = (bf16[2,5,128,128]{3,2,1,0:T(8,128)(2,1)}, bf16[2,5,128,128]{3,2,1,0:T(8,128)(2,1)S(1)}, u32[]{:S(2)}, u32[]{:S(2)}) collective-permute-start(bf16[2,5,128,128]{3,2,1,0:T(8,128)(2,1)} %copy-done.18), channel_id=1, source_target_pairs={{0,6},{2,0},{4,2},{6,4},{1,7},{3,1},{5,3},{7,5},{8,14},{10,8},{12,... | collective-permute-start | bytes 983048 | tf_op jit(solution)/shard_map/ppermute | solution.py:380
  99.8 14.6 %collective-permute-start.15 = (bf16[2,5,128,128]{3,2,1,0:T(8,128)(2,1)S(1)}, bf16[2,5,128,128]{3,2,1,0:T(8,128)(2,1)S(1)}, u32[]{:S(2)}, u32[]{:S(2)}) collective-permute-start(bf16[2,5,128,128]{3,2,1,0:T(8,128)(2,1)S(1)} %copy-done.17), channel_id=1, source_target_pairs={{0,4},{2,6},{4,0},{6,2},{1,5},{3,7},{5,1},{7,3},{8,12},{10,14},{12... | collective-permute-start | bytes 983048 | tf_op jit(solution)/shard_map/ppermute | solution.py:380
  118.0 10.3 %collective-permute-start.18 = (bf16[20,128,128]{2,1,0:T(8,128)(2,1)S(1)}, bf16[20,128,128]{2,1,0:T(8,128)(2,1)S(1)}, u32[]{:S(2)}, u32[]{:S(2)}) collective-permute-start(bf16[20,128,128]{2,1,0:T(8,128)(2,1)S(1)} %get-tuple-element.54), channel_id=1, source_target_pairs={{0,1},{1,0},{2,3},{3,2},{4,5},{5,4},{6,7},{7,6},{8,9},{9,8},{10,11... | collective-permute-start | bytes 1966088 | tf_op jit(solution)/shard_map/ppermute | solution.py:380
  121.4 9.2 %collective-permute-start.19 = (f32[32,256]{1,0:T(8,128)S(1)}, f32[32,256]{1,0:T(8,128)S(1)}, u32[]{:S(2)}, u32[]{:S(2)}) collective-permute-start(f32[32,256]{1,0:T(8,128)S(1)} %broadcast_multiply_fusion), channel_id=1, source_target_pairs={{0,0},{1,32},{2,8},{3,40},{4,16},{5,48},{6,24},{7,56},{8,2},{9,34}... | collective-permute-start | bytes 98312 | tf_op jit(solution)/shard_map/ppermute | solution.py:482
  (11 other events, 9.4 us)

commit v4 on v3

--- a/solution.py
+++ b/solution.py
@@ -45,6 +45,17 @@
         scratch_shapes=list(scratch),
         compiler_params=pltpu.CompilerParams(vmem_limit_bytes=mib * 1024 * 1024),
     )(*args, *after)
+
+
+def gate(value, after):
+    anywhere = pl.BlockSpec(memory_space=pl.ANY)
+    return pl.pallas_call(
+        lambda *refs: None,
+        out_shape=jax.ShapeDtypeStruct(value.shape, value.dtype),
+        in_specs=[anywhere] * (1 + len(after)),
+        out_specs=anywhere,
+        input_output_aliases={0: 0},
+    )(value, *after)
 
 
 def dot(a, b, left=1, right=0):
@@ -411,7 +422,6 @@
         [((C * PASSED, FRAMES, HD), BF)] + [((C * PASSED + 3, FRAMES, HD), BF)] * 2,
         keep,
         swap_cores(give),
-        after=[moved],
     )
     s1, s2 = turn(to_next, "x", X, 1), turn(to_back, "x", X, -1)
     rows = (s0, s1, s2, turn(s1[:PASSED], "x", X, 1), turn(s2[:PASSED], "x", X, -1))
@@ -467,6 +477,7 @@
         *edges,
         scratch=[chunk_scratch] * 3,
         smem=1,
+        after=[top, bottom],
     )
     (term,) = call(
         weight_kernel,
@@ -475,9 +486,9 @@
         partner,
         *rows,
         scratch=[pltpu.VMEM((BLOCKS, C, FRAMES, HD), BF)],
-        after=[r0, top, bottom],
-    )
-    term = lax.all_to_all(term, ACROSS, 0, 0, tiled=True)
+    )
+    h1, h2, h3 = turn(h1, "x", X, 1), turn(h2, "x", X, 2), turn(h3, "x", X, -1)
+    term = lax.all_to_all(gate(term, [r0]), ACROSS, 0, 0, tiled=True)
     grad_weight = jnp.sum(term.astype(F32), axis=0) / math.sqrt(Y * H * LENGTH)
     grad_weight = lax.ppermute(grad_weight, ALL, swap_pairs())
 
@@ -485,9 +496,9 @@
         encode_kernel,
         [(side, BF)] * 2,
         r0,
-        turn(h1, "x", X, 1),
-        turn(h3, "x", X, -1),
-        turn(h2, "x", X, 2),
+        h1,
+        h3,
+        h2,
         weight,
         w1,
         w2,

time: 134 us -> 128 us (0.955); the launches traced: 131 us -> 127 us
  waiting for transfers between devices: 38.7 us -> 31.8 us
  starting transfers between devices: 57.5 us -> 61.6 us
    ppermute x18, waiting for transfers between devices: 34.6 us -> 23.2 us  [turn(): lax.ppermute(value, axis, [(i, (i + shift) % size) for i in range(size)])]
    ppermute x18, starting transfers between devices: 27.5 us -> 33.6 us  [turn(): lax.ppermute(value, axis, [(i, (i + shift) % size) for i in range(size)])]
    all_to_all x1, waiting for transfers between devices: 1.32 us -> 7.2 us  [body(): lax.all_to_all(jnp.broadcast_to(moved[None], (group, ROWS, COLS)), ACROSS...]
    all_to_all x1, starting transfers between devices: 7.46 us -> 5.98 us  [body(): term = lax.all_to_all(gate(term, [r0]), ACROSS, 0, 0, tiled=True)]
    all_to_all x1, starting transfers between devices: 8.7 us -> 7.32 us  [body(): lax.all_to_all(jnp.broadcast_to(moved[None], (group, ROWS, COLS)), ACROSS...]
    unnamed x43 -> x39, local copies, waits for them, and re-layouts: 11.1 us -> 9.93 us
  transfers between devices with their start and end apart: 22 -> 22, of which waited for: 10 -> 9; matrix products, arithmetic and copies ran while one was open for 3% -> 3% of each run, Pallas kernels for 7% -> 7%
where the time goes in v4:
time: 128 us; the launch traced here: 127 us
  starting transfers between devices  61.6 us (48%)
  waiting for transfers between devices  31.8 us (25%)
  Pallas kernels  19 us (15%)
  local copies, waits for them, and re-layouts  12.4 us (10%)
    ppermute x18, starting transfers between devices, turn(): lax.ppermute(value, axis, [(i, (i + shift) % size) for i in range(size)])  33.6 us
    ppermute x18, waiting for transfers between devices, turn(): lax.ppermute(value, axis, [(i, (i + shift) % size) for i in range(size)])  23.2 us
    pallas_call x11, Pallas kernels, call(): pl.pallas_call(run, out_shape=[jax.ShapeDtypeStruct(shape, dtype) for sha...  19 us
    unnamed x39, local copies, waits for them, and re-layouts  9.93 us
    ppermute x1, starting transfers between devices, body(): moved = lax.ppermute(out_weight, ALL, swap_pairs())  7.89 us
    all_to_all x1, starting transfers between devices, body(): lax.all_to_all(jnp.broadcast_to(moved[None], (group, ROWS, COLS)), ACROSS...  7.32 us
    all_to_all x1, waiting for transfers between devices, body(): lax.all_to_all(jnp.broadcast_to(moved[None], (group, ROWS, COLS)), ACROSS...  7.2 us
    ppermute x1, starting transfers between devices, body(): grad_weight = lax.ppermute(grad_weight, ALL, swap_pairs())  6.86 us
  transfers between devices with their start and end apart: 22, of which 9 were waited for; matrix products, arithmetic and copies ran while one was open for 3% of the time, Pallas kernels for 7%

profile of v4, /device:TPU:1, one launch (start us, length us, event | category | flops | bytes accessed | tf_op | source)
XLA Modules:
  0.0 126.9 jit_solution(16129218800258469368)
XLA Ops:
  0.6 2.8 %shard_map.101 = (bf16[20,128,128]{2,1,0:T(8,128)(2,1)}, bf16[20,128,128]{2,1,0:T(8,128)(2,1)}) custom-call(bf16[1,128,1024]{2,1,0:T(8,128)(2,1)} %refs_0_.5, bf16[1,128,1024]{2,1,0:T(8,128)(2,1)} %refs_1_.1, bf16[1,128,1024]{2,1,0:T(8,128)(2,1)} %refs_2_.1, bf16[1,128,2048]{2,1,0:T(8,128)(2,1)} %refs_3_.1), custom_call_target="tpu_custom_call" | custom-call | tf_op jit(solution)/shard_map/pallas_call | solution.py:40
  3.4 3.3 %collective-permute-start = (bf16[20,128,128]{2,1,0:T(8,128)(2,1)}, bf16[20,128,128]{2,1,0:T(8,128)(2,1)S(1)}, u32[]{:S(2)}, u32[]{:S(2)}) collective-permute-start(bf16[20,128,128]{2,1,0:T(8,128)(2,1)} %get-tuple-element.33), channel_id=1, source_target_pairs={{0,1},{1,0},{2,3},{3,2},{4,5},{5,4},{6,7},{7,6},{8,9},{9,8},{10,11... | collective-permute-start | bytes 1966088 | tf_op jit(solution)/shard_map/ppermute | solution.py:391
  6.7 1.9 %collective-permute-done.refs_1_ = bf16[20,128,128]{2,1,0:T(8,128)(2,1)S(1)} collective-permute-done((bf16[20,128,128]{2,1,0:T(8,128)(2,1)}, bf16[20,128,128]{2,1,0:T(8,128)(2,1)S(1)}, u32[]{:S(2)}, u32[]{:S(2)}) %collective-permute-start) | collective-permute-done | bytes 655392 | tf_op jit(solution)/shard_map/ppermute | solution.py:391
  9.7 1.4 %shard_map.102 = (bf16[22,128,128]{2,1,0:T(8,128)(2,1)S(1)}, bf16[25,128,128]{2,1,0:T(8,128)(2,1)}, bf16[25,128,128]{2,1,0:T(8,128)(2,1)}) custom-call(bf16[20,128,128]{2,1,0:T(8,128)(2,1)S(1)} %copy-done.16, bf16[20,128,128]{2,1,0:T(8,128)(2,1)S(1)} %collective-permute-done.refs_1_), custom_call_target="tpu_custom_call" | custom-call | tf_op jit(solution)/shard_map/pallas_call | solution.py:40
  11.1 2.7 %collective-permute-start.2 = (bf16[25,128,128]{2,1,0:T(8,128)(2,1)}, bf16[25,128,128]{2,1,0:T(8,128)(2,1)S(1)}, u32[]{:S(2)}, u32[]{:S(2)}) collective-permute-start(bf16[25,128,128]{2,1,0:T(8,128)(2,1)} %get-tuple-element.36), channel_id=1, source_target_pairs={{0,6},{2,0},{4,2},{6,4},{1,7},{3,1},{5,3},{7,5},{8,14},{10,8},{12,... | collective-permute-start | bytes 2457608 | tf_op jit(solution)/shard_map/ppermute | solution.py:391
  13.8 7.9 %collective-permute-start.5 = (bf16[32,256]{1,0:T(8,128)(2,1)S(1)}, bf16[32,256]{1,0:T(8,128)(2,1)S(1)}, u32[]{:S(2)}, u32[]{:S(2)}) collective-permute-start(bf16[32,256]{1,0:T(8,128)(2,1)S(1)} %copy-done.18), channel_id=1, source_target_pairs={{0,0},{1,32},{2,8},{3,40},{4,16},{5,48},{6,24},{7,56},{8,2},{9,34}... | collective-permute-start | bytes 49160 | tf_op jit(solution)/shard_map/ppermute | solution.py:405
  21.7 1.4 %collective-permute-done.5 = bf16[32,256]{1,0:T(8,128)(2,1)S(1)} collective-permute-done((bf16[32,256]{1,0:T(8,128)(2,1)S(1)}, bf16[32,256]{1,0:T(8,128)(2,1)S(1)}, u32[]{:S(2)}, u32[]{:S(2)}) %collective-permute-start.5) | collective-permute-done | bytes 16416 | tf_op jit(solution)/shard_map/ppermute | solution.py:405
  23.9 7.3 %all-to-all-start = ((bf16[32,32,256]{2,1,0:T(8,128)(2,1)}), bf16[32,32,256]{2,1,0:T(8,128)(2,1)S(1)}, u32[]{:S(2)}, u32[]{:S(2)}) async-start(bf16[32,32,256]{2,1,0:T(8,128)(2,1)} %broadcast_in_dim.2), calls=%async_computation | async-start | bytes 1048576 | tf_op jit(solution)/shard_map/all_to_all | solution.py:406
  33.5 2.7 %collective-permute-start.4 = (bf16[11,128,128]{2,1,0:T(8,128)(2,1)}, bf16[11,128,128]{2,1,0:T(8,128)(2,1)}, u32[]{:S(2)}, u32[]{:S(2)}) collective-permute-start(bf16[11,128,128]{2,1,0:T(8,128)(2,1)} %slice.17), channel_id=1, source_target_pairs={{0,6},{2,0},{4,2},{6,4},{1,7},{3,1},{5,3},{7,5},{8,14},{10,8},{12,... | collective-permute-start | bytes 1081352 | tf_op jit(solution)/shard_map/ppermute | solution.py:391
  36.2 7.2 %all-to-all-done.refs_0_ = bf16[32,32,256]{2,1,0:T(8,128)(2,1)S(1)} async-done(((bf16[32,32,256]{2,1,0:T(8,128)(2,1)}), bf16[32,32,256]{2,1,0:T(8,128)(2,1)S(1)}, u32[]{:S(2)}, u32[]{:S(2)}) %all-to-all-start) | async-done | bytes 524320 | tf_op jit(solution)/shard_map/all_to_all | solution.py:406
  45.3 1.9 %shard_map.104 = (f32[8,128,128]{2,1,0:T(8,128)S(1)}, f32[8,128,128]{2,1,0:T(8,128)S(1)}) custom-call(bf16[256,1024]{1,0:T(8,128)(2,1)S(1)} %shard_map.103.refs_0_.refs_4_, bf16[22,128,128]{2,1,0:T(8,128)(2,1)S(1)} %get-tuple-element.34.refs_1_.refs_2_, bf16[25,128,128]{2,1,0:T(8,128)(2,1)S(1)} %collective-permute-done.1.refs_2_.refs_3_, ...), custom_call_target="tpu_custom_call" | custom-call | tf_op jit(solution)/shard_map/pallas_call | solution.py:40
  47.2 5.6 %collective-permute-start.6 = (f32[8,128,128]{2,1,0:T(8,128)S(1)}, f32[8,128,128]{2,1,0:T(8,128)S(1)}, u32[]{:S(2)}, u32[]{:S(2)}) collective-permute-start(f32[8,128,128]{2,1,0:T(8,128)S(1)} %get-tuple-element.37.refs_6_), channel_id=1, source_target_pairs={{0,1},{1,0},{2,3},{3,2},{4,5},{5,4},{6,7},{7,6},{8,9},{9,8},{10,11... | collective-permute-start | bytes 1572872 | tf_op jit(solution)/shard_map/ppermute | solution.py:391
  52.8 3.1 %collective-permute-start.11 = (bf16[256,1024]{1,0:T(8,128)(2,1)S(1)}, bf16[256,1024]{1,0:T(8,128)(2,1)S(1)}, u32[]{:S(2)}, u32[]{:S(2)}) collective-permute-start(bf16[256,1024]{1,0:T(8,128)(2,1)S(1)} %shard_map.103.refs_0_.refs_4_), channel_id=1, source_target_pairs={{0,6},{2,0},{4,2},{6,4},{1,7},{3,1},{5,3},{7,5},{8,14},{10,8},{12,... | collective-permute-start | bytes 1572872 | tf_op jit(solution)/shard_map/ppermute | solution.py:391
  56.9 2.0 %shard_map.105 = (bf16[8,3,128,128]{3,2,1,0:T(8,128)(2,1)S(1)}, f32[12,128,128]{2,1,0:T(8,128)S(1)}, bf16[3,128,128]{2,1,0:T(8,128)(2,1)S(1)}) custom-call(s32[1,12]{1,0:T(1,128)S(1)} %copy-done.17, bf16[22,128,128]{2,1,0:T(8,128)(2,1)S(1)} %get-tuple-element.34.refs_1_.refs_2_, bf16[25,128,128]{2,1,0:T(8,128)(2,1)S(1)} %collective-permute-done.1.refs_2_.refs_3_, ...), custom_call_target="tpu_custom_call" | custom-call | tf_op jit(solution)/shard_map/pallas_call | solution.py:40
  58.9 2.2 %shard_map.106 = (bf16[1024,128]{1,0:T(8,128)(2,1)S(1)}, f32[12,128,128]{2,1,0:T(8,128)S(1)}, bf16[2,128,128]{2,1,0:T(8,128)(2,1)S(1)}, bf16[2,128,128]{2,1,0:T(8,128)(2,1)S(1)}, bf16[2,128,128]{2,1,0:T(8,128)(2,1)S(1)}) custom-call(s32[1,12]{1,0:T(1,128)S(1)} %copy-done.17, bf16[8,3,128,128]{3,2,1,0:T(8,128)(2,1)S(1)} %get-tuple-element.38.refs_1_, ...), custom_call_target="tpu_custom_call" | custom-call | tf_op jit(solution)/shard_map/pallas_call | solution.py:40
  61.1 3.7 %collective-permute-start.7 = (bf16[2,128,128]{2,1,0:T(8,128)(2,1)S(1)}, bf16[2,128,128]{2,1,0:T(8,128)(2,1)S(1)}, u32[]{:S(2)}, u32[]{:S(2)}) collective-permute-start(bf16[2,128,128]{2,1,0:T(8,128)(2,1)S(1)} %get-tuple-element.43), channel_id=1, source_target_pairs={{0,8},{8,16},{16,24},{24,0},{1,9},{9,17},{17,25},{25,1},{2,10},{10... | collective-permute-start | bytes 196616 | tf_op jit(solution)/shard_map/ppermute | solution.py:391
  64.8 2.2 %collective-permute-start.9 = (bf16[2,128,128]{2,1,0:T(8,128)(2,1)S(1)}, bf16[2,128,128]{2,1,0:T(8,128)(2,1)S(1)}, u32[]{:S(2)}, u32[]{:S(2)}) collective-permute-start(bf16[2,128,128]{2,1,0:T(8,128)(2,1)S(1)} %get-tuple-element.45), channel_id=1, source_target_pairs={{0,24},{8,0},{16,8},{24,16},{1,25},{9,1},{17,9},{25,17},{2,26},{10... | collective-permute-start | bytes 196616 | tf_op jit(solution)/shard_map/ppermute | solution.py:391
  68.2 2.3 %collective-permute-done.8.refs_4_.refs_8_ = bf16[2,128,128]{2,1,0:T(8,128)(2,1)S(1)} collective-permute-done((bf16[2,128,128]{2,1,0:T(8,128)(2,1)S(1)}, bf16[2,128,128]{2,1,0:T(8,128)(2,1)S(1)}, u32[]{:S(2)}, u32[]{:S(2)}) %collective-permute-start.8) | collective-permute-done | bytes 65568 | tf_op jit(solution)/shard_map/ppermute | solution.py:391
  70.5 1.6 %shard_map.107 = (bf16[8,128,128]{2,1,0:T(8,128)(2,1)S(1)}, bf16[12,128,128]{2,1,0:T(8,128)(2,1)S(1)}) custom-call(s32[1,12]{1,0:T(1,128)S(1)} %copy-done.17, bf16[8,3,128,128]{3,2,1,0:T(8,128)(2,1)S(1)} %get-tuple-element.38.refs_1_, f32[12,128,128]{2,1,0:T(8,128)S(1)} %get-tuple-element.42.refs_2_, ...), custom_call_target="tpu_custom_call" | custom-call | tf_op jit(solution)/shard_map/pallas_call | solution.py:40
  72.1 1.5 %collective-permute-start.12 = (bf16[8,128,128]{2,1,0:T(8,128)(2,1)S(1)}, bf16[8,128,128]{2,1,0:T(8,128)(2,1)S(1)}, u32[]{:S(2)}, u32[]{:S(2)}) collective-permute-start(bf16[8,128,128]{2,1,0:T(8,128)(2,1)S(1)} %get-tuple-element.47.refs_4_.refs_0_), channel_id=1, source_target_pairs={{0,1},{1,0},{2,3},{3,2},{4,5},{5,4},{6,7},{7,6},{8,9},{9,8},{10,11... | collective-permute-start | bytes 786440 | tf_op jit(solution)/shard_map/ppermute | solution.py:391
  73.7 2.8 %collective-permute-start.14 = (bf16[128,1024]{1,0:T(8,128)(2,1)S(1)}, bf16[128,1024]{1,0:T(8,128)(2,1)S(1)}, u32[]{:S(2)}, u32[]{:S(2)}) collective-permute-start(bf16[128,1024]{1,0:T(8,128)(2,1)S(1)} %slice.19), channel_id=1, source_target_pairs={{0,6},{2,0},{4,2},{6,4},{1,7},{3,1},{5,3},{7,5},{8,14},{10,8},{12,... | collective-permute-start | bytes 786440 | tf_op jit(solution)/shard_map/ppermute | solution.py:391
  76.5 1.8 %shard_map.111.refs_0_ = bf16[32,32,256]{2,1,0:T(8,128)(2,1)S(1)} custom-call(bf16[8,128,128]{2,1,0:T(8,128)(2,1)S(1)} %get-tuple-element.47.refs_4_.refs_0_, bf16[8,128,128]{2,1,0:T(8,128)(2,1)S(1)} %collective-permute-done.12.refs_5_.refs_1_, bf16[22,128,128]{2,1,0:T(8,128)(2,1)S(1)} %get-tuple-element.34.refs_1_.refs_2_, ...), custom_call_target="tpu_custom_call" | custom-call | tf_op jit(solution)/shard_map/pallas_call | solution.py:40
  79.1 3.6 %collective-permute-done.13.refs_10_.refs_7_ = bf16[128,1024]{1,0:T(8,128)(2,1)S(1)} collective-permute-done((bf16[128,1024]{1,0:T(8,128)(2,1)S(1)}, bf16[128,1024]{1,0:T(8,128)(2,1)S(1)}, u32[]{:S(2)}, u32[]{:S(2)}) %collective-permute-start.13) | collective-permute-done | bytes 262176 | tf_op jit(solution)/shard_map/ppermute | solution.py:391
  82.7 2.5 %shard_map.108 = (bf16[2,5,128,128]{3,2,1,0:T(8,128)(2,1)S(1)}, bf16[2,5,128,128]{3,2,1,0:T(8,128)(2,1)S(1)}, bf16[2,5,128,128]{3,2,1,0:T(8,128)(2,1)S(1)}, bf16[2,5,128,128]{3,2,1,0:T(8,128)(2,1)S(1)}) custom-call(s32[1,12]{1,0:T(1,128)S(1)} %copy-done.17, bf16[8,3,128,128]{3,2,1,0:T(8,128)(2,1)S(1)} %get-tuple-element.38.refs_1_, ...), custom_call_target="tpu_custom_call" | custom-call | tf_op jit(solution)/shard_map/pallas_call | solution.py:40
  86.0 6.0 %all-to-all-start.1 = ((bf16[32,32,256]{2,1,0:T(8,128)(2,1)}), bf16[32,32,256]{2,1,0:T(8,128)(2,1)}, u32[]{:S(2)}, u32[]{:S(2)}) async-start(bf16[32,32,256]{2,1,0:T(8,128)(2,1)} %shard_map.112), calls=%async_computation.1 | async-start | bytes 1048576 | tf_op jit(solution)/shard_map/all_to_all | solution.py:491
  92.1 2.7 %collective-permute-start.16 = (bf16[2,5,128,128]{3,2,1,0:T(8,128)(2,1)S(1)}, bf16[2,5,128,128]{3,2,1,0:T(8,128)(2,1)S(1)}, u32[]{:S(2)}, u32[]{:S(2)}) collective-permute-start(bf16[2,5,128,128]{3,2,1,0:T(8,128)(2,1)S(1)} %get-tuple-element.51), channel_id=1, source_target_pairs={{0,6},{2,0},{4,2},{6,4},{1,7},{3,1},{5,3},{7,5},{8,14},{10,8},{12,... | collective-permute-start | bytes 983048 | tf_op jit(solution)/shard_map/ppermute | solution.py:391
  95.7 5.7 %collective-permute-done.15.refs_1_ = bf16[2,5,128,128]{3,2,1,0:T(8,128)(2,1)S(1)} collective-permute-done((bf16[2,5,128,128]{3,2,1,0:T(8,128)(2,1)S(1)}, bf16[2,5,128,128]{3,2,1,0:T(8,128)(2,1)S(1)}, u32[]{:S(2)}, u32[]{:S(2)}) %collective-permute-start.15) | collective-permute-done | bytes 327712 | tf_op jit(solution)/shard_map/ppermute | solution.py:391
  101.4 7.7 %collective-permute-done.17.refs_3_ = bf16[2,5,128,128]{3,2,1,0:T(8,128)(2,1)S(1)} collective-permute-done((bf16[2,5,128,128]{3,2,1,0:T(8,128)(2,1)S(1)}, bf16[2,5,128,128]{3,2,1,0:T(8,128)(2,1)S(1)}, u32[]{:S(2)}, u32[]{:S(2)}) %collective-permute-start.17) | collective-permute-done | bytes 327712 | tf_op jit(solution)/shard_map/ppermute | solution.py:391
  111.0 1.6 %shard_map.109 = (bf16[20,128,128]{2,1,0:T(8,128)(2,1)S(1)}, bf16[20,128,128]{2,1,0:T(8,128)(2,1)}) custom-call(bf16[2,5,128,128]{3,2,1,0:T(8,128)(2,1)S(1)} %copy-done.9, bf16[2,5,128,128]{3,2,1,0:T(8,128)(2,1)S(1)} %collective-permute-done.15.refs_1_, bf16[2,5,128,128]{3,2,1,0:T(8,128)(2,1)S(1)} %collective-permute-done.16.refs_2_, ...), custom_call_target="tpu_custom_call" | custom-call | tf_op jit(solution)/shard_map/pallas_call | solution.py:40
  113.5 2.3 %collective-permute-start.18 = (bf16[20,128,128]{2,1,0:T(8,128)(2,1)}, bf16[20,128,128]{2,1,0:T(8,128)(2,1)S(1)}, u32[]{:S(2)}, u32[]{:S(2)}) collective-permute-start(bf16[20,128,128]{2,1,0:T(8,128)(2,1)} %get-tuple-element.54), channel_id=1, source_target_pairs={{0,1},{1,0},{2,3},{3,2},{4,5},{5,4},{6,7},{7,6},{8,9},{9,8},{10,11... | collective-permute-start | bytes 1966088 | tf_op jit(solution)/shard_map/ppermute | solution.py:391
  116.9 6.9 %collective-permute-start.19 = (f32[32,256]{1,0:T(8,128)S(1)}, f32[32,256]{1,0:T(8,128)S(1)}, u32[]{:S(2)}, u32[]{:S(2)}) collective-permute-start(f32[32,256]{1,0:T(8,128)S(1)} %broadcast_multiply_fusion), channel_id=1, source_target_pairs={{0,0},{1,32},{2,8},{3,40},{4,16},{5,48},{6,24},{7,56},{8,2},{9,34}... | collective-permute-start | bytes 98312 | tf_op jit(solution)/shard_map/ppermute | solution.py:493
  124.9 1.4 %shard_map.110 = (bf16[1,128,2048]{2,1,0:T(8,128)(2,1)}, bf16[1,128,1024]{2,1,0:T(8,128)(2,1)}, bf16[1,128,1024]{2,1,0:T(8,128)(2,1)}, bf16[1,128,1024]{2,1,0:T(8,128)(2,1)}) custom-call(bf16[20,128,128]{2,1,0:T(8,128)(2,1)S(1)} %copy-done.15, bf16[20,128,128]{2,1,0:T(8,128)(2,1)S(1)} %collective-permute-done.18.refs_1_), custom_call_target="tpu_custom_call" | custom-call | tf_op jit(solution)/shard_map/pallas_call | solution.py:40
  (70 shorter events, 16.5 us)
Async XLA Ops:
  3.4 5.3 %collective-permute-start = (bf16[20,128,128]{2,1,0:T(8,128)(2,1)}, bf16[20,128,128]{2,1,0:T(8,128)(2,1)S(1)}, u32[]{:S(2)}, u32[]{:S(2)}) collective-permute-start(bf16[20,128,128]{2,1,0:T(8,128)(2,1)} %get-tuple-element.33), channel_id=1, source_target_pairs={{0,1},{1,0},{2,3},{3,2},{4,5},{5,4},{6,7},{7,6},{8,9},{9,8},{10,11... | collective-permute-start | bytes 1966088 | tf_op jit(solution)/shard_map/ppermute | solution.py:391
  9.7 4.0 %copy-start.18 = (bf16[32,256]{1,0:T(8,128)(2,1)S(1)}, bf16[32,256]{1,0:T(8,128)(2,1)}, u32[]{:S(2)}) copy-start(bf16[32,256]{1,0:T(8,128)(2,1)} %param.10) | copy-start | bytes 49156
  11.1 20.9 %collective-permute-start.1 = (bf16[25,128,128]{2,1,0:T(8,128)(2,1)}, bf16[25,128,128]{2,1,0:T(8,128)(2,1)S(1)}, u32[]{:S(2)}, u32[]{:S(2)}) collective-permute-start(bf16[25,128,128]{2,1,0:T(8,128)(2,1)} %get-tuple-element.35), channel_id=1, source_target_pairs={{0,2},{2,4},{4,6},{6,0},{1,3},{3,5},{5,7},{7,1},{8,10},{10,12},{12... | collective-permute-start | bytes 2457608 | tf_op jit(solution)/shard_map/ppermute | solution.py:391
  11.1 21.6 %collective-permute-start.2 = (bf16[25,128,128]{2,1,0:T(8,128)(2,1)}, bf16[25,128,128]{2,1,0:T(8,128)(2,1)S(1)}, u32[]{:S(2)}, u32[]{:S(2)}) collective-permute-start(bf16[25,128,128]{2,1,0:T(8,128)(2,1)} %get-tuple-element.36), channel_id=1, source_target_pairs={{0,6},{2,0},{4,2},{6,4},{1,7},{3,1},{5,3},{7,5},{8,14},{10,8},{12,... | collective-permute-start | bytes 2457608 | tf_op jit(solution)/shard_map/ppermute | solution.py:391
  13.8 9.3 %collective-permute-start.5 = (bf16[32,256]{1,0:T(8,128)(2,1)S(1)}, bf16[32,256]{1,0:T(8,128)(2,1)S(1)}, u32[]{:S(2)}, u32[]{:S(2)}) collective-permute-start(bf16[32,256]{1,0:T(8,128)(2,1)S(1)} %copy-done.18), channel_id=1, source_target_pairs={{0,0},{1,32},{2,8},{3,40},{4,16},{5,48},{6,24},{7,56},{8,2},{9,34}... | collective-permute-start | bytes 49160 | tf_op jit(solution)/shard_map/ppermute | solution.py:405
  23.9 19.5 %all-to-all-start = ((bf16[32,32,256]{2,1,0:T(8,128)(2,1)}), bf16[32,32,256]{2,1,0:T(8,128)(2,1)S(1)}, u32[]{:S(2)}, u32[]{:S(2)}) async-start(bf16[32,32,256]{2,1,0:T(8,128)(2,1)} %broadcast_in_dim.2), calls=%async_computation | async-start | bytes 1048576 | tf_op jit(solution)/shard_map/all_to_all | solution.py:406
  32.7 12.6 %collective-permute-start.3 = (bf16[11,128,128]{2,1,0:T(8,128)(2,1)}, bf16[11,128,128]{2,1,0:T(8,128)(2,1)S(1)}, u32[]{:S(2)}, u32[]{:S(2)}) collective-permute-start(bf16[11,128,128]{2,1,0:T(8,128)(2,1)} %slice.16), channel_id=1, source_target_pairs={{0,2},{2,4},{4,6},{6,0},{1,3},{3,5},{5,7},{7,1},{8,10},{10,12},{12... | collective-permute-start | bytes 1081352 | tf_op jit(solution)/shard_map/ppermute | solution.py:391
  33.5 11.8 %collective-permute-start.4 = (bf16[11,128,128]{2,1,0:T(8,128)(2,1)}, bf16[11,128,128]{2,1,0:T(8,128)(2,1)}, u32[]{:S(2)}, u32[]{:S(2)}) collective-permute-start(bf16[11,128,128]{2,1,0:T(8,128)(2,1)} %slice.17), channel_id=1, source_target_pairs={{0,6},{2,0},{4,2},{6,4},{1,7},{3,1},{5,3},{7,5},{8,14},{10,8},{12,... | collective-permute-start | bytes 1081352 | tf_op jit(solution)/shard_map/ppermute | solution.py:391
  45.3 1.9 %copy-start.3 = (bf16[11,128,128]{2,1,0:T(8,128)(2,1)}, bf16[11,128,128]{2,1,0:T(8,128)(2,1)S(1)}, u32[]{:S(2)}) copy-start(bf16[11,128,128]{2,1,0:T(8,128)(2,1)S(1)} %collective-permute-done.3.refs_4_.refs_5_) | copy-start | bytes 1081348
  47.2 8.7 %copy-start.17 = (s32[1,12]{1,0:T(1,128)S(1)}, s32[1,12]{1,0:T(1,128)}, u32[]{:S(2)}) copy-start(s32[1,12]{1,0:T(1,128)} %refs_0_.9) | copy-start | bytes 148
  47.2 11.7 %collective-permute-start.6 = (f32[8,128,128]{2,1,0:T(8,128)S(1)}, f32[8,128,128]{2,1,0:T(8,128)S(1)}, u32[]{:S(2)}, u32[]{:S(2)}) collective-permute-start(f32[8,128,128]{2,1,0:T(8,128)S(1)} %get-tuple-element.37.refs_6_), channel_id=1, source_target_pairs={{0,1},{1,0},{2,3},{3,2},{4,5},{5,4},{6,7},{7,6},{8,9},{9,8},{10,11... | collective-permute-start | bytes 1572872 | tf_op jit(solution)/shard_map/ppermute | solution.py:391
  52.8 15.3 %collective-permute-start.10 = (bf16[256,1024]{1,0:T(8,128)(2,1)S(1)}, bf16[256,1024]{1,0:T(8,128)(2,1)S(1)}, u32[]{:S(2)}, u32[]{:S(2)}) collective-permute-start(bf16[256,1024]{1,0:T(8,128)(2,1)S(1)} %shard_map.103.refs_0_.refs_4_), channel_id=1, source_target_pairs={{0,2},{2,4},{4,6},{6,0},{1,3},{3,5},{5,7},{7,1},{8,10},{10,12},{12... | collective-permute-start | bytes 1572872 | tf_op jit(solution)/shard_map/ppermute | solution.py:391
  52.8 15.3 %collective-permute-start.11 = (bf16[256,1024]{1,0:T(8,128)(2,1)S(1)}, bf16[256,1024]{1,0:T(8,128)(2,1)S(1)}, u32[]{:S(2)}, u32[]{:S(2)}) collective-permute-start(bf16[256,1024]{1,0:T(8,128)(2,1)S(1)} %shard_map.103.refs_0_.refs_4_), channel_id=1, source_target_pairs={{0,6},{2,0},{4,2},{6,4},{1,7},{3,1},{5,3},{7,5},{8,14},{10,8},{12,... | collective-permute-start | bytes 1572872 | tf_op jit(solution)/shard_map/ppermute | solution.py:391
  61.1 7.1 %collective-permute-start.7 = (bf16[2,128,128]{2,1,0:T(8,128)(2,1)S(1)}, bf16[2,128,128]{2,1,0:T(8,128)(2,1)S(1)}, u32[]{:S(2)}, u32[]{:S(2)}) collective-permute-start(bf16[2,128,128]{2,1,0:T(8,128)(2,1)S(1)} %get-tuple-element.43), channel_id=1, source_target_pairs={{0,8},{8,16},{16,24},{24,0},{1,9},{9,17},{17,25},{25,1},{2,10},{10... | collective-permute-start | bytes 196616 | tf_op jit(solution)/shard_map/ppermute | solution.py:391
  64.8 5.7 %collective-permute-start.8 = (bf16[2,128,128]{2,1,0:T(8,128)(2,1)S(1)}, bf16[2,128,128]{2,1,0:T(8,128)(2,1)S(1)}, u32[]{:S(2)}, u32[]{:S(2)}) collective-permute-start(bf16[2,128,128]{2,1,0:T(8,128)(2,1)S(1)} %get-tuple-element.44), channel_id=1, source_target_pairs={{0,16},{8,24},{16,0},{24,8},{1,17},{9,25},{17,1},{25,9},{2,18},{10... | collective-permute-start | bytes 196616 | tf_op jit(solution)/shard_map/ppermute | solution.py:391
  64.8 5.7 %collective-permute-start.9 = (bf16[2,128,128]{2,1,0:T(8,128)(2,1)S(1)}, bf16[2,128,128]{2,1,0:T(8,128)(2,1)S(1)}, u32[]{:S(2)}, u32[]{:S(2)}) collective-permute-start(bf16[2,128,128]{2,1,0:T(8,128)(2,1)S(1)} %get-tuple-element.45), channel_id=1, source_target_pairs={{0,24},{8,0},{16,8},{24,16},{1,25},{9,1},{17,9},{25,17},{2,26},{10... | collective-permute-start | bytes 196616 | tf_op jit(solution)/shard_map/ppermute | solution.py:391
  68.2 5.5 %copy-start.1 = (bf16[256,1024]{1,0:T(8,128)(2,1)}, bf16[256,1024]{1,0:T(8,128)(2,1)S(1)}, u32[]{:S(2)}) copy-start(bf16[256,1024]{1,0:T(8,128)(2,1)S(1)} %collective-permute-done.11.refs_7_.refs_6_) | copy-start | bytes 1572868
  72.1 4.3 %copy-start.5 = (bf16[11,128,128]{2,1,0:T(8,128)(2,1)S(1)}, bf16[11,128,128]{2,1,0:T(8,128)(2,1)}, u32[]{:S(2)}) copy-start(bf16[11,128,128]{2,1,0:T(8,128)(2,1)} %copy-done.3) | copy-start | bytes 1081348
  72.1 4.3 %collective-permute-start.12 = (bf16[8,128,128]{2,1,0:T(8,128)(2,1)S(1)}, bf16[8,128,128]{2,1,0:T(8,128)(2,1)S(1)}, u32[]{:S(2)}, u32[]{:S(2)}) collective-permute-start(bf16[8,128,128]{2,1,0:T(8,128)(2,1)S(1)} %get-tuple-element.47.refs_4_.refs_0_), channel_id=1, source_target_pairs={{0,1},{1,0},{2,3},{3,2},{4,5},{5,4},{6,7},{7,6},{8,9},{9,8},{10,11... | collective-permute-start | bytes 786440 | tf_op jit(solution)/shard_map/ppermute | solution.py:391
  73.7 9.1 %collective-permute-start.13 = (bf16[128,1024]{1,0:T(8,128)(2,1)S(1)}, bf16[128,1024]{1,0:T(8,128)(2,1)S(1)}, u32[]{:S(2)}, u32[]{:S(2)}) collective-permute-start(bf16[128,1024]{1,0:T(8,128)(2,1)S(1)} %slice.18), channel_id=1, source_target_pairs={{0,2},{2,4},{4,6},{6,0},{1,3},{3,5},{5,7},{7,1},{8,10},{10,12},{12... | collective-permute-start | bytes 786440 | tf_op jit(solution)/shard_map/ppermute | solution.py:391
  73.7 9.1 %collective-permute-start.14 = (bf16[128,1024]{1,0:T(8,128)(2,1)S(1)}, bf16[128,1024]{1,0:T(8,128)(2,1)S(1)}, u32[]{:S(2)}, u32[]{:S(2)}) collective-permute-start(bf16[128,1024]{1,0:T(8,128)(2,1)S(1)} %slice.19), channel_id=1, source_target_pairs={{0,6},{2,0},{4,2},{6,4},{1,7},{3,1},{5,3},{7,5},{8,14},{10,8},{12,... | collective-permute-start | bytes 786440 | tf_op jit(solution)/shard_map/ppermute | solution.py:391
  82.7 2.5 %copy-start.10 = (bf16[128,1024]{1,0:T(8,128)(2,1)}, bf16[128,1024]{1,0:T(8,128)(2,1)S(1)}, u32[]{:S(2)}) copy-start(bf16[128,1024]{1,0:T(8,128)(2,1)S(1)} %collective-permute-done.13.refs_10_.refs_7_) | copy-start | bytes 786436
  82.7 2.5 %copy-start.12 = (bf16[128,1024]{1,0:T(8,128)(2,1)}, bf16[128,1024]{1,0:T(8,128)(2,1)S(1)}, u32[]{:S(2)}) copy-start(bf16[128,1024]{1,0:T(8,128)(2,1)S(1)} %collective-permute-done.14.refs_11_.refs_8_) | copy-start | bytes 786436
  86.0 23.1 %copy-start.2 = (bf16[256,1024]{1,0:T(8,128)(2,1)S(1)}, bf16[256,1024]{1,0:T(8,128)(2,1)}, u32[]{:S(2)}) copy-start(bf16[256,1024]{1,0:T(8,128)(2,1)} %copy-done.1) | copy-start | bytes 1572868
  86.0 23.1 %copy-start.11 = (bf16[128,1024]{1,0:T(8,128)(2,1)S(1)}, bf16[128,1024]{1,0:T(8,128)(2,1)}, u32[]{:S(2)}) copy-start(bf16[128,1024]{1,0:T(8,128)(2,1)} %copy-done.10) | copy-start | bytes 786436
  86.0 29.8 %all-to-all-start.1 = ((bf16[32,32,256]{2,1,0:T(8,128)(2,1)}), bf16[32,32,256]{2,1,0:T(8,128)(2,1)}, u32[]{:S(2)}, u32[]{:S(2)}) async-start(bf16[32,32,256]{2,1,0:T(8,128)(2,1)} %shard_map.112), calls=%async_computation.1 | async-start | bytes 1048576 | tf_op jit(solution)/shard_map/all_to_all | solution.py:491
  92.0 9.4 %collective-permute-start.15 = (bf16[2,5,128,128]{3,2,1,0:T(8,128)(2,1)S(1)}, bf16[2,5,128,128]{3,2,1,0:T(8,128)(2,1)S(1)}, u32[]{:S(2)}, u32[]{:S(2)}) collective-permute-start(bf16[2,5,128,128]{3,2,1,0:T(8,128)(2,1)S(1)} %get-tuple-element.50), channel_id=1, source_target_pairs={{0,2},{2,4},{4,6},{6,0},{1,3},{3,5},{5,7},{7,1},{8,10},{10,12},{12... | collective-permute-start | bytes 983048 | tf_op jit(solution)/shard_map/ppermute | solution.py:391
  92.1 9.4 %collective-permute-start.16 = (bf16[2,5,128,128]{3,2,1,0:T(8,128)(2,1)S(1)}, bf16[2,5,128,128]{3,2,1,0:T(8,128)(2,1)S(1)}, u32[]{:S(2)}, u32[]{:S(2)}) collective-permute-start(bf16[2,5,128,128]{3,2,1,0:T(8,128)(2,1)S(1)} %get-tuple-element.51), channel_id=1, source_target_pairs={{0,6},{2,0},{4,2},{6,4},{1,7},{3,1},{5,3},{7,5},{8,14},{10,8},{12,... | collective-permute-start | bytes 983048 | tf_op jit(solution)/shard_map/ppermute | solution.py:391
  94.7 14.4 %collective-permute-start.17 = (bf16[2,5,128,128]{3,2,1,0:T(8,128)(2,1)S(1)}, bf16[2,5,128,128]{3,2,1,0:T(8,128)(2,1)S(1)}, u32[]{:S(2)}, u32[]{:S(2)}) collective-permute-start(bf16[2,5,128,128]{3,2,1,0:T(8,128)(2,1)S(1)} %get-tuple-element.52), channel_id=1, source_target_pairs={{0,4},{2,6},{4,0},{6,2},{1,5},{3,7},{5,1},{7,3},{8,12},{10,14},{12... | collective-permute-start | bytes 983048 | tf_op jit(solution)/shard_map/ppermute | solution.py:391
  113.5 10.3 %collective-permute-start.18 = (bf16[20,128,128]{2,1,0:T(8,128)(2,1)}, bf16[20,128,128]{2,1,0:T(8,128)(2,1)S(1)}, u32[]{:S(2)}, u32[]{:S(2)}) collective-permute-start(bf16[20,128,128]{2,1,0:T(8,128)(2,1)} %get-tuple-element.54), channel_id=1, source_target_pairs={{0,1},{1,0},{2,3},{3,2},{4,5},{5,4},{6,7},{7,6},{8,9},{9,8},{10,11... | collective-permute-start | bytes 1966088 | tf_op jit(solution)/shard_map/ppermute | solution.py:391
  116.9 9.4 %collective-permute-start.19 = (f32[32,256]{1,0:T(8,128)S(1)}, f32[32,256]{1,0:T(8,128)S(1)}, u32[]{:S(2)}, u32[]{:S(2)}) collective-permute-start(f32[32,256]{1,0:T(8,128)S(1)} %broadcast_multiply_fusion), channel_id=1, source_target_pairs={{0,0},{1,32},{2,8},{3,40},{4,16},{5,48},{6,24},{7,56},{8,2},{9,34}... | collective-permute-start | bytes 98312 | tf_op jit(solution)/shard_map/ppermute | solution.py:493
  123.8 1.1 copy-start.15
  (9 other events, 8.2 us)

commit v5 on v4

--- a/solution.py
+++ b/solution.py
@@ -226,7 +226,8 @@
         yield source, jnp.concatenate([wide(part) for part in pair], axis=0)
 
 
-def block_kernel(pieces_ref, weight_ref):
+def cotangent_kernel(pieces_ref, s0, s1, s2, far0, far1, mine_ref, theirs_ref, weight_ref):
+    core = lax.axis_index("c")
     for y in range(Y):
         for h in range(H):
             for z in range(Z):
@@ -234,10 +235,6 @@
                 weight_ref[row : row + ROWS, y * COLS : (y + 1) * COLS] = pieces_ref[
                     (y * H + h) * Z + z
                 ]
-
-
-def cotangent_kernel(weight_ref, s0, s1, s2, far0, far1, mine_ref, theirs_ref):
-    core = lax.axis_index("c")
     weight = weight_ref[...]
     for source, rows in chip_cotangents(s0, s1, s2, far0, far1):
         back = dot(rows, weight, 1, 1)
@@ -426,12 +423,14 @@
     s1, s2 = turn(to_next, "x", X, 1), turn(to_back, "x", X, -1)
     rows = (s0, s1, s2, turn(s1[:PASSED], "x", X, 1), turn(s2[:PASSED], "x", X, -1))
 
-    (weight,) = call(block_kernel, [((2 * HD, HALF), BF)], pieces)
+    mine, theirs, weight = call(
+        cotangent_kernel,
+        [((BLOCKS, FRAMES, HD), F32)] * 2 + [((2 * HD, HALF), BF)],
+        pieces,
+        *rows,
+    )
     w1, w2 = turn(weight, "x", X, 1), turn(weight, "x", X, -1)
     top, bottom = turn(w1[:HD], "x", X, 1), turn(w2[HD:], "x", X, -1)
-    mine, theirs = call(
-        cotangent_kernel, [((BLOCKS, FRAMES, HD), F32)] * 2, weight, *rows
-    )
     heads, own, edge = call(
         state_kernel,
         [((BLOCKS, 3, FRAMES, HD), BF), (state_shape, F32), ((Z - 1, HD, HD), BF)],

time: 128 us -> 126 us (0.984)
  local copies, waits for them, and re-layouts: 12.4 us -> 8.92 us
  waiting for transfers between devices: 31.8 us -> 34.2 us
    unnamed x39 -> x37, local copies, waits for them, and re-layouts: 9.93 us -> 7.24 us
    all_to_all x1, starting transfers between devices: 5.98 us -> 7.36 us  [body(): term = lax.all_to_all(gate(term, [r0]), ACROSS, 0, 0, tiled=True)]
    pallas_call x11 -> x10, Pallas kernels: 19 us -> 17.9 us  [call(): pl.pallas_call(run, out_shape=[jax.ShapeDtypeStruct(shape, dtype) for sha...]
  transfers between devices with their start and end apart: 22 -> 22, of which waited for: 9 -> 10; matrix products, arithmetic and copies ran while one was open for 3% -> 2% of each run, Pallas kernels for 7% -> 6%
where the time goes in v5:
time: 126 us
  starting transfers between devices  62.8 us (50%)
  waiting for transfers between devices  34.2 us (27%)
  Pallas kernels  17.9 us (14%)
  local copies, waits for them, and re-layouts  8.92 us (7%)
    ppermute x18, starting transfers between devices, turn(): lax.ppermute(value, axis, [(i, (i + shift) % size) for i in range(size)])  33.2 us
    ppermute x18, waiting for transfers between devices, turn(): lax.ppermute(value, axis, [(i, (i + shift) % size) for i in range(size)])  24 us
    pallas_call x10, Pallas kernels, call(): pl.pallas_call(run, out_shape=[jax.ShapeDtypeStruct(shape, dtype) for sha...  17.9 us
    all_to_all x1, waiting for transfers between devices, body(): lax.all_to_all(jnp.broadcast_to(moved[None], (group, ROWS, COLS)), ACROSS...  7.97 us
    ppermute x1, starting transfers between devices, body(): moved = lax.ppermute(out_weight, ALL, swap_pairs())  7.89 us
    all_to_all x1, starting transfers between devices, body(): lax.all_to_all(jnp.broadcast_to(moved[None], (group, ROWS, COLS)), ACROSS...  7.45 us
    all_to_all x1, starting transfers between devices, body(): term = lax.all_to_all(gate(term, [r0]), ACROSS, 0, 0, tiled=True)  7.36 us
    unnamed x37, local copies, waits for them, and re-layouts  7.24 us
  transfers between devices with their start and end apart: 22, of which 10 were waited for; matrix products, arithmetic and copies ran while one was open for 2% of the time, Pallas kernels for 6%

profile of v5, /device:TPU:1, one launch (start us, length us, event | category | flops | bytes accessed | tf_op | source)
XLA Modules:
  0.0 125.9 jit_solution(9545807082614474002)
XLA Ops:
  0.6 2.8 %shard_map.101 = (bf16[20,128,128]{2,1,0:T(8,128)(2,1)}, bf16[20,128,128]{2,1,0:T(8,128)(2,1)}) custom-call(bf16[1,128,1024]{2,1,0:T(8,128)(2,1)} %refs_0_.5, bf16[1,128,1024]{2,1,0:T(8,128)(2,1)} %refs_1_.1, bf16[1,128,1024]{2,1,0:T(8,128)(2,1)} %refs_2_.1, bf16[1,128,2048]{2,1,0:T(8,128)(2,1)} %refs_3_.1), custom_call_target="tpu_custom_call" | custom-call | tf_op jit(solution)/shard_map/pallas_call | solution.py:40
  3.4 3.3 %collective-permute-start = (bf16[20,128,128]{2,1,0:T(8,128)(2,1)}, bf16[20,128,128]{2,1,0:T(8,128)(2,1)S(1)}, u32[]{:S(2)}, u32[]{:S(2)}) collective-permute-start(bf16[20,128,128]{2,1,0:T(8,128)(2,1)} %get-tuple-element.34), channel_id=1, source_target_pairs={{0,1},{1,0},{2,3},{3,2},{4,5},{5,4},{6,7},{7,6},{8,9},{9,8},{10,11... | collective-permute-start | bytes 1966088 | tf_op jit(solution)/shard_map/ppermute | solution.py:388
  6.7 1.9 %collective-permute-done.refs_1_ = bf16[20,128,128]{2,1,0:T(8,128)(2,1)S(1)} collective-permute-done((bf16[20,128,128]{2,1,0:T(8,128)(2,1)}, bf16[20,128,128]{2,1,0:T(8,128)(2,1)S(1)}, u32[]{:S(2)}, u32[]{:S(2)}) %collective-permute-start) | collective-permute-done | bytes 655392 | tf_op jit(solution)/shard_map/ppermute | solution.py:388
  8.7 1.1 copy-done.13
  9.7 1.1 shard_map.102
  10.8 2.7 %collective-permute-start.2 = (bf16[25,128,128]{2,1,0:T(8,128)(2,1)S(1)}, bf16[25,128,128]{2,1,0:T(8,128)(2,1)S(1)}, u32[]{:S(2)}, u32[]{:S(2)}) collective-permute-start(bf16[25,128,128]{2,1,0:T(8,128)(2,1)S(1)} %get-tuple-element.37), channel_id=1, source_target_pairs={{0,6},{2,0},{4,2},{6,4},{1,7},{3,1},{5,3},{7,5},{8,14},{10,8},{12,... | collective-permute-start | bytes 2457608 | tf_op jit(solution)/shard_map/ppermute | solution.py:388
  13.5 7.9 %collective-permute-start.5 = (bf16[32,256]{1,0:T(8,128)(2,1)S(1)}, bf16[32,256]{1,0:T(8,128)(2,1)S(1)}, u32[]{:S(2)}, u32[]{:S(2)}) collective-permute-start(bf16[32,256]{1,0:T(8,128)(2,1)S(1)} %copy-done.17), channel_id=1, source_target_pairs={{0,0},{1,32},{2,8},{3,40},{4,16},{5,48},{6,24},{7,56},{8,2},{9,34}... | collective-permute-start | bytes 49160 | tf_op jit(solution)/shard_map/ppermute | solution.py:402
  21.4 1.4 %collective-permute-done.5 = bf16[32,256]{1,0:T(8,128)(2,1)S(1)} collective-permute-done((bf16[32,256]{1,0:T(8,128)(2,1)S(1)}, bf16[32,256]{1,0:T(8,128)(2,1)S(1)}, u32[]{:S(2)}, u32[]{:S(2)}) %collective-permute-start.5) | collective-permute-done | bytes 16416 | tf_op jit(solution)/shard_map/ppermute | solution.py:402
  23.7 7.4 %all-to-all-start = ((bf16[32,32,256]{2,1,0:T(8,128)(2,1)}), bf16[32,32,256]{2,1,0:T(8,128)(2,1)}, u32[]{:S(2)}, u32[]{:S(2)}) async-start(bf16[32,32,256]{2,1,0:T(8,128)(2,1)} %broadcast_in_dim.2), calls=%async_computation | async-start | bytes 1048576 | tf_op jit(solution)/shard_map/all_to_all | solution.py:403
  32.5 2.8 %collective-permute-start.4 = (bf16[11,128,128]{2,1,0:T(8,128)(2,1)S(1)}, bf16[11,128,128]{2,1,0:T(8,128)(2,1)S(1)}, u32[]{:S(2)}, u32[]{:S(2)}) collective-permute-start(bf16[11,128,128]{2,1,0:T(8,128)(2,1)S(1)} %slice.17), channel_id=1, source_target_pairs={{0,6},{2,0},{4,2},{6,4},{1,7},{3,1},{5,3},{7,5},{8,14},{10,8},{12,... | collective-permute-start | bytes 1081352 | tf_op jit(solution)/shard_map/ppermute | solution.py:388
  35.3 8.0 %all-to-all-done.refs_0_ = bf16[32,32,256]{2,1,0:T(8,128)(2,1)} async-done(((bf16[32,32,256]{2,1,0:T(8,128)(2,1)}), bf16[32,32,256]{2,1,0:T(8,128)(2,1)}, u32[]{:S(2)}, u32[]{:S(2)}) %all-to-all-start) | async-done | bytes 524320 | tf_op jit(solution)/shard_map/all_to_all | solution.py:403
  43.2 2.1 %shard_map.103 = (f32[8,128,128]{2,1,0:T(8,128)S(1)}, f32[8,128,128]{2,1,0:T(8,128)S(1)}, bf16[256,1024]{1,0:T(8,128)(2,1)S(1)}) custom-call(bf16[32,32,256]{2,1,0:T(8,128)(2,1)} %all-to-all-done.refs_0_, bf16[22,128,128]{2,1,0:T(8,128)(2,1)S(1)} %get-tuple-element.35.refs_1_.refs_2_, bf16[25,128,128]{2,1,0:T(8,128)(2,1)S(1)} %collective-permute-done.1.refs_2_.refs_3_, ...), custom_call_target="tpu_custom_call" | custom-call | tf_op jit(solution)/shard_map/pallas_call | solution.py:40
  45.4 5.6 %collective-permute-start.6 = (f32[8,128,128]{2,1,0:T(8,128)S(1)}, f32[8,128,128]{2,1,0:T(8,128)S(1)}, u32[]{:S(2)}, u32[]{:S(2)}) collective-permute-start(f32[8,128,128]{2,1,0:T(8,128)S(1)} %get-tuple-element.38.refs_6_), channel_id=1, source_target_pairs={{0,1},{1,0},{2,3},{3,2},{4,5},{5,4},{6,7},{7,6},{8,9},{9,8},{10,11... | collective-permute-start | bytes 1572872 | tf_op jit(solution)/shard_map/ppermute | solution.py:388
  51.0 3.1 %collective-permute-start.11 = (bf16[256,1024]{1,0:T(8,128)(2,1)S(1)}, bf16[256,1024]{1,0:T(8,128)(2,1)S(1)}, u32[]{:S(2)}, u32[]{:S(2)}) collective-permute-start(bf16[256,1024]{1,0:T(8,128)(2,1)S(1)} %get-tuple-element.47.refs_4_), channel_id=1, source_target_pairs={{0,6},{2,0},{4,2},{6,4},{1,7},{3,1},{5,3},{7,5},{8,14},{10,8},{12,... | collective-permute-start | bytes 1572872 | tf_op jit(solution)/shard_map/ppermute | solution.py:388
  56.1 1.7 %shard_map.104 = (bf16[8,3,128,128]{3,2,1,0:T(8,128)(2,1)S(1)}, f32[12,128,128]{2,1,0:T(8,128)S(1)}, bf16[3,128,128]{2,1,0:T(8,128)(2,1)S(1)}) custom-call(s32[1,12]{1,0:T(1,128)S(1)} %copy-done.16, bf16[22,128,128]{2,1,0:T(8,128)(2,1)S(1)} %get-tuple-element.35.refs_1_.refs_2_, bf16[25,128,128]{2,1,0:T(8,128)(2,1)S(1)} %collective-permute-done.1.refs_2_.refs_3_, ...), custom_call_target="tpu_custom_call" | custom-call | tf_op jit(solution)/shard_map/pallas_call | solution.py:40
  57.8 2.5 %shard_map.105 = (bf16[1024,128]{1,0:T(8,128)(2,1)S(1)}, f32[12,128,128]{2,1,0:T(8,128)S(1)}, bf16[2,128,128]{2,1,0:T(8,128)(2,1)S(1)}, bf16[2,128,128]{2,1,0:T(8,128)(2,1)S(1)}, bf16[2,128,128]{2,1,0:T(8,128)(2,1)S(1)}) custom-call(s32[1,12]{1,0:T(1,128)S(1)} %copy-done.16, bf16[8,3,128,128]{3,2,1,0:T(8,128)(2,1)S(1)} %get-tuple-element.39.refs_1_, ...), custom_call_target="tpu_custom_call" | custom-call | tf_op jit(solution)/shard_map/pallas_call | solution.py:40
  60.3 3.2 %collective-permute-start.7 = (bf16[2,128,128]{2,1,0:T(8,128)(2,1)S(1)}, bf16[2,128,128]{2,1,0:T(8,128)(2,1)S(1)}, u32[]{:S(2)}, u32[]{:S(2)}) collective-permute-start(bf16[2,128,128]{2,1,0:T(8,128)(2,1)S(1)} %get-tuple-element.44), channel_id=1, source_target_pairs={{0,8},{8,16},{16,24},{24,0},{1,9},{9,17},{17,25},{25,1},{2,10},{10... | collective-permute-start | bytes 196616 | tf_op jit(solution)/shard_map/ppermute | solution.py:388
  63.5 2.2 %collective-permute-start.9 = (bf16[2,128,128]{2,1,0:T(8,128)(2,1)S(1)}, bf16[2,128,128]{2,1,0:T(8,128)(2,1)S(1)}, u32[]{:S(2)}, u32[]{:S(2)}) collective-permute-start(bf16[2,128,128]{2,1,0:T(8,128)(2,1)S(1)} %get-tuple-element.46), channel_id=1, source_target_pairs={{0,24},{8,0},{16,8},{24,16},{1,25},{9,1},{17,9},{25,17},{2,26},{10... | collective-permute-start | bytes 196616 | tf_op jit(solution)/shard_map/ppermute | solution.py:388
  66.3 2.8 %collective-permute-done.8.refs_4_.refs_8_ = bf16[2,128,128]{2,1,0:T(8,128)(2,1)S(1)} collective-permute-done((bf16[2,128,128]{2,1,0:T(8,128)(2,1)S(1)}, bf16[2,128,128]{2,1,0:T(8,128)(2,1)S(1)}, u32[]{:S(2)}, u32[]{:S(2)}) %collective-permute-start.8) | collective-permute-done | bytes 65568 | tf_op jit(solution)/shard_map/ppermute | solution.py:388
  69.2 1.9 %shard_map.106 = (bf16[8,128,128]{2,1,0:T(8,128)(2,1)S(1)}, bf16[12,128,128]{2,1,0:T(8,128)(2,1)S(1)}) custom-call(s32[1,12]{1,0:T(1,128)S(1)} %copy-done.16, bf16[8,3,128,128]{3,2,1,0:T(8,128)(2,1)S(1)} %get-tuple-element.39.refs_1_, f32[12,128,128]{2,1,0:T(8,128)S(1)} %get-tuple-element.43.refs_2_, ...), custom_call_target="tpu_custom_call" | custom-call | tf_op jit(solution)/shard_map/pallas_call | solution.py:40
  71.1 1.6 %collective-permute-start.12 = (bf16[8,128,128]{2,1,0:T(8,128)(2,1)S(1)}, bf16[8,128,128]{2,1,0:T(8,128)(2,1)S(1)}, u32[]{:S(2)}, u32[]{:S(2)}) collective-permute-start(bf16[8,128,128]{2,1,0:T(8,128)(2,1)S(1)} %get-tuple-element.49.refs_4_.refs_0_), channel_id=1, source_target_pairs={{0,1},{1,0},{2,3},{3,2},{4,5},{5,4},{6,7},{7,6},{8,9},{9,8},{10,11... | collective-permute-start | bytes 786440 | tf_op jit(solution)/shard_map/ppermute | solution.py:388
  72.7 2.8 %collective-permute-start.14 = (bf16[128,1024]{1,0:T(8,128)(2,1)S(1)}, bf16[128,1024]{1,0:T(8,128)(2,1)S(1)}, u32[]{:S(2)}, u32[]{:S(2)}) collective-permute-start(bf16[128,1024]{1,0:T(8,128)(2,1)S(1)} %slice.19), channel_id=1, source_target_pairs={{0,6},{2,0},{4,2},{6,4},{1,7},{3,1},{5,3},{7,5},{8,14},{10,8},{12,... | collective-permute-start | bytes 786440 | tf_op jit(solution)/shard_map/ppermute | solution.py:388
  77.1 4.6 %collective-permute-done.13.refs_10_.refs_7_ = bf16[128,1024]{1,0:T(8,128)(2,1)S(1)} collective-permute-done((bf16[128,1024]{1,0:T(8,128)(2,1)S(1)}, bf16[128,1024]{1,0:T(8,128)(2,1)S(1)}, u32[]{:S(2)}, u32[]{:S(2)}) %collective-permute-start.13) | collective-permute-done | bytes 262176 | tf_op jit(solution)/shard_map/ppermute | solution.py:388
  81.7 2.9 %shard_map.107 = (bf16[2,5,128,128]{3,2,1,0:T(8,128)(2,1)S(1)}, bf16[2,5,128,128]{3,2,1,0:T(8,128)(2,1)S(1)}, bf16[2,5,128,128]{3,2,1,0:T(8,128)(2,1)S(1)}, bf16[2,5,128,128]{3,2,1,0:T(8,128)(2,1)S(1)}) custom-call(s32[1,12]{1,0:T(1,128)S(1)} %copy-done.16, bf16[8,3,128,128]{3,2,1,0:T(8,128)(2,1)S(1)} %get-tuple-element.39.refs_1_, ...), custom_call_target="tpu_custom_call" | custom-call | tf_op jit(solution)/shard_map/pallas_call | solution.py:40
  85.4 7.4 %all-to-all-start.1 = ((bf16[32,32,256]{2,1,0:T(8,128)(2,1)}), bf16[32,32,256]{2,1,0:T(8,128)(2,1)}, u32[]{:S(2)}, u32[]{:S(2)}) async-start(bf16[32,32,256]{2,1,0:T(8,128)(2,1)} %shard_map.111), calls=%async_computation.1 | async-start | bytes 1048576 | tf_op jit(solution)/shard_map/all_to_all | solution.py:490
  92.9 2.7 %collective-permute-start.16 = (bf16[2,5,128,128]{3,2,1,0:T(8,128)(2,1)S(1)}, bf16[2,5,128,128]{3,2,1,0:T(8,128)(2,1)S(1)}, u32[]{:S(2)}, u32[]{:S(2)}) collective-permute-start(bf16[2,5,128,128]{3,2,1,0:T(8,128)(2,1)S(1)} %get-tuple-element.53), channel_id=1, source_target_pairs={{0,6},{2,0},{4,2},{6,4},{1,7},{3,1},{5,3},{7,5},{8,14},{10,8},{12,... | collective-permute-start | bytes 983048 | tf_op jit(solution)/shard_map/ppermute | solution.py:388
  96.5 5.7 %collective-permute-done.15.refs_1_ = bf16[2,5,128,128]{3,2,1,0:T(8,128)(2,1)S(1)} collective-permute-done((bf16[2,5,128,128]{3,2,1,0:T(8,128)(2,1)S(1)}, bf16[2,5,128,128]{3,2,1,0:T(8,128)(2,1)S(1)}, u32[]{:S(2)}, u32[]{:S(2)}) %collective-permute-start.15) | collective-permute-done | bytes 327712 | tf_op jit(solution)/shard_map/ppermute | solution.py:388
  102.2 7.7 %collective-permute-done.17.refs_3_ = bf16[2,5,128,128]{3,2,1,0:T(8,128)(2,1)S(1)} collective-permute-done((bf16[2,5,128,128]{3,2,1,0:T(8,128)(2,1)S(1)}, bf16[2,5,128,128]{3,2,1,0:T(8,128)(2,1)S(1)}, u32[]{:S(2)}, u32[]{:S(2)}) %collective-permute-start.17) | collective-permute-done | bytes 327712 | tf_op jit(solution)/shard_map/ppermute | solution.py:388
  112.6 2.4 %collective-permute-start.18 = (bf16[20,128,128]{2,1,0:T(8,128)(2,1)S(1)}, bf16[20,128,128]{2,1,0:T(8,128)(2,1)S(1)}, u32[]{:S(2)}, u32[]{:S(2)}) collective-permute-start(bf16[20,128,128]{2,1,0:T(8,128)(2,1)S(1)} %get-tuple-element.56), channel_id=1, source_target_pairs={{0,1},{1,0},{2,3},{3,2},{4,5},{5,4},{6,7},{7,6},{8,9},{9,8},{10,11... | collective-permute-start | bytes 1966088 | tf_op jit(solution)/shard_map/ppermute | solution.py:388
  115.0 1.1 convert_reduce_fusion
  116.1 6.9 %collective-permute-start.19 = (f32[32,256]{1,0:T(8,128)S(1)}, f32[32,256]{1,0:T(8,128)S(1)}, u32[]{:S(2)}, u32[]{:S(2)}) collective-permute-start(f32[32,256]{1,0:T(8,128)S(1)} %broadcast_multiply_fusion), channel_id=1, source_target_pairs={{0,0},{1,32},{2,8},{3,40},{4,16},{5,48},{6,24},{7,56},{8,2},{9,34}... | collective-permute-start | bytes 98312 | tf_op jit(solution)/shard_map/ppermute | solution.py:492
  123.0 1.4 %shard_map.109 = (bf16[1,128,2048]{2,1,0:T(8,128)(2,1)}, bf16[1,128,1024]{2,1,0:T(8,128)(2,1)}, bf16[1,128,1024]{2,1,0:T(8,128)(2,1)}, bf16[1,128,1024]{2,1,0:T(8,128)(2,1)}) custom-call(bf16[20,128,128]{2,1,0:T(8,128)(2,1)S(1)} %get-tuple-element.55.refs_0_, bf16[20,128,128]{2,1,0:T(8,128)(2,1)S(1)} %collective-permute-done.18.refs_1_), custom_call_target="tpu_custom_call" | custom-call | tf_op jit(solution)/shard_map/pallas_call | solution.py:40
  (67 shorter events, 12.5 us)
Async XLA Ops:
  3.4 5.3 %collective-permute-start = (bf16[20,128,128]{2,1,0:T(8,128)(2,1)}, bf16[20,128,128]{2,1,0:T(8,128)(2,1)S(1)}, u32[]{:S(2)}, u32[]{:S(2)}) collective-permute-start(bf16[20,128,128]{2,1,0:T(8,128)(2,1)} %get-tuple-element.34), channel_id=1, source_target_pairs={{0,1},{1,0},{2,3},{3,2},{4,5},{5,4},{6,7},{7,6},{8,9},{9,8},{10,11... | collective-permute-start | bytes 1966088 | tf_op jit(solution)/shard_map/ppermute | solution.py:388
  9.7 3.8 %copy-start.17 = (bf16[32,256]{1,0:T(8,128)(2,1)S(1)}, bf16[32,256]{1,0:T(8,128)(2,1)}, u32[]{:S(2)}) copy-start(bf16[32,256]{1,0:T(8,128)(2,1)} %param.10) | copy-start | bytes 49156
  10.8 20.9 %collective-permute-start.1 = (bf16[25,128,128]{2,1,0:T(8,128)(2,1)}, bf16[25,128,128]{2,1,0:T(8,128)(2,1)S(1)}, u32[]{:S(2)}, u32[]{:S(2)}) collective-permute-start(bf16[25,128,128]{2,1,0:T(8,128)(2,1)} %get-tuple-element.36), channel_id=1, source_target_pairs={{0,2},{2,4},{4,6},{6,0},{1,3},{3,5},{5,7},{7,1},{8,10},{10,12},{12... | collective-permute-start | bytes 2457608 | tf_op jit(solution)/shard_map/ppermute | solution.py:388
  10.8 21.6 %collective-permute-start.2 = (bf16[25,128,128]{2,1,0:T(8,128)(2,1)S(1)}, bf16[25,128,128]{2,1,0:T(8,128)(2,1)S(1)}, u32[]{:S(2)}, u32[]{:S(2)}) collective-permute-start(bf16[25,128,128]{2,1,0:T(8,128)(2,1)S(1)} %get-tuple-element.37), channel_id=1, source_target_pairs={{0,6},{2,0},{4,2},{6,4},{1,7},{3,1},{5,3},{7,5},{8,14},{10,8},{12,... | collective-permute-start | bytes 2457608 | tf_op jit(solution)/shard_map/ppermute | solution.py:388
  13.5 9.3 %collective-permute-start.5 = (bf16[32,256]{1,0:T(8,128)(2,1)S(1)}, bf16[32,256]{1,0:T(8,128)(2,1)S(1)}, u32[]{:S(2)}, u32[]{:S(2)}) collective-permute-start(bf16[32,256]{1,0:T(8,128)(2,1)S(1)} %copy-done.17), channel_id=1, source_target_pairs={{0,0},{1,32},{2,8},{3,40},{4,16},{5,48},{6,24},{7,56},{8,2},{9,34}... | collective-permute-start | bytes 49160 | tf_op jit(solution)/shard_map/ppermute | solution.py:402
  23.7 19.6 %all-to-all-start = ((bf16[32,32,256]{2,1,0:T(8,128)(2,1)}), bf16[32,32,256]{2,1,0:T(8,128)(2,1)}, u32[]{:S(2)}, u32[]{:S(2)}) async-start(bf16[32,32,256]{2,1,0:T(8,128)(2,1)} %broadcast_in_dim.2), calls=%async_computation | async-start | bytes 1048576 | tf_op jit(solution)/shard_map/all_to_all | solution.py:403
  32.5 10.8 %collective-permute-start.3 = (bf16[11,128,128]{2,1,0:T(8,128)(2,1)}, bf16[11,128,128]{2,1,0:T(8,128)(2,1)S(1)}, u32[]{:S(2)}, u32[]{:S(2)}) collective-permute-start(bf16[11,128,128]{2,1,0:T(8,128)(2,1)} %slice.16), channel_id=1, source_target_pairs={{0,2},{2,4},{4,6},{6,0},{1,3},{3,5},{5,7},{7,1},{8,10},{10,12},{12... | collective-permute-start | bytes 1081352 | tf_op jit(solution)/shard_map/ppermute | solution.py:388
  32.5 10.7 %collective-permute-start.4 = (bf16[11,128,128]{2,1,0:T(8,128)(2,1)S(1)}, bf16[11,128,128]{2,1,0:T(8,128)(2,1)S(1)}, u32[]{:S(2)}, u32[]{:S(2)}) collective-permute-start(bf16[11,128,128]{2,1,0:T(8,128)(2,1)S(1)} %slice.17), channel_id=1, source_target_pairs={{0,6},{2,0},{4,2},{6,4},{1,7},{3,1},{5,3},{7,5},{8,14},{10,8},{12,... | collective-permute-start | bytes 1081352 | tf_op jit(solution)/shard_map/ppermute | solution.py:388
  43.2 2.1 %copy-start.4 = (bf16[11,128,128]{2,1,0:T(8,128)(2,1)}, bf16[11,128,128]{2,1,0:T(8,128)(2,1)S(1)}, u32[]{:S(2)}) copy-start(bf16[11,128,128]{2,1,0:T(8,128)(2,1)S(1)} %collective-permute-done.4.refs_5_.refs_6_) | copy-start | bytes 1081348
  45.3 12.5 %copy-start.14 = (bf16[256,1024]{1,0:T(8,128)(2,1)}, bf16[256,1024]{1,0:T(8,128)(2,1)S(1)}, u32[]{:S(2)}) copy-start(bf16[256,1024]{1,0:T(8,128)(2,1)S(1)} %get-tuple-element.47.refs_4_) | copy-start | bytes 1572868
  45.3 8.7 %copy-start.16 = (s32[1,12]{1,0:T(1,128)S(1)}, s32[1,12]{1,0:T(1,128)}, u32[]{:S(2)}) copy-start(s32[1,12]{1,0:T(1,128)} %refs_0_.9) | copy-start | bytes 148
  45.4 12.4 %collective-permute-start.6 = (f32[8,128,128]{2,1,0:T(8,128)S(1)}, f32[8,128,128]{2,1,0:T(8,128)S(1)}, u32[]{:S(2)}, u32[]{:S(2)}) collective-permute-start(f32[8,128,128]{2,1,0:T(8,128)S(1)} %get-tuple-element.38.refs_6_), channel_id=1, source_target_pairs={{0,1},{1,0},{2,3},{3,2},{4,5},{5,4},{6,7},{7,6},{8,9},{9,8},{10,11... | collective-permute-start | bytes 1572872 | tf_op jit(solution)/shard_map/ppermute | solution.py:388
  51.0 15.3 %collective-permute-start.10 = (bf16[256,1024]{1,0:T(8,128)(2,1)S(1)}, bf16[256,1024]{1,0:T(8,128)(2,1)S(1)}, u32[]{:S(2)}, u32[]{:S(2)}) collective-permute-start(bf16[256,1024]{1,0:T(8,128)(2,1)S(1)} %get-tuple-element.47.refs_4_), channel_id=1, source_target_pairs={{0,2},{2,4},{4,6},{6,0},{1,3},{3,5},{5,7},{7,1},{8,10},{10,12},{12... | collective-permute-start | bytes 1572872 | tf_op jit(solution)/shard_map/ppermute | solution.py:388
  51.0 15.3 %collective-permute-start.11 = (bf16[256,1024]{1,0:T(8,128)(2,1)S(1)}, bf16[256,1024]{1,0:T(8,128)(2,1)S(1)}, u32[]{:S(2)}, u32[]{:S(2)}) collective-permute-start(bf16[256,1024]{1,0:T(8,128)(2,1)S(1)} %get-tuple-element.47.refs_4_), channel_id=1, source_target_pairs={{0,6},{2,0},{4,2},{6,4},{1,7},{3,1},{5,3},{7,5},{8,14},{10,8},{12,... | collective-permute-start | bytes 1572872 | tf_op jit(solution)/shard_map/ppermute | solution.py:388
  60.3 6.0 %collective-permute-start.7 = (bf16[2,128,128]{2,1,0:T(8,128)(2,1)S(1)}, bf16[2,128,128]{2,1,0:T(8,128)(2,1)S(1)}, u32[]{:S(2)}, u32[]{:S(2)}) collective-permute-start(bf16[2,128,128]{2,1,0:T(8,128)(2,1)S(1)} %get-tuple-element.44), channel_id=1, source_target_pairs={{0,8},{8,16},{16,24},{24,0},{1,9},{9,17},{17,25},{25,1},{2,10},{10... | collective-permute-start | bytes 196616 | tf_op jit(solution)/shard_map/ppermute | solution.py:388
  63.5 5.7 %collective-permute-start.8 = (bf16[2,128,128]{2,1,0:T(8,128)(2,1)S(1)}, bf16[2,128,128]{2,1,0:T(8,128)(2,1)S(1)}, u32[]{:S(2)}, u32[]{:S(2)}) collective-permute-start(bf16[2,128,128]{2,1,0:T(8,128)(2,1)S(1)} %get-tuple-element.45), channel_id=1, source_target_pairs={{0,16},{8,24},{16,0},{24,8},{1,17},{9,25},{17,1},{25,9},{2,18},{10... | collective-permute-start | bytes 196616 | tf_op jit(solution)/shard_map/ppermute | solution.py:388
  63.5 5.7 %collective-permute-start.9 = (bf16[2,128,128]{2,1,0:T(8,128)(2,1)S(1)}, bf16[2,128,128]{2,1,0:T(8,128)(2,1)S(1)}, u32[]{:S(2)}, u32[]{:S(2)}) collective-permute-start(bf16[2,128,128]{2,1,0:T(8,128)(2,1)S(1)} %get-tuple-element.46), channel_id=1, source_target_pairs={{0,24},{8,0},{16,8},{24,16},{1,25},{9,1},{17,9},{25,17},{2,26},{10... | collective-permute-start | bytes 196616 | tf_op jit(solution)/shard_map/ppermute | solution.py:388
  69.2 6.3 %copy-start.6 = (bf16[11,128,128]{2,1,0:T(8,128)(2,1)S(1)}, bf16[11,128,128]{2,1,0:T(8,128)(2,1)}, u32[]{:S(2)}) copy-start(bf16[11,128,128]{2,1,0:T(8,128)(2,1)} %copy-done.4) | copy-start | bytes 1081348
  71.1 4.4 %copy-start.3 = (bf16[11,128,128]{2,1,0:T(8,128)(2,1)S(1)}, bf16[11,128,128]{2,1,0:T(8,128)(2,1)}, u32[]{:S(2)}) copy-start(bf16[11,128,128]{2,1,0:T(8,128)(2,1)} %copy-done.1) | copy-start | bytes 1081348
  71.1 4.4 %collective-permute-start.12 = (bf16[8,128,128]{2,1,0:T(8,128)(2,1)S(1)}, bf16[8,128,128]{2,1,0:T(8,128)(2,1)S(1)}, u32[]{:S(2)}, u32[]{:S(2)}) collective-permute-start(bf16[8,128,128]{2,1,0:T(8,128)(2,1)S(1)} %get-tuple-element.49.refs_4_.refs_0_), channel_id=1, source_target_pairs={{0,1},{1,0},{2,3},{3,2},{4,5},{5,4},{6,7},{7,6},{8,9},{9,8},{10,11... | collective-permute-start | bytes 786440 | tf_op jit(solution)/shard_map/ppermute | solution.py:388
  72.6 9.1 %collective-permute-start.13 = (bf16[128,1024]{1,0:T(8,128)(2,1)S(1)}, bf16[128,1024]{1,0:T(8,128)(2,1)S(1)}, u32[]{:S(2)}, u32[]{:S(2)}) collective-permute-start(bf16[128,1024]{1,0:T(8,128)(2,1)S(1)} %slice.18), channel_id=1, source_target_pairs={{0,2},{2,4},{4,6},{6,0},{1,3},{3,5},{5,7},{7,1},{8,10},{10,12},{12... | collective-permute-start | bytes 786440 | tf_op jit(solution)/shard_map/ppermute | solution.py:388
  72.7 9.1 %collective-permute-start.14 = (bf16[128,1024]{1,0:T(8,128)(2,1)S(1)}, bf16[128,1024]{1,0:T(8,128)(2,1)S(1)}, u32[]{:S(2)}, u32[]{:S(2)}) collective-permute-start(bf16[128,1024]{1,0:T(8,128)(2,1)S(1)} %slice.19), channel_id=1, source_target_pairs={{0,6},{2,0},{4,2},{6,4},{1,7},{3,1},{5,3},{7,5},{8,14},{10,8},{12,... | collective-permute-start | bytes 786440 | tf_op jit(solution)/shard_map/ppermute | solution.py:388
  81.7 3.0 %copy-start.9 = (bf16[128,1024]{1,0:T(8,128)(2,1)}, bf16[128,1024]{1,0:T(8,128)(2,1)S(1)}, u32[]{:S(2)}) copy-start(bf16[128,1024]{1,0:T(8,128)(2,1)S(1)} %collective-permute-done.13.refs_10_.refs_7_) | copy-start | bytes 786436
  81.7 3.0 %copy-start.11 = (bf16[128,1024]{1,0:T(8,128)(2,1)}, bf16[128,1024]{1,0:T(8,128)(2,1)S(1)}, u32[]{:S(2)}) copy-start(bf16[128,1024]{1,0:T(8,128)(2,1)S(1)} %collective-permute-done.14.refs_11_.refs_8_) | copy-start | bytes 786436
  85.4 24.5 %copy-start.8 = (bf16[2,5,128,128]{3,2,1,0:T(8,128)(2,1)S(1)}, bf16[2,5,128,128]{3,2,1,0:T(8,128)(2,1)}, u32[]{:S(2)}) copy-start(bf16[2,5,128,128]{3,2,1,0:T(8,128)(2,1)} %copy-done.7) | copy-start | bytes 983044
  85.4 24.5 %copy-start.10 = (bf16[128,1024]{1,0:T(8,128)(2,1)S(1)}, bf16[128,1024]{1,0:T(8,128)(2,1)}, u32[]{:S(2)}) copy-start(bf16[128,1024]{1,0:T(8,128)(2,1)} %copy-done.9) | copy-start | bytes 786436
  85.4 29.6 %all-to-all-start.1 = ((bf16[32,32,256]{2,1,0:T(8,128)(2,1)}), bf16[32,32,256]{2,1,0:T(8,128)(2,1)}, u32[]{:S(2)}, u32[]{:S(2)}) async-start(bf16[32,32,256]{2,1,0:T(8,128)(2,1)} %shard_map.111), calls=%async_computation.1 | async-start | bytes 1048576 | tf_op jit(solution)/shard_map/all_to_all | solution.py:490
  92.8 9.4 %collective-permute-start.15 = (bf16[2,5,128,128]{3,2,1,0:T(8,128)(2,1)S(1)}, bf16[2,5,128,128]{3,2,1,0:T(8,128)(2,1)S(1)}, u32[]{:S(2)}, u32[]{:S(2)}) collective-permute-start(bf16[2,5,128,128]{3,2,1,0:T(8,128)(2,1)S(1)} %get-tuple-element.52), channel_id=1, source_target_pairs={{0,2},{2,4},{4,6},{6,0},{1,3},{3,5},{5,7},{7,1},{8,10},{10,12},{12... | collective-permute-start | bytes 983048 | tf_op jit(solution)/shard_map/ppermute | solution.py:388
  92.9 9.4 %collective-permute-start.16 = (bf16[2,5,128,128]{3,2,1,0:T(8,128)(2,1)S(1)}, bf16[2,5,128,128]{3,2,1,0:T(8,128)(2,1)S(1)}, u32[]{:S(2)}, u32[]{:S(2)}) collective-permute-start(bf16[2,5,128,128]{3,2,1,0:T(8,128)(2,1)S(1)} %get-tuple-element.53), channel_id=1, source_target_pairs={{0,6},{2,0},{4,2},{6,4},{1,7},{3,1},{5,3},{7,5},{8,14},{10,8},{12,... | collective-permute-start | bytes 983048 | tf_op jit(solution)/shard_map/ppermute | solution.py:388
  95.5 14.4 %collective-permute-start.17 = (bf16[2,5,128,128]{3,2,1,0:T(8,128)(2,1)S(1)}, bf16[2,5,128,128]{3,2,1,0:T(8,128)(2,1)S(1)}, u32[]{:S(2)}, u32[]{:S(2)}) collective-permute-start(bf16[2,5,128,128]{3,2,1,0:T(8,128)(2,1)S(1)} %get-tuple-element.54), channel_id=1, source_target_pairs={{0,4},{2,6},{4,0},{6,2},{1,5},{3,7},{5,1},{7,3},{8,12},{10,14},{12... | collective-permute-start | bytes 983048 | tf_op jit(solution)/shard_map/ppermute | solution.py:388
  112.6 10.4 %collective-permute-start.18 = (bf16[20,128,128]{2,1,0:T(8,128)(2,1)S(1)}, bf16[20,128,128]{2,1,0:T(8,128)(2,1)S(1)}, u32[]{:S(2)}, u32[]{:S(2)}) collective-permute-start(bf16[20,128,128]{2,1,0:T(8,128)(2,1)S(1)} %get-tuple-element.56), channel_id=1, source_target_pairs={{0,1},{1,0},{2,3},{3,2},{4,5},{5,4},{6,7},{7,6},{8,9},{9,8},{10,11... | collective-permute-start | bytes 1966088 | tf_op jit(solution)/shard_map/ppermute | solution.py:388
  116.1 9.2 %collective-permute-start.19 = (f32[32,256]{1,0:T(8,128)S(1)}, f32[32,256]{1,0:T(8,128)S(1)}, u32[]{:S(2)}, u32[]{:S(2)}) collective-permute-start(f32[32,256]{1,0:T(8,128)S(1)} %broadcast_multiply_fusion), channel_id=1, source_target_pairs={{0,0},{1,32},{2,8},{3,40},{4,16},{5,48},{6,24},{7,56},{8,2},{9,34}... | collective-permute-start | bytes 98312 | tf_op jit(solution)/shard_map/ppermute | solution.py:492
  (8 other events, 8.7 us)

commit v6 on v5

--- a/solution.py
+++ b/solution.py
@@ -476,7 +476,6 @@
         *edges,
         scratch=[chunk_scratch] * 3,
         smem=1,
-        after=[top, bottom],
     )
     (term,) = call(
         weight_kernel,
@@ -487,7 +486,7 @@
         scratch=[pltpu.VMEM((BLOCKS, C, FRAMES, HD), BF)],
     )
     h1, h2, h3 = turn(h1, "x", X, 1), turn(h2, "x", X, 2), turn(h3, "x", X, -1)
-    term = lax.all_to_all(gate(term, [r0]), ACROSS, 0, 0, tiled=True)
+    term = lax.all_to_all(gate(term, [r0, top, bottom]), ACROSS, 0, 0, tiled=True)
     grad_weight = jnp.sum(term.astype(F32), axis=0) / math.sqrt(Y * H * LENGTH)
     grad_weight = lax.ppermute(grad_weight, ALL, swap_pairs())
 

time: 126 us -> 120 us (0.952)
  waiting for transfers between devices: 34.2 us -> 29.4 us
    ppermute x18, waiting for transfers between devices: 24 us -> 19.1 us  [turn(): lax.ppermute(value, axis, [(i, (i + shift) % size) for i in range(size)])]
    ppermute x18, starting transfers between devices: 33.2 us -> 34.5 us  [turn(): lax.ppermute(value, axis, [(i, (i + shift) % size) for i in range(size)])]
    unnamed x37 -> x29, local copies, waits for them, and re-layouts: 7.24 us -> 6.28 us
  transfers between devices with their start and end apart: 22 -> 22, of which waited for: 10 -> 11; matrix products, arithmetic and copies ran while one was open for 2% -> 2% of each run, Pallas kernels for 6% -> 8%
where the time goes in v6:
time: 120 us
  starting transfers between devices  62.9 us (52%)
  waiting for transfers between devices  29.4 us (24%)
  Pallas kernels  17.6 us (15%)
  local copies, waits for them, and re-layouts  7.95 us (7%)
    ppermute x18, starting transfers between devices, turn(): lax.ppermute(value, axis, [(i, (i + shift) % size) for i in range(size)])  34.5 us
    ppermute x18, waiting for transfers between devices, turn(): lax.ppermute(value, axis, [(i, (i + shift) % size) for i in range(size)])  19.1 us
    pallas_call x10, Pallas kernels, call(): pl.pallas_call(run, out_shape=[jax.ShapeDtypeStruct(shape, dtype) for sha...  17.6 us
    all_to_all x1, waiting for transfers between devices, body(): lax.all_to_all(jnp.broadcast_to(moved[None], (group, ROWS, COLS)), ACROSS...  7.98 us
    ppermute x1, starting transfers between devices, body(): moved = lax.ppermute(out_weight, ALL, swap_pairs())  7.89 us
    all_to_all x1, starting transfers between devices, body(): lax.all_to_all(jnp.broadcast_to(moved[None], (group, ROWS, COLS)), ACROSS...  7.45 us
    ppermute x1, starting transfers between devices, body(): grad_weight = lax.ppermute(grad_weight, ALL, swap_pairs())  6.88 us
    unnamed x29, local copies, waits for them, and re-layouts  6.28 us
  transfers between devices with their start and end apart: 22, of which 11 were waited for; matrix products, arithmetic and copies ran while one was open for 2% of the time, Pallas kernels for 8%

profile of v6, /device:TPU:1, one launch (start us, length us, event | category | flops | bytes accessed | tf_op | source)
XLA Modules:
  0.0 119.8 jit_solution(4108490764421181742)
XLA Ops:
  0.6 2.7 %shard_map.101 = (bf16[20,128,128]{2,1,0:T(8,128)(2,1)}, bf16[20,128,128]{2,1,0:T(8,128)(2,1)}) custom-call(bf16[1,128,1024]{2,1,0:T(8,128)(2,1)} %refs_0_.5, bf16[1,128,1024]{2,1,0:T(8,128)(2,1)} %refs_1_.1, bf16[1,128,1024]{2,1,0:T(8,128)(2,1)} %refs_2_.1, bf16[1,128,2048]{2,1,0:T(8,128)(2,1)} %refs_3_.1), custom_call_target="tpu_custom_call" | custom-call | tf_op jit(solution)/shard_map/pallas_call | solution.py:40
  3.4 3.3 %collective-permute-start = (bf16[20,128,128]{2,1,0:T(8,128)(2,1)}, bf16[20,128,128]{2,1,0:T(8,128)(2,1)S(1)}, u32[]{:S(2)}, u32[]{:S(2)}) collective-permute-start(bf16[20,128,128]{2,1,0:T(8,128)(2,1)} %get-tuple-element.34), channel_id=1, source_target_pairs={{0,1},{1,0},{2,3},{3,2},{4,5},{5,4},{6,7},{7,6},{8,9},{9,8},{10,11... | collective-permute-start | bytes 1966088 | tf_op jit(solution)/shard_map/ppermute | solution.py:388
  6.7 1.9 %collective-permute-done.refs_1_ = bf16[20,128,128]{2,1,0:T(8,128)(2,1)S(1)} collective-permute-done((bf16[20,128,128]{2,1,0:T(8,128)(2,1)}, bf16[20,128,128]{2,1,0:T(8,128)(2,1)S(1)}, u32[]{:S(2)}, u32[]{:S(2)}) %collective-permute-start) | collective-permute-done | bytes 655392 | tf_op jit(solution)/shard_map/ppermute | solution.py:388
  10.8 2.7 %collective-permute-start.2 = (bf16[25,128,128]{2,1,0:T(8,128)(2,1)S(1)}, bf16[25,128,128]{2,1,0:T(8,128)(2,1)S(1)}, u32[]{:S(2)}, u32[]{:S(2)}) collective-permute-start(bf16[25,128,128]{2,1,0:T(8,128)(2,1)S(1)} %get-tuple-element.37), channel_id=1, source_target_pairs={{0,6},{2,0},{4,2},{6,4},{1,7},{3,1},{5,3},{7,5},{8,14},{10,8},{12,... | collective-permute-start | bytes 2457608 | tf_op jit(solution)/shard_map/ppermute | solution.py:388
  13.5 7.9 %collective-permute-start.5 = (bf16[32,256]{1,0:T(8,128)(2,1)S(1)}, bf16[32,256]{1,0:T(8,128)(2,1)S(1)}, u32[]{:S(2)}, u32[]{:S(2)}) collective-permute-start(bf16[32,256]{1,0:T(8,128)(2,1)S(1)} %copy-done.13), channel_id=1, source_target_pairs={{0,0},{1,32},{2,8},{3,40},{4,16},{5,48},{6,24},{7,56},{8,2},{9,34}... | collective-permute-start | bytes 49160 | tf_op jit(solution)/shard_map/ppermute | solution.py:402
  21.4 1.4 %collective-permute-done.5 = bf16[32,256]{1,0:T(8,128)(2,1)S(1)} collective-permute-done((bf16[32,256]{1,0:T(8,128)(2,1)S(1)}, bf16[32,256]{1,0:T(8,128)(2,1)S(1)}, u32[]{:S(2)}, u32[]{:S(2)}) %collective-permute-start.5) | collective-permute-done | bytes 16416 | tf_op jit(solution)/shard_map/ppermute | solution.py:402
  23.6 7.4 %all-to-all-start = ((bf16[32,32,256]{2,1,0:T(8,128)(2,1)}), bf16[32,32,256]{2,1,0:T(8,128)(2,1)}, u32[]{:S(2)}, u32[]{:S(2)}) async-start(bf16[32,32,256]{2,1,0:T(8,128)(2,1)} %broadcast_in_dim.2), calls=%async_computation | async-start | bytes 1048576 | tf_op jit(solution)/shard_map/all_to_all | solution.py:403
  32.5 2.8 %collective-permute-start.4 = (bf16[11,128,128]{2,1,0:T(8,128)(2,1)S(1)}, bf16[11,128,128]{2,1,0:T(8,128)(2,1)S(1)}, u32[]{:S(2)}, u32[]{:S(2)}) collective-permute-start(bf16[11,128,128]{2,1,0:T(8,128)(2,1)S(1)} %slice.17), channel_id=1, source_target_pairs={{0,6},{2,0},{4,2},{6,4},{1,7},{3,1},{5,3},{7,5},{8,14},{10,8},{12,... | collective-permute-start | bytes 1081352 | tf_op jit(solution)/shard_map/ppermute | solution.py:388
  35.2 8.0 %all-to-all-done.refs_0_ = bf16[32,32,256]{2,1,0:T(8,128)(2,1)} async-done(((bf16[32,32,256]{2,1,0:T(8,128)(2,1)}), bf16[32,32,256]{2,1,0:T(8,128)(2,1)}, u32[]{:S(2)}, u32[]{:S(2)}) %all-to-all-start) | async-done | bytes 524320 | tf_op jit(solution)/shard_map/all_to_all | solution.py:403
  43.2 2.1 %shard_map.103 = (f32[8,128,128]{2,1,0:T(8,128)S(1)}, f32[8,128,128]{2,1,0:T(8,128)S(1)}, bf16[256,1024]{1,0:T(8,128)(2,1)S(1)}) custom-call(bf16[32,32,256]{2,1,0:T(8,128)(2,1)} %all-to-all-done.refs_0_, bf16[22,128,128]{2,1,0:T(8,128)(2,1)S(1)} %get-tuple-element.35.refs_1_.refs_2_, bf16[25,128,128]{2,1,0:T(8,128)(2,1)S(1)} %collective-permute-done.1.refs_2_.refs_3_, ...), custom_call_target="tpu_custom_call" | custom-call | tf_op jit(solution)/shard_map/pallas_call | solution.py:40
  45.3 5.6 %collective-permute-start.6 = (f32[8,128,128]{2,1,0:T(8,128)S(1)}, f32[8,128,128]{2,1,0:T(8,128)S(1)}, u32[]{:S(2)}, u32[]{:S(2)}) collective-permute-start(f32[8,128,128]{2,1,0:T(8,128)S(1)} %get-tuple-element.38.refs_6_), channel_id=1, source_target_pairs={{0,1},{1,0},{2,3},{3,2},{4,5},{5,4},{6,7},{7,6},{8,9},{9,8},{10,11... | collective-permute-start | bytes 1572872 | tf_op jit(solution)/shard_map/ppermute | solution.py:388
  50.9 3.1 %collective-permute-start.11 = (bf16[256,1024]{1,0:T(8,128)(2,1)S(1)}, bf16[256,1024]{1,0:T(8,128)(2,1)S(1)}, u32[]{:S(2)}, u32[]{:S(2)}) collective-permute-start(bf16[256,1024]{1,0:T(8,128)(2,1)S(1)} %get-tuple-element.47.refs_4_), channel_id=1, source_target_pairs={{0,6},{2,0},{4,2},{6,4},{1,7},{3,1},{5,3},{7,5},{8,14},{10,8},{12,... | collective-permute-start | bytes 1572872 | tf_op jit(solution)/shard_map/ppermute | solution.py:388
  56.0 1.5 %shard_map.104 = (bf16[8,3,128,128]{3,2,1,0:T(8,128)(2,1)S(1)}, f32[12,128,128]{2,1,0:T(8,128)S(1)}, bf16[3,128,128]{2,1,0:T(8,128)(2,1)S(1)}) custom-call(s32[1,12]{1,0:T(1,128)S(1)} %copy-done.12, bf16[22,128,128]{2,1,0:T(8,128)(2,1)S(1)} %get-tuple-element.35.refs_1_.refs_2_, bf16[25,128,128]{2,1,0:T(8,128)(2,1)S(1)} %collective-permute-done.1.refs_2_.refs_3_, ...), custom_call_target="tpu_custom_call" | custom-call | tf_op jit(solution)/shard_map/pallas_call | solution.py:40
  57.6 2.2 %shard_map.105 = (bf16[1024,128]{1,0:T(8,128)(2,1)S(1)}, f32[12,128,128]{2,1,0:T(8,128)S(1)}, bf16[2,128,128]{2,1,0:T(8,128)(2,1)S(1)}, bf16[2,128,128]{2,1,0:T(8,128)(2,1)S(1)}, bf16[2,128,128]{2,1,0:T(8,128)(2,1)S(1)}) custom-call(s32[1,12]{1,0:T(1,128)S(1)} %copy-done.12, bf16[8,3,128,128]{3,2,1,0:T(8,128)(2,1)S(1)} %get-tuple-element.39.refs_1_, ...), custom_call_target="tpu_custom_call" | custom-call | tf_op jit(solution)/shard_map/pallas_call | solution.py:40
  59.7 2.1 %collective-permute-start.7 = (bf16[2,128,128]{2,1,0:T(8,128)(2,1)S(1)}, bf16[2,128,128]{2,1,0:T(8,128)(2,1)S(1)}, u32[]{:S(2)}, u32[]{:S(2)}) collective-permute-start(bf16[2,128,128]{2,1,0:T(8,128)(2,1)S(1)} %get-tuple-element.44), channel_id=1, source_target_pairs={{0,8},{8,16},{16,24},{24,0},{1,9},{9,17},{17,25},{25,1},{2,10},{10... | collective-permute-start | bytes 196616 | tf_op jit(solution)/shard_map/ppermute | solution.py:388
  61.8 2.0 %collective-permute-start.8 = (bf16[2,128,128]{2,1,0:T(8,128)(2,1)S(1)}, bf16[2,128,128]{2,1,0:T(8,128)(2,1)S(1)}, u32[]{:S(2)}, u32[]{:S(2)}) collective-permute-start(bf16[2,128,128]{2,1,0:T(8,128)(2,1)S(1)} %get-tuple-element.45), channel_id=1, source_target_pairs={{0,16},{8,24},{16,0},{24,8},{1,17},{9,25},{17,1},{25,9},{2,18},{10... | collective-permute-start | bytes 196616 | tf_op jit(solution)/shard_map/ppermute | solution.py:388
  63.8 2.3 %collective-permute-start.9 = (bf16[2,128,128]{2,1,0:T(8,128)(2,1)S(1)}, bf16[2,128,128]{2,1,0:T(8,128)(2,1)S(1)}, u32[]{:S(2)}, u32[]{:S(2)}) collective-permute-start(bf16[2,128,128]{2,1,0:T(8,128)(2,1)S(1)} %get-tuple-element.46), channel_id=1, source_target_pairs={{0,24},{8,0},{16,8},{24,16},{1,25},{9,1},{17,9},{25,17},{2,26},{10... | collective-permute-start | bytes 196616 | tf_op jit(solution)/shard_map/ppermute | solution.py:388
  66.5 1.1 collective-permute-done.9.refs_5_.refs_9_
  67.6 1.6 %shard_map.106 = (bf16[8,128,128]{2,1,0:T(8,128)(2,1)S(1)}, bf16[12,128,128]{2,1,0:T(8,128)(2,1)S(1)}) custom-call(s32[1,12]{1,0:T(1,128)S(1)} %copy-done.12, bf16[8,3,128,128]{3,2,1,0:T(8,128)(2,1)S(1)} %get-tuple-element.39.refs_1_, f32[12,128,128]{2,1,0:T(8,128)S(1)} %get-tuple-element.43.refs_2_, ...), custom_call_target="tpu_custom_call" | custom-call | tf_op jit(solution)/shard_map/pallas_call | solution.py:40
  69.2 1.9 %collective-permute-start.12 = (bf16[8,128,128]{2,1,0:T(8,128)(2,1)S(1)}, bf16[8,128,128]{2,1,0:T(8,128)(2,1)S(1)}, u32[]{:S(2)}, u32[]{:S(2)}) collective-permute-start(bf16[8,128,128]{2,1,0:T(8,128)(2,1)S(1)} %get-tuple-element.49.refs_4_.refs_0_), channel_id=1, source_target_pairs={{0,1},{1,0},{2,3},{3,2},{4,5},{5,4},{6,7},{7,6},{8,9},{9,8},{10,11... | collective-permute-start | bytes 786440 | tf_op jit(solution)/shard_map/ppermute | solution.py:388
  71.3 2.7 %collective-permute-start.17 = (bf16[128,1024]{1,0:T(8,128)(2,1)S(1)}, bf16[128,1024]{1,0:T(8,128)(2,1)}, u32[]{:S(2)}, u32[]{:S(2)}) collective-permute-start(bf16[128,1024]{1,0:T(8,128)(2,1)S(1)} %slice.19), channel_id=1, source_target_pairs={{0,6},{2,0},{4,2},{6,4},{1,7},{3,1},{5,3},{7,5},{8,14},{10,8},{12,... | collective-permute-start | bytes 786440 | tf_op jit(solution)/shard_map/ppermute | solution.py:388
  75.7 2.5 %shard_map.107 = (bf16[2,5,128,128]{3,2,1,0:T(8,128)(2,1)S(1)}, bf16[2,5,128,128]{3,2,1,0:T(8,128)(2,1)S(1)}, bf16[2,5,128,128]{3,2,1,0:T(8,128)(2,1)S(1)}, bf16[2,5,128,128]{3,2,1,0:T(8,128)(2,1)S(1)}) custom-call(s32[1,12]{1,0:T(1,128)S(1)} %copy-done.12, bf16[8,3,128,128]{3,2,1,0:T(8,128)(2,1)S(1)} %get-tuple-element.39.refs_1_, ...), custom_call_target="tpu_custom_call" | custom-call | tf_op jit(solution)/shard_map/pallas_call | solution.py:40
  78.9 1.6 %collective-permute-done.16.refs_7_.refs_2_ = bf16[128,1024]{1,0:T(8,128)(2,1)} collective-permute-done((bf16[128,1024]{1,0:T(8,128)(2,1)S(1)}, bf16[128,1024]{1,0:T(8,128)(2,1)}, u32[]{:S(2)}, u32[]{:S(2)}) %collective-permute-start.16) | collective-permute-done | bytes 262176 | tf_op jit(solution)/shard_map/ppermute | solution.py:388
  80.5 6.1 %all-to-all-start.1 = ((bf16[32,32,256]{2,1,0:T(8,128)(2,1)}), bf16[32,32,256]{2,1,0:T(8,128)(2,1)}, u32[]{:S(2)}, u32[]{:S(2)}) async-start(bf16[32,32,256]{2,1,0:T(8,128)(2,1)} %shard_map.111), calls=%async_computation.1 | async-start | bytes 1048576 | tf_op jit(solution)/shard_map/all_to_all | solution.py:489
  86.7 2.7 %collective-permute-start.14 = (bf16[2,5,128,128]{3,2,1,0:T(8,128)(2,1)S(1)}, bf16[2,5,128,128]{3,2,1,0:T(8,128)(2,1)S(1)}, u32[]{:S(2)}, u32[]{:S(2)}) collective-permute-start(bf16[2,5,128,128]{3,2,1,0:T(8,128)(2,1)S(1)} %get-tuple-element.53), channel_id=1, source_target_pairs={{0,6},{2,0},{4,2},{6,4},{1,7},{3,1},{5,3},{7,5},{8,14},{10,8},{12,... | collective-permute-start | bytes 983048 | tf_op jit(solution)/shard_map/ppermute | solution.py:388
  90.3 5.8 %collective-permute-done.13.refs_1_ = bf16[2,5,128,128]{3,2,1,0:T(8,128)(2,1)S(1)} collective-permute-done((bf16[2,5,128,128]{3,2,1,0:T(8,128)(2,1)S(1)}, bf16[2,5,128,128]{3,2,1,0:T(8,128)(2,1)S(1)}, u32[]{:S(2)}, u32[]{:S(2)}) %collective-permute-start.13) | collective-permute-done | bytes 327712 | tf_op jit(solution)/shard_map/ppermute | solution.py:388
  96.2 7.6 %collective-permute-done.15.refs_3_ = bf16[2,5,128,128]{3,2,1,0:T(8,128)(2,1)S(1)} collective-permute-done((bf16[2,5,128,128]{3,2,1,0:T(8,128)(2,1)S(1)}, bf16[2,5,128,128]{3,2,1,0:T(8,128)(2,1)S(1)}, u32[]{:S(2)}, u32[]{:S(2)}) %collective-permute-start.15) | collective-permute-done | bytes 327712 | tf_op jit(solution)/shard_map/ppermute | solution.py:388
  104.8 1.7 %shard_map.108 = (bf16[20,128,128]{2,1,0:T(8,128)(2,1)S(1)}, bf16[20,128,128]{2,1,0:T(8,128)(2,1)S(1)}) custom-call(bf16[2,5,128,128]{3,2,1,0:T(8,128)(2,1)S(1)} %copy-done.8, bf16[2,5,128,128]{3,2,1,0:T(8,128)(2,1)S(1)} %collective-permute-done.13.refs_1_, bf16[2,5,128,128]{3,2,1,0:T(8,128)(2,1)S(1)} %collective-permute-done.14.refs_2_, ...), custom_call_target="tpu_custom_call" | custom-call | tf_op jit(solution)/shard_map/pallas_call | solution.py:40
  106.6 2.3 %collective-permute-start.18 = (bf16[20,128,128]{2,1,0:T(8,128)(2,1)S(1)}, bf16[20,128,128]{2,1,0:T(8,128)(2,1)S(1)}, u32[]{:S(2)}, u32[]{:S(2)}) collective-permute-start(bf16[20,128,128]{2,1,0:T(8,128)(2,1)S(1)} %get-tuple-element.56), channel_id=1, source_target_pairs={{0,1},{1,0},{2,3},{3,2},{4,5},{5,4},{6,7},{7,6},{8,9},{9,8},{10,11... | collective-permute-start | bytes 1966088 | tf_op jit(solution)/shard_map/ppermute | solution.py:388
  108.9 1.1 convert_reduce_fusion
  110.1 6.9 %collective-permute-start.19 = (f32[32,256]{1,0:T(8,128)S(1)}, f32[32,256]{1,0:T(8,128)S(1)}, u32[]{:S(2)}, u32[]{:S(2)}) collective-permute-start(f32[32,256]{1,0:T(8,128)S(1)} %broadcast_multiply_fusion), channel_id=1, source_target_pairs={{0,0},{1,32},{2,8},{3,40},{4,16},{5,48},{6,24},{7,56},{8,2},{9,34}... | collective-permute-start | bytes 98312 | tf_op jit(solution)/shard_map/ppermute | solution.py:491
  117.0 1.4 %shard_map.109 = (bf16[1,128,2048]{2,1,0:T(8,128)(2,1)}, bf16[1,128,1024]{2,1,0:T(8,128)(2,1)}, bf16[1,128,1024]{2,1,0:T(8,128)(2,1)}, bf16[1,128,1024]{2,1,0:T(8,128)(2,1)}) custom-call(bf16[20,128,128]{2,1,0:T(8,128)(2,1)S(1)} %get-tuple-element.55.refs_0_, bf16[20,128,128]{2,1,0:T(8,128)(2,1)S(1)} %collective-permute-done.18.refs_1_), custom_call_target="tpu_custom_call" | custom-call | tf_op jit(solution)/shard_map/pallas_call | solution.py:40
  (59 shorter events, 12.9 us)
Async XLA Ops:
  3.4 5.3 %collective-permute-start = (bf16[20,128,128]{2,1,0:T(8,128)(2,1)}, bf16[20,128,128]{2,1,0:T(8,128)(2,1)S(1)}, u32[]{:S(2)}, u32[]{:S(2)}) collective-permute-start(bf16[20,128,128]{2,1,0:T(8,128)(2,1)} %get-tuple-element.34), channel_id=1, source_target_pairs={{0,1},{1,0},{2,3},{3,2},{4,5},{5,4},{6,7},{7,6},{8,9},{9,8},{10,11... | collective-permute-start | bytes 1966088 | tf_op jit(solution)/shard_map/ppermute | solution.py:388
  8.6 1.1 copy-start.9
  9.7 3.8 %copy-start.13 = (bf16[32,256]{1,0:T(8,128)(2,1)S(1)}, bf16[32,256]{1,0:T(8,128)(2,1)}, u32[]{:S(2)}) copy-start(bf16[32,256]{1,0:T(8,128)(2,1)} %param.10) | copy-start | bytes 49156
  10.8 20.9 %collective-permute-start.1 = (bf16[25,128,128]{2,1,0:T(8,128)(2,1)}, bf16[25,128,128]{2,1,0:T(8,128)(2,1)S(1)}, u32[]{:S(2)}, u32[]{:S(2)}) collective-permute-start(bf16[25,128,128]{2,1,0:T(8,128)(2,1)} %get-tuple-element.36), channel_id=1, source_target_pairs={{0,2},{2,4},{4,6},{6,0},{1,3},{3,5},{5,7},{7,1},{8,10},{10,12},{12... | collective-permute-start | bytes 2457608 | tf_op jit(solution)/shard_map/ppermute | solution.py:388
  10.8 21.6 %collective-permute-start.2 = (bf16[25,128,128]{2,1,0:T(8,128)(2,1)S(1)}, bf16[25,128,128]{2,1,0:T(8,128)(2,1)S(1)}, u32[]{:S(2)}, u32[]{:S(2)}) collective-permute-start(bf16[25,128,128]{2,1,0:T(8,128)(2,1)S(1)} %get-tuple-element.37), channel_id=1, source_target_pairs={{0,6},{2,0},{4,2},{6,4},{1,7},{3,1},{5,3},{7,5},{8,14},{10,8},{12,... | collective-permute-start | bytes 2457608 | tf_op jit(solution)/shard_map/ppermute | solution.py:388
  13.5 9.3 %collective-permute-start.5 = (bf16[32,256]{1,0:T(8,128)(2,1)S(1)}, bf16[32,256]{1,0:T(8,128)(2,1)S(1)}, u32[]{:S(2)}, u32[]{:S(2)}) collective-permute-start(bf16[32,256]{1,0:T(8,128)(2,1)S(1)} %copy-done.13), channel_id=1, source_target_pairs={{0,0},{1,32},{2,8},{3,40},{4,16},{5,48},{6,24},{7,56},{8,2},{9,34}... | collective-permute-start | bytes 49160 | tf_op jit(solution)/shard_map/ppermute | solution.py:402
  23.6 19.6 %all-to-all-start = ((bf16[32,32,256]{2,1,0:T(8,128)(2,1)}), bf16[32,32,256]{2,1,0:T(8,128)(2,1)}, u32[]{:S(2)}, u32[]{:S(2)}) async-start(bf16[32,32,256]{2,1,0:T(8,128)(2,1)} %broadcast_in_dim.2), calls=%async_computation | async-start | bytes 1048576 | tf_op jit(solution)/shard_map/all_to_all | solution.py:403
  32.4 10.8 %collective-permute-start.3 = (bf16[11,128,128]{2,1,0:T(8,128)(2,1)}, bf16[11,128,128]{2,1,0:T(8,128)(2,1)S(1)}, u32[]{:S(2)}, u32[]{:S(2)}) collective-permute-start(bf16[11,128,128]{2,1,0:T(8,128)(2,1)} %slice.16), channel_id=1, source_target_pairs={{0,2},{2,4},{4,6},{6,0},{1,3},{3,5},{5,7},{7,1},{8,10},{10,12},{12... | collective-permute-start | bytes 1081352 | tf_op jit(solution)/shard_map/ppermute | solution.py:388
  32.5 10.7 %collective-permute-start.4 = (bf16[11,128,128]{2,1,0:T(8,128)(2,1)S(1)}, bf16[11,128,128]{2,1,0:T(8,128)(2,1)S(1)}, u32[]{:S(2)}, u32[]{:S(2)}) collective-permute-start(bf16[11,128,128]{2,1,0:T(8,128)(2,1)S(1)} %slice.17), channel_id=1, source_target_pairs={{0,6},{2,0},{4,2},{6,4},{1,7},{3,1},{5,3},{7,5},{8,14},{10,8},{12,... | collective-permute-start | bytes 1081352 | tf_op jit(solution)/shard_map/ppermute | solution.py:388
  43.2 2.1 %copy-start.1 = (bf16[11,128,128]{2,1,0:T(8,128)(2,1)}, bf16[11,128,128]{2,1,0:T(8,128)(2,1)S(1)}, u32[]{:S(2)}) copy-start(bf16[11,128,128]{2,1,0:T(8,128)(2,1)S(1)} %collective-permute-done.3.refs_4_.refs_5_) | copy-start | bytes 1081348
  43.2 2.1 %copy-start.4 = (bf16[11,128,128]{2,1,0:T(8,128)(2,1)}, bf16[11,128,128]{2,1,0:T(8,128)(2,1)S(1)}, u32[]{:S(2)}) copy-start(bf16[11,128,128]{2,1,0:T(8,128)(2,1)S(1)} %collective-permute-done.4.refs_5_.refs_6_) | copy-start | bytes 1081348
  45.3 12.2 %copy-start.10 = (bf16[256,1024]{1,0:T(8,128)(2,1)}, bf16[256,1024]{1,0:T(8,128)(2,1)S(1)}, u32[]{:S(2)}) copy-start(bf16[256,1024]{1,0:T(8,128)(2,1)S(1)} %get-tuple-element.47.refs_4_) | copy-start | bytes 1572868
  45.3 8.7 %copy-start.12 = (s32[1,12]{1,0:T(1,128)S(1)}, s32[1,12]{1,0:T(1,128)}, u32[]{:S(2)}) copy-start(s32[1,12]{1,0:T(1,128)} %refs_0_.9) | copy-start | bytes 148
  45.3 12.2 %collective-permute-start.6 = (f32[8,128,128]{2,1,0:T(8,128)S(1)}, f32[8,128,128]{2,1,0:T(8,128)S(1)}, u32[]{:S(2)}, u32[]{:S(2)}) collective-permute-start(f32[8,128,128]{2,1,0:T(8,128)S(1)} %get-tuple-element.38.refs_6_), channel_id=1, source_target_pairs={{0,1},{1,0},{2,3},{3,2},{4,5},{5,4},{6,7},{7,6},{8,9},{9,8},{10,11... | collective-permute-start | bytes 1572872 | tf_op jit(solution)/shard_map/ppermute | solution.py:388
  50.9 15.3 %collective-permute-start.10 = (bf16[256,1024]{1,0:T(8,128)(2,1)S(1)}, bf16[256,1024]{1,0:T(8,128)(2,1)S(1)}, u32[]{:S(2)}, u32[]{:S(2)}) collective-permute-start(bf16[256,1024]{1,0:T(8,128)(2,1)S(1)} %get-tuple-element.47.refs_4_), channel_id=1, source_target_pairs={{0,2},{2,4},{4,6},{6,0},{1,3},{3,5},{5,7},{7,1},{8,10},{10,12},{12... | collective-permute-start | bytes 1572872 | tf_op jit(solution)/shard_map/ppermute | solution.py:388
  50.9 15.3 %collective-permute-start.11 = (bf16[256,1024]{1,0:T(8,128)(2,1)S(1)}, bf16[256,1024]{1,0:T(8,128)(2,1)S(1)}, u32[]{:S(2)}, u32[]{:S(2)}) collective-permute-start(bf16[256,1024]{1,0:T(8,128)(2,1)S(1)} %get-tuple-element.47.refs_4_), channel_id=1, source_target_pairs={{0,6},{2,0},{4,2},{6,4},{1,7},{3,1},{5,3},{7,5},{8,14},{10,8},{12,... | collective-permute-start | bytes 1572872 | tf_op jit(solution)/shard_map/ppermute | solution.py:388
  59.7 6.5 %collective-permute-start.7 = (bf16[2,128,128]{2,1,0:T(8,128)(2,1)S(1)}, bf16[2,128,128]{2,1,0:T(8,128)(2,1)S(1)}, u32[]{:S(2)}, u32[]{:S(2)}) collective-permute-start(bf16[2,128,128]{2,1,0:T(8,128)(2,1)S(1)} %get-tuple-element.44), channel_id=1, source_target_pairs={{0,8},{8,16},{16,24},{24,0},{1,9},{9,17},{17,25},{25,1},{2,10},{10... | collective-permute-start | bytes 196616 | tf_op jit(solution)/shard_map/ppermute | solution.py:388
  61.8 4.7 %collective-permute-start.8 = (bf16[2,128,128]{2,1,0:T(8,128)(2,1)S(1)}, bf16[2,128,128]{2,1,0:T(8,128)(2,1)S(1)}, u32[]{:S(2)}, u32[]{:S(2)}) collective-permute-start(bf16[2,128,128]{2,1,0:T(8,128)(2,1)S(1)} %get-tuple-element.45), channel_id=1, source_target_pairs={{0,16},{8,24},{16,0},{24,8},{1,17},{9,25},{17,1},{25,9},{2,18},{10... | collective-permute-start | bytes 196616 | tf_op jit(solution)/shard_map/ppermute | solution.py:388
  63.8 3.8 %collective-permute-start.9 = (bf16[2,128,128]{2,1,0:T(8,128)(2,1)S(1)}, bf16[2,128,128]{2,1,0:T(8,128)(2,1)S(1)}, u32[]{:S(2)}, u32[]{:S(2)}) collective-permute-start(bf16[2,128,128]{2,1,0:T(8,128)(2,1)S(1)} %get-tuple-element.46), channel_id=1, source_target_pairs={{0,24},{8,0},{16,8},{24,16},{1,25},{9,1},{17,9},{25,17},{2,26},{10... | collective-permute-start | bytes 196616 | tf_op jit(solution)/shard_map/ppermute | solution.py:388
  69.2 4.8 %collective-permute-start.12 = (bf16[8,128,128]{2,1,0:T(8,128)(2,1)S(1)}, bf16[8,128,128]{2,1,0:T(8,128)(2,1)S(1)}, u32[]{:S(2)}, u32[]{:S(2)}) collective-permute-start(bf16[8,128,128]{2,1,0:T(8,128)(2,1)S(1)} %get-tuple-element.49.refs_4_.refs_0_), channel_id=1, source_target_pairs={{0,1},{1,0},{2,3},{3,2},{4,5},{5,4},{6,7},{7,6},{8,9},{9,8},{10,11... | collective-permute-start | bytes 786440 | tf_op jit(solution)/shard_map/ppermute | solution.py:388
  71.1 2.9 %copy-start.6 = (bf16[11,128,128]{2,1,0:T(8,128)(2,1)S(1)}, bf16[11,128,128]{2,1,0:T(8,128)(2,1)}, u32[]{:S(2)}) copy-start(bf16[11,128,128]{2,1,0:T(8,128)(2,1)} %copy-done.4) | copy-start | bytes 1081348
  71.2 2.9 %copy-start.3 = (bf16[11,128,128]{2,1,0:T(8,128)(2,1)S(1)}, bf16[11,128,128]{2,1,0:T(8,128)(2,1)}, u32[]{:S(2)}) copy-start(bf16[11,128,128]{2,1,0:T(8,128)(2,1)} %copy-done.1) | copy-start | bytes 1081348
  71.2 9.3 %collective-permute-start.16 = (bf16[128,1024]{1,0:T(8,128)(2,1)S(1)}, bf16[128,1024]{1,0:T(8,128)(2,1)}, u32[]{:S(2)}, u32[]{:S(2)}) collective-permute-start(bf16[128,1024]{1,0:T(8,128)(2,1)S(1)} %slice.18), channel_id=1, source_target_pairs={{0,2},{2,4},{4,6},{6,0},{1,3},{3,5},{5,7},{7,1},{8,10},{10,12},{12... | collective-permute-start | bytes 786440 | tf_op jit(solution)/shard_map/ppermute | solution.py:388
  71.3 9.2 %collective-permute-start.17 = (bf16[128,1024]{1,0:T(8,128)(2,1)S(1)}, bf16[128,1024]{1,0:T(8,128)(2,1)}, u32[]{:S(2)}, u32[]{:S(2)}) collective-permute-start(bf16[128,1024]{1,0:T(8,128)(2,1)S(1)} %slice.19), channel_id=1, source_target_pairs={{0,6},{2,0},{4,2},{6,4},{1,7},{3,1},{5,3},{7,5},{8,14},{10,8},{12,... | collective-permute-start | bytes 786440 | tf_op jit(solution)/shard_map/ppermute | solution.py:388
  80.5 23.3 %copy-start.8 = (bf16[2,5,128,128]{3,2,1,0:T(8,128)(2,1)S(1)}, bf16[2,5,128,128]{3,2,1,0:T(8,128)(2,1)}, u32[]{:S(2)}) copy-start(bf16[2,5,128,128]{3,2,1,0:T(8,128)(2,1)} %copy-done.7) | copy-start | bytes 983044
  80.5 28.4 %all-to-all-start.1 = ((bf16[32,32,256]{2,1,0:T(8,128)(2,1)}), bf16[32,32,256]{2,1,0:T(8,128)(2,1)}, u32[]{:S(2)}, u32[]{:S(2)}) async-start(bf16[32,32,256]{2,1,0:T(8,128)(2,1)} %shard_map.111), calls=%async_computation.1 | async-start | bytes 1048576 | tf_op jit(solution)/shard_map/all_to_all | solution.py:489
  86.6 9.5 %collective-permute-start.13 = (bf16[2,5,128,128]{3,2,1,0:T(8,128)(2,1)S(1)}, bf16[2,5,128,128]{3,2,1,0:T(8,128)(2,1)S(1)}, u32[]{:S(2)}, u32[]{:S(2)}) collective-permute-start(bf16[2,5,128,128]{3,2,1,0:T(8,128)(2,1)S(1)} %get-tuple-element.52), channel_id=1, source_target_pairs={{0,2},{2,4},{4,6},{6,0},{1,3},{3,5},{5,7},{7,1},{8,10},{10,12},{12... | collective-permute-start | bytes 983048 | tf_op jit(solution)/shard_map/ppermute | solution.py:388
  86.7 9.4 %collective-permute-start.14 = (bf16[2,5,128,128]{3,2,1,0:T(8,128)(2,1)S(1)}, bf16[2,5,128,128]{3,2,1,0:T(8,128)(2,1)S(1)}, u32[]{:S(2)}, u32[]{:S(2)}) collective-permute-start(bf16[2,5,128,128]{3,2,1,0:T(8,128)(2,1)S(1)} %get-tuple-element.53), channel_id=1, source_target_pairs={{0,6},{2,0},{4,2},{6,4},{1,7},{3,1},{5,3},{7,5},{8,14},{10,8},{12,... | collective-permute-start | bytes 983048 | tf_op jit(solution)/shard_map/ppermute | solution.py:388
  89.4 14.4 %collective-permute-start.15 = (bf16[2,5,128,128]{3,2,1,0:T(8,128)(2,1)S(1)}, bf16[2,5,128,128]{3,2,1,0:T(8,128)(2,1)S(1)}, u32[]{:S(2)}, u32[]{:S(2)}) collective-permute-start(bf16[2,5,128,128]{3,2,1,0:T(8,128)(2,1)S(1)} %get-tuple-element.54), channel_id=1, source_target_pairs={{0,4},{2,6},{4,0},{6,2},{1,5},{3,7},{5,1},{7,3},{8,12},{10,14},{12... | collective-permute-start | bytes 983048 | tf_op jit(solution)/shard_map/ppermute | solution.py:388
  103.8 1.0 copy-start.11
  106.6 10.3 %collective-permute-start.18 = (bf16[20,128,128]{2,1,0:T(8,128)(2,1)S(1)}, bf16[20,128,128]{2,1,0:T(8,128)(2,1)S(1)}, u32[]{:S(2)}, u32[]{:S(2)}) collective-permute-start(bf16[20,128,128]{2,1,0:T(8,128)(2,1)S(1)} %get-tuple-element.56), channel_id=1, source_target_pairs={{0,1},{1,0},{2,3},{3,2},{4,5},{5,4},{6,7},{7,6},{8,9},{9,8},{10,11... | collective-permute-start | bytes 1966088 | tf_op jit(solution)/shard_map/ppermute | solution.py:388
  110.1 9.2 %collective-permute-start.19 = (f32[32,256]{1,0:T(8,128)S(1)}, f32[32,256]{1,0:T(8,128)S(1)}, u32[]{:S(2)}, u32[]{:S(2)}) collective-permute-start(f32[32,256]{1,0:T(8,128)S(1)} %broadcast_multiply_fusion), channel_id=1, source_target_pairs={{0,0},{1,32},{2,8},{3,40},{4,16},{5,48},{6,24},{7,56},{8,2},{9,34}... | collective-permute-start | bytes 98312 | tf_op jit(solution)/shard_map/ppermute | solution.py:491
  (4 other events, 3.5 us)
